TPU v7x, 32 devices: a whole 2x2x4 slice. The times are simulated.
32 devices in a mesh: slide: 4 (over y, x), blk: 8 (over z, core).
Axes of the slice: x: 2, y: 2, z: 4, core: 2. Of those that a mesh axis runs over, the one named last changes fastest.
Arguments:
- counts: int32 [4, 1024, 13500], P('slide', 'blk'), may hold values from 0 to 7, as said below
- library: int32 [4, 1024], P('slide', 'blk'), may hold values from 2000 to 39999
- coords: int32 [4, 1024, 2], P('slide', 'blk'), may hold values from 0 to 1023
- noise: float32 [4, 1024, 512], P('slide', 'blk'), may hold values from -5 to 5
- decoded_cot: bfloat16 [4, 1024, 13500], P('slide', 'blk'), may hold values from -6 to 6
- prior_cot: float32 [4, 1024], P('slide', 'blk'), may hold values from -6 to 6
- embed_t: bfloat16 [1024, 13500], P('blk'), may hold values from -0.0546875 to 0.0546875
- w_qkv: bfloat16 [1024, 3072], P('blk'), may hold values from -0.1875 to 0.1875
- w_attn_out: bfloat16 [1024, 1024], P('blk'), may hold values from -0.625 to 0.625
- w_up: bfloat16 [1024, 4096], P('blk'), may hold values from -0.1875 to 0.1875
- up_bias: bfloat16 [4096], P('blk'), may hold values from -3 to 3
- w_down: bfloat16 [4096, 1024], P('blk'), may hold values from -0.09375 to 0.09375
- w_latent: bfloat16 [1024, 1024], P('blk'), may hold values from -0.046875 to 0.046875
- w_decode: bfloat16 [512, 13500], P('blk'), may hold values from -0.25 to 0.25
- comp_means: bfloat16 [512, 16], P('blk'), may hold values from -3 to 3
- norm_params: bfloat16 [1024, 4], P('blk'), as said below
Outputs:
- decoded: bfloat16 [4, 1024, 13500], P('slide', 'blk')
- prior: float32 [4, 1024], P('slide', 'blk')
- expr_grad: float32 [4, 1024, 13500], P('slide', 'blk')
- embed_grad: float32 [1024, 13500], P('blk')
- qkv_grad: float32 [1024, 3072], P('blk')
- attn_out_grad: float32 [1024, 1024], P('blk')
- up_grad: float32 [1024, 4096], P('blk')
- up_bias_grad: float32 [4096], P('blk')
- down_grad: float32 [4096, 1024], P('blk')
- latent_grad: float32 [1024, 1024], P('blk')
- decode_grad: float32 [512, 13500], P('blk')
- means_grad: float32 [512, 16], P('blk')
- norm_grad: float32 [1024, 4], P('blk')
Inputs may be any that keep to these rules, and one draw needn't show every extreme that they name: Most counts are zero; the others are 1 to 7. `norm_params`: columns 0 and 2 are gains near 1; columns 1 and 3 are shifts of order a fifth, of either sign.
All inputs are finite; a program needn't handle non-finite values.
Results may differ from a plain program's by a relative error of at most 0.02.
Values may be sent and summed in bfloat16 or wider, within the bound.
No kernel may reach another device: no remote copies, remote signals or barrier semaphores. Data moves between devices by JAX's collectives and lax.ppermute only.
A program may use at most 384 MiB of HBM per device.

v0:
```python
import math

import jax
import jax.numpy as jnp
from jax import lax
from jax.sharding import PartitionSpec as P

HEADS = 16
HEAD_DIM = 64


eps_norm = 1e-05


def contract_rows(former, latter):
    return lax.dot_general(
        former, latter, (((0,), (0,)), ((), ())), preferred_element_type=jnp.float32
    )


def contract_cols(former, latter):
    return lax.dot_general(
        former, latter, (((1,), (1,)), ((), ())), preferred_element_type=jnp.float32
    )


def layer_norm(tensor, norm_gain, norm_shift):
    center = tensor - jnp.mean(tensor, axis=-1, keepdims=True)
    inverse = lax.rsqrt(jnp.mean(center * center, axis=-1, keepdims=True) + eps_norm)
    return center * inverse * norm_gain + norm_shift


def spatial_code(coords, model_width):
    quarter = model_width // 4
    frequency = jnp.exp(-math.log(10000.0) * jnp.arange(quarter, dtype=jnp.float32) / quarter)
    first_axis = coords[..., 0:1].astype(jnp.float32) * frequency
    second_axis = coords[..., 1:2].astype(jnp.float32) * frequency
    return jnp.concatenate(
        [jnp.sin(first_axis), jnp.cos(first_axis), jnp.sin(second_axis), jnp.cos(second_axis)],
        axis=-1,
    )


def mixture_term(latent, centres):
    scores = (
        jnp.dot(
            latent, centres, precision=lax.Precision.HIGHEST, preferred_element_type=jnp.float32
        )
        - 0.5 * jnp.sum(centres * centres, axis=0)
    ) * latent.shape[-1] ** (-0.5)
    return -jax.nn.logsumexp(scores, axis=-1)


def split_single(rows_in, head_count):
    arrived_rows = rows_in.shape[0]
    block_rows = 512
    return rows_in.reshape(
        (arrived_rows // block_rows, block_rows, head_count, rows_in.shape[1] // head_count)
    )


def split_blocks(key_rows, value_rows, head_count):
    return (split_single(key_rows, head_count), split_single(value_rows, head_count))


def local(
    counts,
    library,
    coords,
    noise,
    decoded_cot,
    prior_cot,
    embed_t,
    w_qkv,
    w_attn_out,
    w_up,
    up_bias,
    w_down,
    w_latent,
    w_decode,
    comp_means,
    norm_params,
):
    gathered = (
        lax.all_gather(embed_t, "blk", axis=0, tiled=True),
        lax.all_gather(w_qkv, "blk", axis=0, tiled=True),
        lax.all_gather(w_attn_out, "blk", axis=0, tiled=True),
        lax.all_gather(w_up, "blk", axis=0, tiled=True),
        lax.all_gather(up_bias, "blk", axis=0, tiled=True),
        lax.all_gather(w_down, "blk", axis=0, tiled=True),
        lax.all_gather(w_latent, "blk", axis=0, tiled=True),
        lax.all_gather(w_decode, "blk", axis=0, tiled=True),
        lax.all_gather(comp_means, "blk", axis=0, tiled=True),
        lax.all_gather(norm_params, "blk", axis=0, tiled=True),
    )
    (
        embedding,
        weight_qkv,
        weight_out,
        weight_up,
        bias_up,
        weight_down,
        weight_latent,
        weight_decode,
        centres,
        norm_table,
    ) = gathered
    head_count = HEADS
    head_width = HEAD_DIM
    scaling = head_width ** (-0.5)
    model_width = embedding.shape[0]
    latent_width = weight_decode.shape[0]
    blk_count = lax.axis_size("blk")
    expression = jnp.log1p(
        counts[0].astype(jnp.float32) * 10000.0 / library[0].astype(jnp.float32)[:, None]
    )
    expression_low = expression.astype(jnp.bfloat16)
    local_cells = expression.shape[0]
    norm_float = norm_table.astype(jnp.float32)
    h_zero = contract_cols(expression_low, embedding) + spatial_code(coords[0], model_width)
    normed_one, norm_one_back = jax.vjp(layer_norm, h_zero, norm_float[:, 0], norm_float[:, 1])
    normed_one_low = normed_one.astype(jnp.bfloat16)
    projected = jnp.dot(normed_one_low, weight_qkv, preferred_element_type=jnp.float32).astype(
        jnp.bfloat16
    )
    queries = projected[:, :model_width].reshape(local_cells, head_count, head_width)
    key_rows = projected[:, model_width : 2 * model_width]
    value_rows = projected[:, 2 * model_width :]
    stat_start = (
        jnp.full((head_count, local_cells), -1e30, jnp.float32),
        jnp.zeros((head_count, local_cells), jnp.float32),
    )
    key_blocks = split_single(lax.all_gather(key_rows, "blk", axis=0, tiled=True), head_count)

    def per_block(status, key_block):
        running_max, running_sum = status
        scores = (
            jnp.einsum("thd,khd->htk", queries, key_block, preferred_element_type=jnp.float32)
            * scaling
        )
        new_max = jnp.maximum(running_max, jnp.max(scores, axis=-1))
        running_sum = running_sum * jnp.exp(running_max - new_max) + jnp.sum(
            jnp.exp(scores - new_max[..., None]), axis=-1
        )
        return ((new_max, running_sum), None)

    result, unused = lax.scan(per_block, stat_start, key_blocks)
    running_max, running_sum = result
    log_total = running_max + jnp.log(running_sum)
    arrived = (
        lax.all_gather(key_rows, "blk", axis=0, tiled=True),
        lax.all_gather(value_rows, "blk", axis=0, tiled=True),
    )
    key_blocks, value_blocks = split_blocks(arrived[0], arrived[1], head_count)

    def per_block(weighted, block_pair):
        scores = (
            jnp.einsum("thd,khd->htk", queries, block_pair[0], preferred_element_type=jnp.float32)
            * scaling
        )
        probs_low = jnp.exp(scores - log_total[..., None]).astype(jnp.bfloat16)
        weighted = weighted + jnp.einsum(
            "htk,khd->htd", probs_low, block_pair[1], preferred_element_type=jnp.float32
        )
        return (weighted, None)

    result, unused = lax.scan(
        per_block,
        jnp.zeros((head_count, local_cells, head_width), jnp.float32),
        (key_blocks, value_blocks),
    )
    attended_cells = jnp.transpose(result, (1, 0, 2))
    attended_low = attended_cells.reshape(local_cells, model_width).astype(jnp.bfloat16)
    h_one = h_zero + jnp.dot(attended_low, weight_out, preferred_element_type=jnp.float32)
    normed_two, norm_two_back = jax.vjp(layer_norm, h_one, norm_float[:, 2], norm_float[:, 3])
    normed_two_low = normed_two.astype(jnp.bfloat16)
    hidden_pre = jnp.dot(
        normed_two_low, weight_up, preferred_element_type=jnp.float32
    ) + bias_up.astype(jnp.float32)
    hidden_act, gelu_back = jax.vjp(jax.nn.gelu, hidden_pre)
    hidden_low = hidden_act.astype(jnp.bfloat16)
    h_two = h_one + jnp.dot(hidden_low, weight_down, preferred_element_type=jnp.float32)
    h_two_low = h_two.astype(jnp.bfloat16)
    latent_pre = jnp.dot(h_two_low, weight_latent, preferred_element_type=jnp.float32)
    spread = jnp.exp(0.5 * latent_pre[:, latent_width:])
    latent = latent_pre[:, :latent_width] + spread * noise[0]
    latent_low = latent.astype(jnp.bfloat16)
    decoded = jnp.dot(latent_low, weight_decode, preferred_element_type=jnp.float32).astype(
        jnp.bfloat16
    )
    prior, prior_back = jax.vjp(mixture_term, latent, centres.astype(jnp.float32))
    out_grad = decoded_cot[0]
    latent_from_decode = contract_cols(out_grad, weight_decode)
    latent_from_prior, centre_grad = prior_back(prior_cot[0])
    latent_total = latent_from_decode + latent_from_prior
    pre_grad = jnp.concatenate(
        [latent_total, latent_total * noise[0] * spread * 0.5], axis=-1
    ).astype(jnp.bfloat16)
    latent_weight_grad = contract_rows(h_two_low, pre_grad)
    h_two_grad = contract_cols(pre_grad, weight_latent)
    down_input = h_two_grad.astype(jnp.bfloat16)
    down_grad = contract_rows(hidden_low, down_input)
    hidden_grad = contract_cols(down_input, weight_down)
    pre_hidden_grad = gelu_back(hidden_grad)[0].astype(jnp.bfloat16)
    up_bias_grad = jnp.sum(pre_hidden_grad.astype(jnp.float32), axis=0)
    up_grad = contract_rows(normed_two_low, pre_hidden_grad)
    normed_two_grad = contract_cols(pre_hidden_grad, weight_up)
    h_one_part, gain_two_grad, shift_two_grad = norm_two_back(normed_two_grad)
    h_one_grad = h_two_grad + h_one_part
    out_input = h_one_grad.astype(jnp.bfloat16)
    attn_out_grad = contract_rows(attended_low, out_input)
    attended_grad = contract_cols(out_input, weight_out).astype(jnp.bfloat16)
    out_heads = attended_grad.reshape(local_cells, head_count, head_width)
    row_delta = jnp.sum(out_heads.astype(jnp.float32) * attended_cells, axis=-1).T
    query_zero = jnp.zeros((head_count, local_cells, head_width), jnp.float32)
    start_back = (query_zero, jnp.zeros((local_cells * blk_count, 2 * model_width), jnp.float32))
    arrived = (
        lax.all_gather(key_rows, "blk", axis=0, tiled=True),
        lax.all_gather(value_rows, "blk", axis=0, tiled=True),
    )
    key_blocks, value_blocks = split_blocks(arrived[0], arrived[1], head_count)
    arrived_rows = arrived[0].shape[0]

    def per_block(query_sum, block_pair):
        scores = (
            jnp.einsum("thd,khd->htk", queries, block_pair[0], preferred_element_type=jnp.float32)
            * scaling
        )
        probs = jnp.exp(scores - log_total[..., None])
        prob_grad = jnp.einsum(
            "thd,khd->htk", out_heads, block_pair[1], preferred_element_type=jnp.float32
        )
        score_grad = (probs * (prob_grad - row_delta[..., None])).astype(jnp.bfloat16)
        query_sum = query_sum + jnp.einsum(
            "htk,khd->htd", score_grad, block_pair[0], preferred_element_type=jnp.float32
        )
        key_part = (
            jnp.einsum("htk,thd->khd", score_grad, queries, preferred_element_type=jnp.float32)
            * scaling
        )
        value_part = jnp.einsum(
            "htk,thd->khd",
            probs.astype(jnp.bfloat16),
            out_heads,
            preferred_element_type=jnp.float32,
        )
        block_rows = key_part.shape[0]
        return (
            query_sum,
            jnp.concatenate(
                [key_part.reshape(block_rows, -1), value_part.reshape(block_rows, -1)], axis=-1
            ),
        )

    query_total, stacked = lax.scan(per_block, start_back[0], (key_blocks, value_blocks))
    stacked = stacked.reshape(arrived_rows, stacked.shape[-1])
    carried_back = (query_total, stacked)
    query_total = carried_back[0]
    own_pairs = lax.psum_scatter(
        carried_back[1].astype(jnp.bfloat16), "blk", scatter_dimension=0, tiled=True
    ).astype(jnp.float32)
    query_rows = jnp.transpose(query_total * scaling, (1, 0, 2)).reshape(local_cells, model_width)
    projected_grad = jnp.concatenate([query_rows, own_pairs], axis=-1).astype(jnp.bfloat16)
    qkv_grad = contract_rows(normed_one_low, projected_grad)
    normed_one_grad = contract_cols(projected_grad, weight_qkv)
    h_zero_part, gain_one_grad, shift_one_grad = norm_one_back(normed_one_grad)
    h_zero_low = (h_one_grad + h_zero_part).astype(jnp.bfloat16)
    expr_grad = jnp.dot(h_zero_low, embedding, preferred_element_type=jnp.float32)
    norm_grad = jnp.stack([gain_one_grad, shift_one_grad, gain_two_grad, shift_two_grad], axis=0).T
    centre_grad = centre_grad.T.T
    embed_slot = contract_rows(h_zero_low, expression_low)
    decode_slot = contract_rows(latent_low, out_grad)
    block_parts = (
        lax.psum_scatter(
            embed_slot.astype(jnp.bfloat16), "blk", scatter_dimension=0, tiled=True
        ).astype(jnp.float32),
        lax.psum_scatter(
            qkv_grad.astype(jnp.bfloat16), "blk", scatter_dimension=0, tiled=True
        ).astype(jnp.float32),
        lax.psum_scatter(
            attn_out_grad.astype(jnp.bfloat16), "blk", scatter_dimension=0, tiled=True
        ).astype(jnp.float32),
        lax.psum_scatter(
            up_grad.astype(jnp.bfloat16), "blk", scatter_dimension=0, tiled=True
        ).astype(jnp.float32),
        lax.psum_scatter(
            up_bias_grad.astype(jnp.bfloat16), "blk", scatter_dimension=0, tiled=True
        ).astype(jnp.float32),
        lax.psum_scatter(
            down_grad.astype(jnp.bfloat16), "blk", scatter_dimension=0, tiled=True
        ).astype(jnp.float32),
        lax.psum_scatter(
            latent_weight_grad.astype(jnp.bfloat16), "blk", scatter_dimension=0, tiled=True
        ).astype(jnp.float32),
        lax.psum_scatter(
            decode_slot.astype(jnp.bfloat16), "blk", scatter_dimension=0, tiled=True
        ).astype(jnp.float32),
        lax.psum_scatter(
            centre_grad.astype(jnp.bfloat16), "blk", scatter_dimension=0, tiled=True
        ).astype(jnp.float32),
        lax.psum_scatter(
            norm_grad.astype(jnp.bfloat16), "blk", scatter_dimension=0, tiled=True
        ).astype(jnp.float32),
    )
    summed = (
        lax.psum(block_parts[0].astype(jnp.bfloat16), "slide").astype(jnp.float32),
        lax.psum(block_parts[1].astype(jnp.bfloat16), "slide").astype(jnp.float32),
        lax.psum(block_parts[2].astype(jnp.bfloat16), "slide").astype(jnp.float32),
        lax.psum(block_parts[3].astype(jnp.bfloat16), "slide").astype(jnp.float32),
        lax.psum(block_parts[4].astype(jnp.bfloat16), "slide").astype(jnp.float32),
        lax.psum(block_parts[5].astype(jnp.bfloat16), "slide").astype(jnp.float32),
        lax.psum(block_parts[6].astype(jnp.bfloat16), "slide").astype(jnp.float32),
        lax.psum(block_parts[7].astype(jnp.bfloat16), "slide").astype(jnp.float32),
        lax.psum(block_parts[8].astype(jnp.bfloat16), "slide").astype(jnp.float32),
        lax.psum(block_parts[9].astype(jnp.bfloat16), "slide").astype(jnp.float32),
    )
    embed_out = summed[0]
    decode_out = summed[7]
    return (
        decoded[None],
        prior[None],
        expr_grad[None],
        embed_out,
        summed[1],
        summed[2],
        summed[3],
        summed[4],
        summed[5],
        summed[6],
        decode_out,
        summed[8],
        summed[9],
    )


def solution(mesh):
    placed = (
        P("slide", "blk", None),
        P("slide", "blk"),
        P("slide", "blk", None),
        P("slide", "blk", None),
        P("slide", "blk", None),
        P("slide", "blk"),
        P("blk", None),
        P("blk", None),
        P("blk", None),
        P("blk", None),
        P("blk"),
        P("blk", None),
        P("blk", None),
        P("blk", None),
        P("blk", None),
        P("blk", None),
    )
    return jax.shard_map(
        local,
        mesh=mesh,
        in_specs=placed,
        out_specs=(
            P("slide", "blk", None),
            P("slide", "blk"),
            P("slide", "blk", None),
            P("blk", None),
            P("blk", None),
            P("blk", None),
            P("blk", None),
            P("blk"),
            P("blk", None),
            P("blk", None),
            P("blk", None),
            P("blk", None),
            P("blk", None),
        ),
        check_vma=False,
    )
```

profile of v0, /device:TPU:0, one launch (start us, length us, event | category | flops | bytes accessed | tf_op | source)
XLA Modules:
  0.0 1906.6 jit_solution(8758914148801531065)
XLA Ops:
  33.1 221.0 %all-gather.12.cloned.1.call-done = bf16[1024,13500]{0,1:T(8,128)(2,1)} async-done(((bf16[128,13500]{0,1:T(8,128)(2,1)}), bf16[1024,13500]{0,1:T(8,128)(2,1)}) %all-gather.12.cloned.1.call-update) | async-done | bytes 27648016 | tf_op jit(solution)/shard_map/all_gather | solution.py:85
  254.1 17.8 fusion.95
  273.0 46.3 %all-gather.14.cloned.1.call-done = bf16[1024,3072]{1,0:T(8,128)(2,1)} async-done(((bf16[128,3072]{1,0:T(8,128)(2,1)}), bf16[1024,3072]{1,0:T(8,128)(2,1)}) %all-gather.14.cloned.1.call-update) | async-done | bytes 6291472 | tf_op jit(solution)/shard_map/all_gather | solution.py:86
  327.7 14.4 all-gather
  342.8 14.3 all-gather.1
  357.3 90.1 %all-gather.28.cloned.1.call-done = bf16[512,13500]{1,0:T(8,128)(2,1)} async-done(((bf16[64,13500]{1,0:T(8,128)(2,1)}), bf16[512,13500]{1,0:T(8,128)(2,1)}) %all-gather.28.cloned.1.call-update) | async-done | bytes 13824016 | tf_op jit(solution)/shard_map/all_gather | solution.py:92
  459.5 17.3 all-gather.16.cloned.1.call-done
  488.7 14.2 while.37
  540.8 79.9 %all-gather.22.cloned.1.call-done = bf16[1024,4096]{1,0:T(8,128)(2,1)} async-done(((bf16[128,4096]{1,0:T(8,128)(2,1)}), bf16[1024,4096]{1,0:T(8,128)(2,1)}) %all-gather.22.cloned.1.call-update) | async-done | bytes 8388624 | tf_op jit(solution)/shard_map/all_gather | solution.py:88
  626.9 76.0 %all-gather.24.cloned.1.call-done = bf16[4096,1024]{1,0:T(8,128)(2,1)} async-done(((bf16[512,1024]{1,0:T(8,128)(2,1)}), bf16[4096,1024]{1,0:T(8,128)(2,1)}) %all-gather.24.cloned.1.call-update) | async-done | bytes 8388624 | tf_op jit(solution)/shard_map/all_gather | solution.py:90
  709.2 23.0 %all-gather.26.cloned.1.call-done = bf16[1024,1024]{1,0:T(8,128)(2,1)} async-done(((bf16[128,1024]{1,0:T(8,128)(2,1)}), bf16[1024,1024]{1,0:T(8,128)(2,1)}) %all-gather.26.cloned.1.call-update) | async-done | bytes 2097168 | tf_op jit(solution)/shard_map/all_gather | solution.py:91
  755.9 40.1 %while.39 = (s32[]{:T(128)}, f32[16,128,64]{1,2,0:T(8,128)}, bf16[2,512,2048]{2,1,0:T(8,128)(2,1)}, bf16[2,512,16,64]{1,3,2,0:T(8,128)(2,1)}, bf16[128,16,64]{0,...) while((s32[]{:T(128)}, f32[16,128,64]{1,2,0:T(8,128)}, ...), condition=%wide.region_17.18_spmd.clone, body=%wide.region_16.17_spmd.clone.sunk | while | flops 684982272 | bytes 91251008 | solution.py:255
  799.6 46.0 %reduce-scatter.17.cloned.1.call-done = bf16[128,2048]{1,0:T(8,128)(2,1)} async-done(((bf16[1024,2048]{1,0:T(8,128)(2,1)}), bf16[128,2048]{1,0:T(8,128)(2,1)}) %reduce-scatter.17.cloned.1.call-update) | async-done | bytes 524304 | tf_op jit(solution)/shard_map/reduce_scatter | solution.py:259
  852.9 16.7 convolution_convert_fusion
  869.6 33.6 %copy.80 = bf16[1024,13500]{1,0:T(8,128)(2,1)} copy(bf16[1024,13500]{0,1:T(8,128)(2,1)} %convolution_convert_fusion) | data formatting | bytes 55296000
  942.5 230.8 %reduce-scatter.31.cloned.1.call-done = bf16[128,13500]{1,0:T(8,128)(2,1)} async-done(((bf16[1024,13500]{1,0:T(8,128)(2,1)}), bf16[128,13500]{1,0:T(8,128)(2,1)}) %reduce-scatter.31.cloned.1.call-update) | async-done | bytes 3456016
  1179.2 31.2 %reduce-scatter.21.cloned.1.call-done = bf16[128,1024]{1,0:T(8,128)(2,1)} async-done(((bf16[1024,1024]{1,0:T(8,128)(2,1)}), bf16[128,1024]{1,0:T(8,128)(2,1)}) %reduce-scatter.21.cloned.1.call-update) | async-done | bytes 262160 | tf_op jit(solution)/shard_map/reduce_scatter | solution.py:280
  1210.4 37.3 %reduce-scatter.27.cloned.1.call-done = bf16[128,1024]{1,0:T(8,128)(2,1)} async-done(((bf16[1024,1024]{1,0:T(8,128)(2,1)}), bf16[128,1024]{1,0:T(8,128)(2,1)}) %reduce-scatter.27.cloned.1.call-update) | async-done | bytes 262160 | tf_op jit(solution)/shard_map/reduce_scatter | solution.py:292
  1247.7 90.5 %reduce-scatter.23.cloned.1.call-done = bf16[128,4096]{1,0:T(8,128)(2,1)} async-done(((bf16[1024,4096]{1,0:T(8,128)(2,1)}), bf16[128,4096]{1,0:T(8,128)(2,1)}) %reduce-scatter.23.cloned.1.call-update) | async-done | bytes 1048592 | tf_op jit(solution)/shard_map/reduce_scatter | solution.py:283
  1338.2 90.1 %reduce-scatter.25.cloned.1.call-done = bf16[512,1024]{1,0:T(8,128)(2,1)} async-done(((bf16[4096,1024]{1,0:T(8,128)(2,1)}), bf16[512,1024]{1,0:T(8,128)(2,1)}) %reduce-scatter.25.cloned.1.call-update) | async-done | bytes 1048592 | tf_op jit(solution)/shard_map/reduce_scatter | solution.py:289
  1428.3 70.9 %reduce-scatter.19.cloned.1.call-done = bf16[128,3072]{1,0:T(8,128)(2,1)} async-done(((bf16[1024,3072]{1,0:T(8,128)(2,1)}), bf16[128,3072]{1,0:T(8,128)(2,1)}) %reduce-scatter.19.cloned.1.call-update) | async-done | bytes 786448 | tf_op jit(solution)/shard_map/reduce_scatter | solution.py:277
  1499.3 142.1 %reduce-scatter.29.cloned.1.call-done = bf16[64,13500]{1,0:T(8,128)(2,1)} async-done(((bf16[512,13500]{1,0:T(8,128)(2,1)}), bf16[64,13500]{1,0:T(8,128)(2,1)}) %reduce-scatter.29.cloned.1.call-update) | async-done | bytes 1728016 | tf_op jit(solution)/shard_map/reduce_scatter | solution.py:295
  1686.4 43.8 %copy.79 = f32[1,128,13500]{1,0,2:T(1,128)} copy(f32[1,128,13500]{1,2,0:T(8,128)S(1)} %convolution_bitcast_fusion) | data formatting | bytes 13824000
  1743.4 143.2 %all-reduce.5.cloned.1.call-done = (bf16[128,13500]{0,1:T(8,128)(2,1)}, bf16[128,3072]{1,0:T(8,128)(2,1)}, bf16[128,1024]{1,0:T(8,128)(2,1)}, bf16[128,4096]{1,0...) async-done(((bf16[128,13500]{0,1:T(8,128)(2,1)}, bf16[128,3072]{1,0:T(8,128)(2,1)}, bf16[128,1024]{1,0:T(8,128)(2,1)}, ...) | async-done | bytes 8591888 | tf_op jit(solution)/shard_map/psum | solution.py:306
  (281 shorter events, 321.4 us)
Async XLA Ops:
  7.2 440.2 %copy-start = (bf16[1,128,13500]{1,2,0:T(8,128)(2,1)S(1)}, bf16[1,128,13500]{1,2,0:T(8,128)(2,1)}, u32[]{:S(2)}) copy-start(bf16[1,128,13500]{1,2,0:T(8,128)(2,1)} %param.26) | copy-start | bytes 10368004
  7.2 246.9 %all-gather.12.cloned.1.call-start = ((), (), s32[]{:S(2)}) async-start(), calls=%async_computation.10 | async-start | bytes 31113216 | tf_op jit(solution)/shard_map/all_gather | solution.py:85
  8.0 311.3 %all-gather.14.cloned.1.call-start = ((), (), s32[]{:S(2)}) async-start(), calls=%async_computation.11 | async-start | bytes 7077888 | tf_op jit(solution)/shard_map/all_gather | solution.py:86
  8.7 438.7 %all-gather.28.cloned.1.call-start = ((), (), s32[]{:S(2)}) async-start(), calls=%async_computation.18 | async-start | bytes 15630336 | tf_op jit(solution)/shard_map/all_gather | solution.py:92
  9.4 467.4 %all-gather.16.cloned.1.call-start = ((), (), s32[]{:S(2)}) async-start(), calls=%async_computation.12 | async-start | bytes 2359296 | tf_op jit(solution)/shard_map/all_gather | solution.py:151
  23.0 231.1 %copy-start.42 = (f32[128]{0:T(128)}, f32[128]{0:T(128)S(1)}, u32[]{:S(2)}) copy-start(f32[128]{0:T(128)S(1)} %convert_bitcast_fusion.2) | copy-start | bytes 1540
  23.0 296.2 %copy-start.28 = (f32[1024,1]{0,1:T(1,128)}, f32[1024,1]{0,1:T(1,128)S(1)}, u32[]{:S(2)}) copy-start(f32[1024,1]{0,1:T(1,128)S(1)} %get-tuple-element.397) | copy-start | bytes 12292
  324.2 183.2 %all-gather.18.cloned.1.call-start = ((), (), s32[]{:S(2)}) async-start(), calls=%async_computation.13 | async-start | bytes 2359296 | tf_op jit(solution)/shard_map/all_gather | solution.py:152
  324.8 212.7 %all-gather.20.cloned.1.call-start = ((), (), s32[]{:S(2)}) async-start(), calls=%async_computation.14 | async-start | bytes 2359296 | tf_op jit(solution)/shard_map/all_gather | solution.py:87
  325.4 295.3 %all-gather.22.cloned.1.call-start = ((), (), s32[]{:S(2)}) async-start(), calls=%async_computation.15 | async-start | bytes 9437184 | tf_op jit(solution)/shard_map/all_gather | solution.py:88
  326.1 376.8 %all-gather.24.cloned.1.call-start = ((), (), s32[]{:S(2)}) async-start(), calls=%async_computation.16 | async-start | bytes 9437184 | tf_op jit(solution)/shard_map/all_gather | solution.py:90
  326.9 405.3 %all-gather.26.cloned.1.call-start = ((), (), s32[]{:S(2)}) async-start(), calls=%async_computation.17 | async-start | bytes 2359296 | tf_op jit(solution)/shard_map/all_gather | solution.py:91
  327.6 518.0 %reduce-scatter.17.cloned.1.call-start = ((), (), s32[]{:S(2)}) async-start(), calls=%async_computation.19 | async-start | bytes 4718592 | tf_op jit(solution)/shard_map/reduce_scatter | solution.py:259
  527.4 93.3 %copy-start.30 = (f32[8,1,512]{2,1,0:T(1,128)S(1)}, f32[8,1,512]{2,1,0:T(1,128)}, u32[]{:S(2)}) copy-start(f32[8,1,512]{2,1,0:T(1,128)} %convert_element_type.220) | copy-start | bytes 49156
  796.0 377.4 %reduce-scatter.31.cloned.1.call-start = ((), (), s32[]{:S(2)}) async-start(), calls=%async_computation.26 | async-start | bytes 31260672
  903.2 307.2 %reduce-scatter.21.cloned.1.call-start = ((), (), s32[]{:S(2)}) async-start(), calls=%async_computation.21 | async-start | bytes 2359296 | tf_op jit(solution)/shard_map/reduce_scatter | solution.py:280
  906.4 341.2 %reduce-scatter.27.cloned.1.call-start = ((), (), s32[]{:S(2)}) async-start(), calls=%async_computation.24 | async-start | bytes 2359296 | tf_op jit(solution)/shard_map/reduce_scatter | solution.py:292
  909.8 428.4 %reduce-scatter.23.cloned.1.call-start = ((), (), s32[]{:S(2)}) async-start(), calls=%async_computation.22 | async-start | bytes 9437184 | tf_op jit(solution)/shard_map/reduce_scatter | solution.py:283
  917.2 511.1 %reduce-scatter.25.cloned.1.call-start = ((), (), s32[]{:S(2)}) async-start(), calls=%async_computation.23 | async-start | bytes 9437184 | tf_op jit(solution)/shard_map/reduce_scatter | solution.py:289
  924.7 574.6 %reduce-scatter.19.cloned.1.call-start = ((), (), s32[]{:S(2)}) async-start(), calls=%async_computation.20 | async-start | bytes 7077888 | tf_op jit(solution)/shard_map/reduce_scatter | solution.py:277
  931.2 710.2 %reduce-scatter.29.cloned.1.call-start = ((), (), s32[]{:S(2)}) async-start(), calls=%async_computation.25 | async-start | bytes 15630336 | tf_op jit(solution)/shard_map/reduce_scatter | solution.py:295
  939.2 733.3 %reduce-scatter.33.cloned.1.call-start = ((), (), s32[]{:S(2)}) async-start(), calls=%async_computation.27 | async-start | bytes 147456
  941.4 788.8 %reduce-scatter.35.cloned.1.call-start = ((), (), s32[]{:S(2)}) async-start(), calls=%async_computation.28 | async-start | bytes 294912
  942.5 944.0 %all-reduce.5.cloned.1.call-start = ((), (), s32[]{:S(2)}) async-start(), calls=%async_computation.29 | async-start | bytes 17203200 | tf_op jit(solution)/shard_map/psum | solution.py:306
  (51 other events, 422.4 us)
Sparse Core Ops, SparseCore 0:
  9.6 244.4 all-gather.11
  255.7 63.4 all-gather.13
  320.9 126.4 all-gather.27
  449.4 27.3 all-gather.15
  478.8 28.5 all-gather.17
  508.9 28.5 all-gather.19
  539.1 81.5 all-gather.21
  622.3 80.5 all-gather.23
  704.5 27.6 all-gather.25
  796.1 49.4 reduce-scatter.16
  903.3 269.9 reduce-scatter.30
  1176.1 34.2 reduce-scatter.20
  1213.2 34.3 reduce-scatter.26
  1249.8 88.3 reduce-scatter.22
  1340.3 87.9 reduce-scatter.24
  1431.0 68.1 reduce-scatter.18
  1501.4 139.9 reduce-scatter.28
  1644.1 28.4 reduce-scatter.32
  1675.5 28.5 reduce-scatter.34
  1709.3 177.1 all-reduce.4
where the time goes:
time: 1920 us; the launch traced here: 1910 us
  waiting for transfers between devices  1460 us (76%)
  matrix products  187 us (10%)
  local copies, waits for them, and re-layouts  137 us (7%)
  blocking collectives  66.8 us (3%)
  other arithmetic  41.9 us (2%)
    unnamed x23, waiting for transfers between devices  238 us
    all_gather x1, waiting for transfers between devices, local(): lax.all_gather(embed_t, 'blk', axis=0, tiled=True)  221 us
    psum x1, waiting for transfers between devices, local(): lax.psum(block_parts[0].astype(jnp.bfloat16), 'slide').astype(jnp.float32)  143 us
    reduce_scatter x1, waiting for transfers between devices, local(): lax.psum_scatter(decode_slot.astype(jnp.bfloat16), 'blk', scatter_dimensi...  142 us
    unnamed x99, local copies, waits for them, and re-layouts  104 us
    reduce_scatter x1, waiting for transfers between devices, local(): lax.psum_scatter(up_grad.astype(jnp.bfloat16), 'blk', scatter_dimension=0...  90.5 us
    reduce_scatter x1, waiting for transfers between devices, local(): lax.psum_scatter(down_grad.astype(jnp.bfloat16), 'blk', scatter_dimension...  90.1 us
    all_gather x1, waiting for transfers between devices, local(): lax.all_gather(w_decode, 'blk', axis=0, tiled=True)  90.1 us
  transfers between devices with their start and end apart: 20, of which 19 were waited for; matrix products, arithmetic and copies ran while one was open for 12% of the time, Pallas kernels for 0%

commit v1 on v0

--- a/solution.py
+++ b/solution.py
@@ -333,6 +333,342 @@
     )
 
 
+def peers(offset, count):
+    return [(place, place ^ offset) for place in range(count)]
+
+
+def swap(pieces):
+    count = len(pieces)
+    return [pieces[0]] + [
+        lax.ppermute(pieces[k], "slide", peers(k, count)) for k in range(1, count)
+    ]
+
+
+def share(rows, count):
+    return swap([rows] * count)
+
+
+def in_order(pieces, me, axis):
+    stacked = jnp.stack(pieces)
+    return jnp.concatenate(
+        [
+            lax.dynamic_index_in_dim(stacked, jnp.bitwise_xor(me, k), 0, keepdims=False)
+            for k in range(len(pieces))
+        ],
+        axis=axis,
+    )
+
+
+def collect(partials):
+    arrived = swap([partials[0]] + [piece.astype(jnp.bfloat16) for piece in partials[1:]])
+    total = arrived[0]
+    for piece in arrived[1:]:
+        total = total + piece.astype(jnp.float32)
+    return total
+
+
+def gather_blk(piece, axis=0):
+    return lax.all_gather(piece, "blk", axis=axis, tiled=True)
+
+
+def scatter_blk(piece):
+    return lax.psum_scatter(
+        piece.astype(jnp.bfloat16), "blk", scatter_dimension=0, tiled=True
+    )
+
+
+def split_rows(rows, count):
+    height = rows.shape[0] // count
+    return [rows[k * height : (k + 1) * height] for k in range(count)]
+
+
+def split_model(
+    counts,
+    library,
+    coords,
+    noise,
+    decoded_cot,
+    prior_cot,
+    embed_t,
+    w_qkv,
+    w_attn_out,
+    w_up,
+    up_bias,
+    w_down,
+    w_latent,
+    w_decode,
+    comp_means,
+    norm_params,
+):
+    slides = lax.axis_size("slide")
+    blocks = lax.axis_size("blk")
+    me = lax.axis_index("slide")
+    genes = embed_t.shape[1]
+    cells = counts.shape[1]
+    model_width = w_attn_out.shape[1]
+    own_rows = w_qkv.shape[0]
+    latent_width = w_decode.shape[0] * blocks
+    mixture_count = comp_means.shape[1]
+    quarter = -(-genes // (slides * 128)) * 128
+    padded = quarter * slides
+    head_part = model_width // slides
+    pair = model_width // blocks
+    pairs = head_part // pair
+    ff_part = up_bias.shape[0] // slides
+    scaling = HEAD_DIM ** (-0.5)
+
+    def gene_part(rows, place):
+        return lax.dynamic_slice_in_dim(rows, place * quarter, quarter, 1)
+
+    def pad_genes(rows):
+        return jnp.pad(rows, ((0, 0), (0, padded - genes)))
+
+    def place_of(k):
+        return jnp.bitwise_xor(me, k)
+
+    embedding = gather_blk(gene_part(pad_genes(embed_t), me))
+    qkv_part = lax.dynamic_index_in_dim(
+        w_qkv.reshape(own_rows, 3, slides, pairs, pair), me, 2, keepdims=False
+    )
+    qkv_part = jnp.transpose(qkv_part, (0, 2, 1, 3)).reshape(own_rows, pairs * 3 * pair)
+    bias_part = lax.dynamic_slice_in_dim(up_bias, me * ff_part, ff_part, 0)
+    mean_cols = comp_means.size // own_rows
+    small = jnp.concatenate(
+        [norm_params, comp_means.reshape(own_rows, mean_cols), bias_part.reshape(own_rows, -1)],
+        axis=1,
+    )
+    small_cols = small.shape[1]
+    small = jnp.pad(small, ((0, 0), (0, 128 - small_cols)))
+    first = gather_blk(jnp.concatenate([qkv_part, small], axis=1))
+    weight_qkv = first[:, : pairs * 3 * pair].reshape(model_width, pairs, 3 * pair)
+    small_all = first[:, pairs * 3 * pair :]
+    norm_float = small_all[:, :4].astype(jnp.float32)
+    centres = small_all[:, 4 : 4 + mean_cols].reshape(latent_width, mixture_count)
+    bias_up = small_all[:, 4 + mean_cols : small_cols].reshape(-1).astype(jnp.float32)
+    weight_out = gather_blk(w_attn_out)
+    up_part = lax.dynamic_index_in_dim(
+        w_up.reshape(own_rows, blocks, slides, ff_part), me, 2, keepdims=False
+    ).reshape(own_rows, blocks * ff_part)
+    weight_up = gather_blk(up_part)
+    weight_down = gather_blk(lax.dynamic_slice_in_dim(w_down, me * ff_part, ff_part, 0))
+    weight_latent = gather_blk(w_latent)
+    weight_decode = gather_blk(gene_part(pad_genes(w_decode), me))
+
+    expression = jnp.log1p(
+        counts[0].astype(jnp.float32) * 10000.0 / library[0].astype(jnp.float32)[:, None]
+    )
+    expression_low = pad_genes(expression.astype(jnp.bfloat16))
+    expr_parts = swap([gene_part(expression_low, place_of(k)) for k in range(slides)])
+    h_zero = collect([contract_cols(part, embedding) for part in expr_parts])
+    h_zero = h_zero + spatial_code(coords[0], model_width)
+    normed_one, norm_one_back = jax.vjp(layer_norm, h_zero, norm_float[:, 0], norm_float[:, 1])
+    normed_one_all = jnp.concatenate(share(normed_one.astype(jnp.bfloat16), slides), axis=0)
+    projected = jnp.einsum(
+        "ck,kpf->pcf", normed_one_all, weight_qkv, preferred_element_type=jnp.float32
+    ).astype(jnp.bfloat16)
+
+    def to_heads(rows):
+        return lax.all_to_all(
+            rows.reshape(blocks, cells, rows.shape[-1]), "blk", 0, 0, tiled=True
+        ).reshape(blocks * cells, rows.shape[-1])
+
+    head_rows = to_heads(projected)
+    per_pair = pair // HEAD_DIM
+
+    def heads_of(rows):
+        return jnp.transpose(rows.reshape(blocks * cells, per_pair, HEAD_DIM), (1, 0, 2))
+
+    queries = heads_of(head_rows[:, :pair])
+    key_rows = heads_of(head_rows[:, pair : 2 * pair])
+    value_rows = heads_of(head_rows[:, 2 * pair :])
+    scores = (
+        jnp.einsum("htd,hkd->htk", queries, key_rows, preferred_element_type=jnp.float32)
+        * scaling
+    )
+    probs = jax.nn.softmax(scores, axis=-1)
+    probs_low = probs.astype(jnp.bfloat16)
+    head_out = jnp.einsum(
+        "htk,hkd->thd", probs_low, value_rows, preferred_element_type=jnp.float32
+    ).astype(jnp.bfloat16)
+    own_heads = to_heads(head_out.reshape(blocks * cells, pair)).reshape(
+        pairs, slides, cells, pair
+    )
+    attended_parts = swap(
+        [
+            jnp.transpose(own_heads[:, k], (1, 0, 2)).reshape(cells, head_part)
+            for k in range(slides)
+        ]
+    )
+    attended_low = in_order(attended_parts, me, 1)
+    h_one = h_zero + jnp.dot(attended_low, weight_out, preferred_element_type=jnp.float32)
+    normed_two, norm_two_back = jax.vjp(layer_norm, h_one, norm_float[:, 2], norm_float[:, 3])
+    normed_two_all = jnp.concatenate(share(normed_two.astype(jnp.bfloat16), slides), axis=0)
+    hidden_pre = (
+        jnp.dot(normed_two_all, weight_up, preferred_element_type=jnp.float32) + bias_up
+    )
+    hidden_act, gelu_back = jax.vjp(jax.nn.gelu, hidden_pre)
+    hidden_low = hidden_act.astype(jnp.bfloat16)
+    h_two = h_one + collect(
+        split_rows(jnp.dot(hidden_low, weight_down, preferred_element_type=jnp.float32), slides)
+    )
+    h_two_low = h_two.astype(jnp.bfloat16)
+    latent_pre = jnp.dot(h_two_low, weight_latent, preferred_element_type=jnp.float32)
+    spread = jnp.exp(0.5 * latent_pre[:, latent_width:])
+    latent = latent_pre[:, :latent_width] + spread * noise[0]
+    prior, prior_back = jax.vjp(mixture_term, latent, centres.astype(jnp.float32))
+
+    cot_all = pad_genes(decoded_cot[0])
+    cot_parts = swap([gene_part(cot_all, place_of(k)) for k in range(slides)])
+    latent_from_decode = collect([contract_cols(part, weight_decode) for part in cot_parts])
+    latent_from_prior, centre_grad = prior_back(prior_cot[0])
+    latent_total = latent_from_decode + latent_from_prior
+    pre_grad = jnp.concatenate(
+        [latent_total, latent_total * noise[0] * spread * 0.5], axis=-1
+    ).astype(jnp.bfloat16)
+    pre_grad_all = jnp.concatenate(share(pre_grad, slides), axis=0)
+    h_two_grad_all = contract_cols(pre_grad_all, weight_latent)
+    down_input = h_two_grad_all.astype(jnp.bfloat16)
+    hidden_grad = contract_cols(down_input, weight_down)
+    pre_hidden_grad = gelu_back(hidden_grad)[0].astype(jnp.bfloat16)
+    normed_two_grad = collect(split_rows(contract_cols(pre_hidden_grad, weight_up), slides))
+    h_one_part, gain_two_grad, shift_two_grad = norm_two_back(normed_two_grad)
+    h_one_grad = h_two_grad_all[:cells] + h_one_part
+    out_input = h_one_grad.astype(jnp.bfloat16)
+    attended_grad = contract_cols(out_input, weight_out).astype(jnp.bfloat16)
+
+    def column_part(rows, width, place):
+        return lax.dynamic_slice_in_dim(rows, place * width, width, 1)
+
+    grad_parts = swap([column_part(attended_grad, head_part, place_of(k)) for k in range(slides)])
+    grad_pairs = jnp.stack([part.reshape(cells, pairs, pair) for part in grad_parts])
+    grad_pairs = jnp.transpose(grad_pairs, (2, 0, 1, 3))
+    out_heads = heads_of(to_heads(grad_pairs))
+    prob_grad = jnp.einsum(
+        "htd,hkd->htk", out_heads, value_rows, preferred_element_type=jnp.float32
+    )
+    row_delta = jnp.sum(probs * prob_grad, axis=-1, keepdims=True)
+    score_grad = (probs * (prob_grad - row_delta)).astype(jnp.bfloat16)
+    query_grad = (
+        jnp.einsum("htk,hkd->thd", score_grad, key_rows, preferred_element_type=jnp.float32)
+        * scaling
+    )
+    key_grad = (
+        jnp.einsum("htk,htd->khd", score_grad, queries, preferred_element_type=jnp.float32)
+        * scaling
+    )
+    value_grad = jnp.einsum(
+        "htk,htd->khd", probs_low, out_heads, preferred_element_type=jnp.float32
+    )
+    head_grads = jnp.concatenate(
+        [
+            part.reshape(blocks * cells, pair).astype(jnp.bfloat16)
+            for part in (query_grad, key_grad, value_grad)
+        ],
+        axis=1,
+    )
+    projected_grad = to_heads(head_grads).reshape(pairs, slides * cells, 3 * pair)
+    normed_one_grad = collect(
+        split_rows(
+            jnp.einsum(
+                "pcf,kpf->ck", projected_grad, weight_qkv, preferred_element_type=jnp.float32
+            ),
+            slides,
+        )
+    )
+    h_zero_part, gain_one_grad, shift_one_grad = norm_one_back(normed_one_grad)
+    h_zero_low = (h_one_grad + h_zero_part).astype(jnp.bfloat16)
+    h_zero_parts = share(h_zero_low, slides)
+    expr_grad_parts = swap(
+        [
+            jnp.dot(part, embedding, preferred_element_type=jnp.float32).astype(jnp.bfloat16)
+            for part in h_zero_parts
+        ]
+    )
+    expr_grad = in_order(expr_grad_parts, me, 1)[:, :genes].astype(jnp.float32)
+
+    latent_all = jnp.concatenate(share(latent.astype(jnp.bfloat16), slides), axis=0)
+    decoded_rows = jnp.dot(latent_all, weight_decode, preferred_element_type=jnp.float32)
+    decoded = in_order(swap(split_rows(decoded_rows.astype(jnp.bfloat16), slides)), me, 1)
+    decoded = decoded[:, :genes]
+
+    def whole(piece, axis):
+        return in_order(share(piece, slides), me, axis)
+
+    cot_stack = jnp.concatenate(cot_parts, axis=0)
+    decode_grad = whole(scatter_blk(contract_rows(latent_all, cot_stack)), 1)[:, :genes]
+    h_two_all = jnp.concatenate(share(h_two_low, slides), axis=0)
+    latent_part = model_width // slides
+    latent_grad = whole(
+        scatter_blk(contract_rows(h_two_all, column_part(pre_grad_all, latent_part, me))), 1
+    )
+    down_grad = whole(scatter_blk(contract_rows(hidden_low, down_input)), 0)
+    up_grad = scatter_blk(contract_rows(normed_two_all, pre_hidden_grad))
+    up_grad = whole(up_grad.reshape(own_rows, blocks, 1, ff_part), 2)
+    attended_all = jnp.concatenate(share(attended_low, slides), axis=0)
+    out_parts = swap([column_part(out_input, head_part, place_of(k)) for k in range(slides)])
+    attn_out_grad = whole(
+        scatter_blk(contract_rows(attended_all, jnp.concatenate(out_parts, axis=0))), 1
+    )
+    qkv_grad = jnp.einsum(
+        "ck,pcf->kpf", normed_one_all, projected_grad, preferred_element_type=jnp.float32
+    ).reshape(model_width, pairs * 3 * pair)
+    up_bias_grad = jnp.sum(pre_hidden_grad.astype(jnp.float32), axis=0)
+    small_grad = jnp.concatenate(
+        [
+            jnp.stack([gain_one_grad, shift_one_grad, gain_two_grad, shift_two_grad], axis=1),
+            centre_grad.reshape(model_width, mean_cols),
+            up_bias_grad.reshape(model_width, -1),
+        ],
+        axis=1,
+    )
+    small_grad = jnp.pad(small_grad, ((0, 0), (0, 128 - small_cols)))
+    first_grad = scatter_blk(jnp.concatenate([qkv_grad, small_grad], axis=1))
+    first_parts = share(first_grad, slides)
+    qkv_grad = in_order(
+        [
+            jnp.transpose(
+                part[:, : pairs * 3 * pair].reshape(own_rows, pairs, 3, 1, pair), (0, 2, 3, 1, 4)
+            )
+            for part in first_parts
+        ],
+        me,
+        2,
+    ).reshape(own_rows, 3 * model_width)
+    small_parts = [part[:, pairs * 3 * pair :] for part in first_parts]
+    summed = sum(part.astype(jnp.float32) for part in small_parts)
+    up_bias_out = in_order(
+        [part[:, 4 + mean_cols : small_cols].reshape(-1) for part in small_parts], me, 0
+    )
+    embed_grad = whole(
+        scatter_blk(contract_rows(jnp.concatenate(h_zero_parts, axis=0), jnp.concatenate(expr_parts, axis=0))),
+        1,
+    )[:, :genes]
+
+    def wide(piece):
+        return piece.astype(jnp.float32)
+
+    return (
+        decoded[None],
+        prior[None],
+        expr_grad[None],
+        wide(embed_grad),
+        wide(qkv_grad),
+        wide(attn_out_grad),
+        wide(up_grad.reshape(own_rows, -1)),
+        wide(up_bias_out),
+        wide(down_grad),
+        wide(latent_grad),
+        wide(decode_grad),
+        summed[:, 4 : 4 + mean_cols].reshape(comp_means.shape),
+        summed[:, :4],
+    )
+
+
+def fits(mesh):
+    slides, blocks = mesh.shape["slide"], mesh.shape["blk"]
+    return slides & (slides - 1) == 0 and HEADS % slides == 0 and HEADS % blocks == 0
+
+
 def solution(mesh):
     placed = (
         P("slide", "blk", None),
@@ -353,7 +689,7 @@
         P("blk", None),
     )
     return jax.shard_map(
-        local,
+        split_model if fits(mesh) else local,
         mesh=mesh,
         in_specs=placed,
         out_specs=(

time: 1920 us -> 781 us (0.41)
  waiting for transfers between devices: 1460 us -> 378 us
  starting transfers between devices: 1.01 us -> 111 us
  blocking collectives: 66.8 us -> 0 us
  matrix products: 187 us -> 122 us
  local copies, waits for them, and re-layouts: 137 us -> 86.5 us
    reduce_scatter x7 -> x6, waiting for transfers between devices: 508 us -> 0.07 us  [scatter_blk(): lax.psum_scatter(piece.astype(jnp.bfloat16), 'blk', scatter_dimension=0,...]
    all_gather x9 -> x7, waiting for transfers between devices: 566 us -> 80 us  [gather_blk(): return lax.all_gather(piece, 'blk', axis=axis, tiled=True)]
    unnamed x23 -> x15, waiting for transfers between devices: 238 us -> 0.74 us
    ppermute x0 -> x78, waiting for transfers between devices: none -> 222 us  [swap(): lax.ppermute(pieces[k], 'slide', peers(k, count))]
    psum x1 -> x0, waiting for transfers between devices: 143 us -> none  [local(): lax.psum(block_parts[0].astype(jnp.bfloat16), 'slide').astype(jnp.float32)]
    ppermute x0 -> x78, starting transfers between devices: none -> 95.4 us  [swap(): lax.ppermute(pieces[k], 'slide', peers(k, count))]
    all_to_all x0 -> x4, waiting for transfers between devices: none -> 75.8 us  [to_heads(): lax.all_to_all(rows.reshape(blocks, cells, rows.shape[-1]), 'blk', 0, 0,...]
    unnamed x99 -> x227, local copies, waits for them, and re-layouts: 104 us -> 51.8 us
  transfers between devices with their start and end apart: 20 -> 96, of which waited for: 19 -> 49; matrix products, arithmetic and copies ran while one was open for 12% -> 29% of each run, Pallas kernels for 0% -> 0%
where the time goes in v1:
time: 781 us; the launch traced here: 769 us
  waiting for transfers between devices  378 us (48%)
  matrix products  122 us (16%)
  starting transfers between devices  111 us (14%)
  local copies, waits for them, and re-layouts  86.5 us (11%)
  other arithmetic  55.1 us (7%)
  between operations  16.1 us (2%)
    ppermute x78, waiting for transfers between devices, swap(): lax.ppermute(pieces[k], 'slide', peers(k, count))  222 us
    ppermute x78, starting transfers between devices, swap(): lax.ppermute(pieces[k], 'slide', peers(k, count))  95.4 us
    all_gather x7, waiting for transfers between devices, gather_blk(): return lax.all_gather(piece, 'blk', axis=axis, tiled=True)  80 us
    all_to_all x4, waiting for transfers between devices, to_heads(): lax.all_to_all(rows.reshape(blocks, cells, rows.shape[-1]), 'blk', 0, 0,...  75.8 us
    unnamed x227, local copies, waits for them, and re-layouts  51.8 us
    dot_general x12, matrix products, contract_cols(): lax.dot_general(former, latter, (((1,), (1,)), ((), ())), preferred_eleme...  33.1 us
    dot_general x6, matrix products, contract_rows(): lax.dot_general(former, latter, (((0,), (0,)), ((), ())), preferred_eleme...  25.7 us
    dot_general x4, matrix products, split_model(): jnp.dot(part, embedding, preferred_element_type=jnp.float32)  18.5 us
  transfers between devices with their start and end apart: 96, of which 49 were waited for; matrix products, arithmetic and copies ran while one was open for 29% of the time, Pallas kernels for 0%

profile of v1, /device:TPU:0, one launch (start us, length us, event | category | flops | bytes accessed | tf_op | source)
XLA Modules:
  0.0 768.9 jit_solution(9181506467027972096)
XLA Ops:
  17.4 8.2 %convert_multiply_fusion = f32[1,128,13500]{1,0,2:T(1,128)} fusion(s32[1,128,13500]{1,0,2:T(1,128)} %param.16), kind=kLoop, calls=%fused_computation.10 | loop fusion | flops 3456000 | bytes 13824000 | tf_op jit(solution)/shard_map/mul | solution.py:458
  43.2 13.7 %collective-permute-done = bf16[128,3456]{0,1:T(8,128)(2,1)S(1)} collective-permute-done((bf16[128,3456]{0,1:T(8,128)(2,1)}, bf16[128,3456]{0,1:T(8,128)(2,1)S(1)}, u32[]{:S(2)}, u32[]{:S(2)}) %collective-permute-start) | collective-permute-done | bytes 884768 | tf_op jit(solution)/shard_map/ppermute | solution.py:343
  56.8 58.7 %all-gather.8.cloned.1.call-done = bf16[1024,3456]{0,1:T(8,128)(2,1)} async-done(((bf16[128,3456]{0,1:T(8,128)(2,1)}), bf16[1024,3456]{0,1:T(8,128)(2,1)}) %all-gather.8.cloned.1.call-update) | async-done | bytes 7077904 | tf_op jit(solution)/shard_map/all_gather | solution.py:371
  129.6 8.1 %collective-permute-done.3 = bf16[128,1024]{1,0:T(8,128)(2,1)S(1)} collective-permute-done((bf16[128,1024]{1,0:T(8,128)(2,1)S(1)}, bf16[128,1024]{1,0:T(8,128)(2,1)S(1)}, u32[]{:S(2)}, u32[]{:S(2)}) %collective-permute-start.3) | collective-permute-done | bytes 262176 | tf_op jit(solution)/shard_map/ppermute | solution.py:343
  142.0 6.5 collective-permute-done.8
  168.7 23.4 %all-to-all-done = bf16[8,128,384]{2,1,0:T(8,128)(2,1)S(1)} async-done(((bf16[8,128,384]{2,1,0:T(8,128)(2,1)}), bf16[8,128,384]{2,1,0:T(8,128)(2,1)S(1)}, u32[]{:S(2)}, u32[]{:S(2)}) %all-to-all-start) | async-done | bytes 786464 | tf_op jit(solution)/shard_map/all_to_all | solution.py:471
  209.9 14.0 %all-to-all-done.1 = bf16[8,128,128]{2,1,0:T(8,128)(2,1)S(1)} async-done(((bf16[8,128,128]{2,1,0:T(8,128)(2,1)}), bf16[8,128,128]{2,1,0:T(8,128)(2,1)S(1)}, u32[]{:S(2)}, u32[]{:S(2)}) %all-to-all-start.1) | async-done | bytes 262176 | tf_op jit(solution)/shard_map/all_to_all | solution.py:471
  254.5 11.6 %all-gather.16.cloned.1.call-done = bf16[1024,1024]{1,0:T(8,128)(2,1)} async-done(((bf16[128,1024]{1,0:T(8,128)(2,1)}), bf16[1024,1024]{1,0:T(8,128)(2,1)}) %all-gather.16.cloned.1.call-update) | async-done | bytes 2097168 | tf_op jit(solution)/shard_map/all_gather | solution.py:371
  289.6 6.7 all-gather.18.cloned.1.call-done
  384.5 8.1 %all-to-all-done.2 = bf16[8,128,128]{2,1,0:T(8,128)(2,1)S(1)} async-done(((bf16[8,128,128]{2,1,0:T(8,128)(2,1)}), bf16[8,128,128]{2,1,0:T(8,128)(2,1)S(1)}, u32[]{:S(2)}, u32[]{:S(2)}) %all-to-all-start.2) | async-done | bytes 262176 | tf_op jit(solution)/shard_map/all_to_all | solution.py:471
  413.4 30.4 %all-to-all-done.3 = bf16[8,128,384]{1,2,0:T(8,128)(2,1)S(1)} async-done(((bf16[8,128,384]{1,2,0:T(8,128)(2,1)}), bf16[8,128,384]{1,2,0:T(8,128)(2,1)S(1)}, u32[]{:S(2)}, u32[]{:S(2)}) %all-to-all-start.3) | async-done | bytes 786464 | tf_op jit(solution)/shard_map/all_to_all | solution.py:471
  476.3 6.0 convolution_convert_fusion.1
  496.0 8.5 %convolution_convert_fusion = bf16[1024,3456]{1,0:T(8,128)(2,1)} fusion(bf16[128,3456]{0,1:T(8,128)(2,1)} %collective-permute-done.4, bf16[128,3456]{0,1:T(8,128)(2,1)} %collective-permute-done.2, bf16[128,3456]{0,1:T(8,128)(2,1)S(1)} %copy-done.13, bf16[128,3456]{0,1:T(8,128)(2,1)S(1)} %copy-done.8, bf16[128,1024]{1,0:T(8,128)(2,1)S(1)} %collective-permute-done.46, ...), kind=kOutput, calls=%fused_computation.4 | convolution fusion | flops 3645767680 | bytes 11665408 | tf_op jit(solution)/shard_map/dot_general | solution.py:16
  514.1 19.5 %collective-permute-done.23 = bf16[128,3456]{1,0:T(8,128)(2,1)S(1)} collective-permute-done((bf16[128,3456]{1,0:T(8,128)(2,1)S(1)}, bf16[128,3456]{1,0:T(8,128)(2,1)S(1)}, u32[]{:S(2)}, u32[]{:S(2)}) %collective-permute-start.23) | collective-permute-done | bytes 884768 | tf_op jit(solution)/shard_map/ppermute | solution.py:343
  533.5 16.3 %collective-permute-done.22 = bf16[128,3456]{1,0:T(8,128)(2,1)S(1)} collective-permute-done((bf16[128,3456]{1,0:T(8,128)(2,1)S(1)}, bf16[128,3456]{1,0:T(8,128)(2,1)S(1)}, u32[]{:S(2)}, u32[]{:S(2)}) %collective-permute-start.22) | collective-permute-done | bytes 884768 | tf_op jit(solution)/shard_map/ppermute | solution.py:343
  558.2 5.9 copy.201
  567.7 6.5 convolution_convert_fusion.3
  575.7 6.3 convolution_convert_fusion.4
  598.6 18.4 %collective-permute-done.45 = bf16[128,3456]{1,0:T(8,128)(2,1)S(1)} collective-permute-done((bf16[128,3456]{1,0:T(8,128)(2,1)}, bf16[128,3456]{1,0:T(8,128)(2,1)S(1)}, u32[]{:S(2)}, u32[]{:S(2)}) %collective-permute-start.45) | collective-permute-done | bytes 884768 | tf_op jit(solution)/shard_map/ppermute | solution.py:343
  676.3 8.5 %collective-permute-done.76 = bf16[64,3456]{1,0:T(8,128)(2,1)S(1)} collective-permute-done((bf16[64,3456]{1,0:T(8,128)(2,1)}, bf16[64,3456]{1,0:T(8,128)(2,1)S(1)}, u32[]{:S(2)}, u32[]{:S(2)}) %collective-permute-start.76) | collective-permute-done | bytes 442400 | tf_op jit(solution)/shard_map/ppermute | solution.py:343
  691.8 18.2 %collective-permute-done.50 = bf16[128,3456]{1,0:T(8,128)(2,1)S(1)} collective-permute-done((bf16[128,3456]{1,0:T(8,128)(2,1)}, bf16[128,3456]{1,0:T(8,128)(2,1)S(1)}, u32[]{:S(2)}, u32[]{:S(2)}) %collective-permute-start.50) | collective-permute-done | bytes 884768 | tf_op jit(solution)/shard_map/ppermute | solution.py:343
  710.0 18.0 %collective-permute-done.49 = bf16[128,3456]{1,0:T(8,128)(2,1)S(1)} collective-permute-done((bf16[128,3456]{1,0:T(8,128)(2,1)}, bf16[128,3456]{1,0:T(8,128)(2,1)S(1)}, u32[]{:S(2)}, u32[]{:S(2)}) %collective-permute-start.49) | collective-permute-done | bytes 884768 | tf_op jit(solution)/shard_map/ppermute | solution.py:343
  734.6 8.2 %copy.203 = f32[128,13500]{0,1:T(8,128)} copy(f32[128,13500]{1,0:T(8,128)} %fusion.23) | data formatting | bytes 13824000
  746.9 15.3 %copy.202 = f32[1,128,13500]{1,0,2:T(1,128)} copy(f32[1,128,13500]{2,1,0:T(8,128)} %fusion.25) | data formatting | bytes 13824000
  (599 shorter events, 408.0 us)
Async XLA Ops:
  10.7 104.8 %all-gather.8.cloned.1.call-start = ((), (), s32[]{:S(2)}) async-start(), calls=%async_computation.11 | async-start | bytes 7962624 | tf_op jit(solution)/shard_map/all_gather | solution.py:371
  13.4 193.2 %all-gather.20.cloned.1.call-start = ((), (), s32[]{:S(2)}) async-start(), calls=%async_computation.17 | async-start | bytes 3981312 | tf_op jit(solution)/shard_map/all_gather | solution.py:371
  14.3 219.2 %all-gather.12.cloned.1.call-start = ((), (), s32[]{:S(2)}) async-start(), calls=%async_computation.13 | async-start | bytes 2359296 | tf_op jit(solution)/shard_map/all_gather | solution.py:371
  14.9 231.9 %all-gather.14.cloned.1.call-start = ((), (), s32[]{:S(2)}) async-start(), calls=%async_computation.14 | async-start | bytes 2359296 | tf_op jit(solution)/shard_map/all_gather | solution.py:371
  17.3 248.8 %all-gather.16.cloned.1.call-start = ((), (), s32[]{:S(2)}) async-start(), calls=%async_computation.15 | async-start | bytes 2359296 | tf_op jit(solution)/shard_map/all_gather | solution.py:371
  36.1 85.2 %collective-permute-start.2 = (bf16[128,3456]{0,1:T(8,128)(2,1)}, bf16[128,3456]{0,1:T(8,128)(2,1)}, u32[]{:S(2)}, u32[]{:S(2)}) collective-permute-start(bf16[128,3456]{0,1:T(8,128)(2,1)} %get-tuple-element.104), channel_id=1, source_target_pairs={{0,16},{8,24},{16,0},{24,8},{1,17},{9,25},{17,1},{25,9},{2,18},{10... | collective-permute-start | bytes 2654216 | tf_op jit(solution)/shard_map/ppermute | solution.py:343
  37.6 87.7 %collective-permute-start.4 = (bf16[128,3456]{0,1:T(8,128)(2,1)}, bf16[128,3456]{0,1:T(8,128)(2,1)}, u32[]{:S(2)}, u32[]{:S(2)}) collective-permute-start(bf16[128,3456]{0,1:T(8,128)(2,1)} %get-tuple-element.105), channel_id=1, source_target_pairs={{0,24},{8,16},{16,8},{24,0},{1,25},{9,17},{17,9},{25,1},{2,26},{10... | collective-permute-start | bytes 2654216 | tf_op jit(solution)/shard_map/ppermute | solution.py:343
  154.6 37.5 %all-to-all-start = ((bf16[8,128,384]{2,1,0:T(8,128)(2,1)}), bf16[8,128,384]{2,1,0:T(8,128)(2,1)S(1)}, u32[]{:S(2)}, u32[]{:S(2)}) async-start(bf16[8,128,384]{2,1,0:T(8,128)(2,1)} %bitcast.15), calls=%async_computation | async-start | bytes 1572864 | tf_op jit(solution)/shard_map/all_to_all | solution.py:471
  158.1 138.2 %all-gather.18.cloned.1.call-start = ((), (), s32[]{:S(2)}) async-start(), calls=%async_computation.16 | async-start | bytes 2359296 | tf_op jit(solution)/shard_map/all_gather | solution.py:371
  163.1 62.7 %collective-permute-start.24 = (bf16[128,3456]{0,1:T(8,128)(2,1)}, bf16[128,3456]{0,1:T(8,128)(2,1)}, u32[]{:S(2)}, u32[]{:S(2)}) collective-permute-start(bf16[128,3456]{0,1:T(8,128)(2,1)} %get-tuple-element.99), channel_id=1, source_target_pairs={{0,8},{8,0},{16,24},{24,16},{1,9},{9,1},{17,25},{25,17},{2,10},{10... | collective-permute-start | bytes 2654216 | tf_op jit(solution)/shard_map/ppermute | solution.py:343
  164.3 74.3 %collective-permute-start.26 = (bf16[128,3456]{0,1:T(8,128)(2,1)}, bf16[128,3456]{0,1:T(8,128)(2,1)}, u32[]{:S(2)}, u32[]{:S(2)}) collective-permute-start(bf16[128,3456]{0,1:T(8,128)(2,1)} %get-tuple-element.100), channel_id=1, source_target_pairs={{0,16},{8,24},{16,0},{24,8},{1,17},{9,25},{17,1},{25,9},{2,18},{10... | collective-permute-start | bytes 2654216 | tf_op jit(solution)/shard_map/ppermute | solution.py:343
  165.1 107.9 %collective-permute-start.28 = (bf16[128,3456]{0,1:T(8,128)(2,1)}, bf16[128,3456]{0,1:T(8,128)(2,1)}, u32[]{:S(2)}, u32[]{:S(2)}) collective-permute-start(bf16[128,3456]{0,1:T(8,128)(2,1)} %get-tuple-element.101), channel_id=1, source_target_pairs={{0,24},{8,16},{16,8},{24,0},{1,25},{9,17},{17,9},{25,1},{2,26},{10... | collective-permute-start | bytes 2654216 | tf_op jit(solution)/shard_map/ppermute | solution.py:343
  206.4 345.3 %reduce-scatter.18.cloned.1.call-start = ((), (), s32[]{:S(2)}) async-start(), calls=%async_computation.22 | async-start | bytes 589824 | tf_op jit(solution)/shard_map/reduce_scatter | solution.py:375
  232.1 68.1 %collective-permute-start.25 = (bf16[128,512]{1,0:T(8,128)(2,1)}, bf16[128,512]{1,0:T(8,128)(2,1)}, u32[]{:S(2)}, u32[]{:S(2)}) collective-permute-start(bf16[128,512]{1,0:T(8,128)(2,1)} %convolution_convert_fusion.19), channel_id=1, source_target_pairs={{0,8},{8,0},{16,24},{24,16},{1,9},{9,1},{17,25},{25,17},{2,10},{10... | collective-permute-start | bytes 393224 | tf_op jit(solution)/shard_map/ppermute | solution.py:343
  246.5 53.8 %collective-permute-start.27 = (bf16[128,512]{1,0:T(8,128)(2,1)}, bf16[128,512]{1,0:T(8,128)(2,1)}, u32[]{:S(2)}, u32[]{:S(2)}) collective-permute-start(bf16[128,512]{1,0:T(8,128)(2,1)} %convolution_convert_fusion.18), channel_id=1, source_target_pairs={{0,16},{8,24},{16,0},{24,8},{1,17},{9,25},{17,1},{25,9},{2,18},{10... | collective-permute-start | bytes 393224 | tf_op jit(solution)/shard_map/ppermute | solution.py:343
  335.2 229.0 %reduce-scatter.12.cloned.1.call-start = ((), (), s32[]{:S(2)}) async-start(), calls=%async_computation.19 | async-start | bytes 589824 | tf_op jit(solution)/shard_map/reduce_scatter | solution.py:375
  363.3 227.7 %reduce-scatter.16.cloned.1.call-start = ((), (), s32[]{:S(2)}) async-start(), calls=%async_computation.21 | async-start | bytes 2359296 | tf_op jit(solution)/shard_map/reduce_scatter | solution.py:375
  381.6 238.5 %reduce-scatter.14.cloned.1.call-start = ((), (), s32[]{:S(2)}) async-start(), calls=%async_computation.20 | async-start | bytes 2359296 | tf_op jit(solution)/shard_map/reduce_scatter | solution.py:375
  412.4 227.0 %reduce-scatter.22.cloned.1.call-start = ((), (), s32[]{:S(2)}) async-start(), calls=%async_computation.24 | async-start | bytes 2064384
  468.3 193.8 %reduce-scatter.20.cloned.1.call-start = ((), (), s32[]{:S(2)}) async-start(), calls=%async_computation.23 | async-start | bytes 3981312 | tf_op jit(solution)/shard_map/reduce_scatter | solution.py:375
  482.3 203.9 %reduce-scatter.10.cloned.1.call-start = ((), (), s32[]{:S(2)}) async-start(), calls=%async_computation.18 | async-start | bytes 7962624 | tf_op jit(solution)/shard_map/reduce_scatter | solution.py:375
  511.6 38.3 %collective-permute-start.22 = (bf16[128,3456]{1,0:T(8,128)(2,1)S(1)}, bf16[128,3456]{1,0:T(8,128)(2,1)S(1)}, u32[]{:S(2)}, u32[]{:S(2)}) collective-permute-start(bf16[128,3456]{1,0:T(8,128)(2,1)S(1)} %get-tuple-element.97), channel_id=1, source_target_pairs={{0,16},{8,24},{16,0},{24,8},{1,17},{9,25},{17,1},{25,9},{2,18},{10... | collective-permute-start | bytes 2654216 | tf_op jit(solution)/shard_map/ppermute | solution.py:343
  687.8 40.2 %collective-permute-start.49 = (bf16[128,3456]{1,0:T(8,128)(2,1)}, bf16[128,3456]{1,0:T(8,128)(2,1)S(1)}, u32[]{:S(2)}, u32[]{:S(2)}) collective-permute-start(bf16[128,3456]{1,0:T(8,128)(2,1)} %reduce-scatter.10.cloned.1.call-done), channel_id=1, source_target_pairs={{0,16},{8,24},{16,0},{24,8},{1,17},{9,25},{17,1},{25,9},{2,18},{10... | collective-permute-start | bytes 2654216 | tf_op jit(solution)/shard_map/ppermute | solution.py:343
  688.5 39.5 %collective-permute-start.48 = (bf16[128,3456]{1,0:T(8,128)(2,1)}, bf16[128,3456]{1,0:T(8,128)(2,1)S(1)}, u32[]{:S(2)}, u32[]{:S(2)}) collective-permute-start(bf16[128,3456]{1,0:T(8,128)(2,1)} %reduce-scatter.10.cloned.1.call-done), channel_id=1, source_target_pairs={{0,8},{8,0},{16,24},{24,16},{1,9},{9,1},{17,25},{25,17},{2,10},{10... | collective-permute-start | bytes 2654216 | tf_op jit(solution)/shard_map/ppermute | solution.py:343
  (176 other events, 2192.5 us)
Sparse Core Ops, SparseCore 0:
  10.8 31.5 all-gather.9
  44.6 70.8 all-gather.7
  117.7 39.6 all-gather.19
  158.9 38.4 all-gather.11
  198.9 36.8 all-gather.13
  237.8 28.2 all-gather.15
  267.7 28.5 all-gather.17
  335.3 28.5 reduce-scatter.17
  366.9 29.7 reduce-scatter.11
  399.4 40.5 reduce-scatter.15
  442.8 40.4 reduce-scatter.13
  485.5 33.9 reduce-scatter.21
  522.4 42.0 reduce-scatter.19
  566.8 75.7 reduce-scatter.9

commit v2 on v1

--- a/solution.py
+++ b/solution.py
@@ -1,8 +1,11 @@
+import functools
 import math
 
 import jax
 import jax.numpy as jnp
 from jax import lax
+from jax.experimental import pallas as pl
+from jax.experimental.pallas import tpu as pltpu
 from jax.sharding import PartitionSpec as P
 
 HEADS = 16
@@ -348,6 +351,10 @@
     return swap([rows] * count)
 
 
+def after(value, *earlier):
+    return lax.optimization_barrier((value,) + earlier)[0]
+
+
 def in_order(pieces, me, axis):
     stacked = jnp.stack(pieces)
     return jnp.concatenate(
@@ -371,15 +378,600 @@
     return lax.all_gather(piece, "blk", axis=axis, tiled=True)
 
 
-def scatter_blk(piece):
-    return lax.psum_scatter(
-        piece.astype(jnp.bfloat16), "blk", scatter_dimension=0, tiled=True
-    )
+def scatter_blk(piece, axis=0):
+    return lax.psum_scatter(piece, "blk", scatter_dimension=axis, tiled=True)
 
 
 def split_rows(rows, count):
     height = rows.shape[0] // count
     return [rows[k * height : (k + 1) * height] for k in range(count)]
+
+
+ROWS = 432
+TALL = 1728
+WIDE = 3456
+CHUNKS = 2
+SMALL = 16
+COST = pl.CostEstimate(flops=0, bytes_accessed=0, transcendentals=0)
+
+
+def expression_kernel(count, quarter, genes, me_ref, library_ref, counts_ref, *rest):
+    outs, buffers, sems = rest[:count], rest[count], rest[count + 1]
+    me = me_ref[0]
+    tail = genes - (count - 1) * quarter
+    library = library_ref[...].astype(jnp.float32)
+
+    def copy(k, rows):
+        start = pl.multiple_of(jnp.bitwise_xor(me, k) * quarter, 8)
+        return pltpu.make_async_copy(
+            counts_ref.at[pl.ds(start, rows), 0, :],
+            buffers.at[k, pl.ds(0, rows), :],
+            sems.at[k],
+        )
+
+    def each(k, act):
+        last = jnp.bitwise_xor(me, k) == count - 1
+
+        @pl.when(last)
+        def _():
+            act(copy(k, tail))
+
+        @pl.when(jnp.logical_not(last))
+        def _():
+            act(copy(k, quarter))
+
+    order = list(range(1, count)) + [0]
+    for k in order:
+        each(k, lambda one: one.start())
+    for k in order:
+        each(k, lambda one: one.wait())
+        have = genes - jnp.bitwise_xor(me, k) * quarter
+
+        @pl.loop(0, quarter // ROWS)
+        def _(step):
+            start = pl.multiple_of(step * ROWS, ROWS)
+            values = buffers[k, pl.ds(start, ROWS), :].astype(jnp.float32)
+            values = jnp.log1p(values * 10000.0 / library)
+            row = start + lax.broadcasted_iota(jnp.int32, values.shape, 0)
+            outs[k][pl.ds(start, ROWS), :] = jnp.where(row < have, values, 0.0).astype(jnp.bfloat16)
+
+
+def expression_parts(counts, library, me, count, quarter):
+    genes = counts.shape[2]
+    cells = counts.shape[1]
+    part = jax.ShapeDtypeStruct((quarter, cells), jnp.bfloat16)
+    return pl.pallas_call(
+        functools.partial(expression_kernel, count, quarter, genes),
+        out_shape=[part] * count,
+        in_specs=[
+            pl.BlockSpec(memory_space=pltpu.SMEM),
+            pl.BlockSpec(memory_space=pltpu.VMEM),
+            pl.BlockSpec(memory_space=pltpu.HBM),
+        ],
+        out_specs=[pl.BlockSpec(memory_space=pltpu.VMEM)] * count,
+        scratch_shapes=[
+            pltpu.VMEM((count, quarter, cells), jnp.int32),
+            pltpu.SemaphoreType.DMA((count,)),
+        ],
+        compiler_params=pltpu.CompilerParams(vmem_limit_bytes=40 * 2**20),
+        cost_estimate=COST,
+        name="expression",
+    )(me.reshape(1), library, jnp.transpose(counts, (2, 0, 1)))
+
+
+def spread_kernel(count, quarter, genes, me_ref, *rest):
+    pieces, out, held, wide, sems_in, sems_out = rest[:count], *rest[count:]
+    me = me_ref[0]
+    tail = genes - (count - 1) * quarter
+
+    def arrive(k):
+        return pltpu.make_async_copy(pieces[k], held.at[k], sems_in.at[k])
+
+    def leave(k):
+        rows = tail if k == count - 1 else quarter
+        return pltpu.make_async_copy(
+            wide.at[k, pl.ds(0, rows), :], out.at[pl.ds(k * quarter, rows), 0, :], sems_out.at[k]
+        )
+
+    for k in range(count):
+        arrive(k).start()
+    for k in range(count):
+        arrive(k).wait()
+    for k in range(count):
+        source = jnp.bitwise_xor(me, k)
+
+        @pl.loop(0, quarter // ROWS)
+        def _(step):
+            rows = pl.ds(pl.multiple_of(step * ROWS, ROWS), ROWS)
+            wide[k, rows, :] = held[source, rows, :].astype(jnp.float32)
+
+        leave(k).start()
+    for k in range(count):
+        leave(k).wait()
+
+
+def spread_parts(pieces, me, genes):
+    count = len(pieces)
+    quarter, cells = pieces[0].shape
+    out = pl.pallas_call(
+        functools.partial(spread_kernel, count, quarter, genes),
+        out_shape=jax.ShapeDtypeStruct((genes, 1, cells), jnp.float32),
+        in_specs=[pl.BlockSpec(memory_space=pltpu.SMEM)]
+        + [pl.BlockSpec(memory_space=pl.ANY)] * count,
+        out_specs=pl.BlockSpec(memory_space=pltpu.HBM),
+        scratch_shapes=[
+            pltpu.VMEM((count, quarter, cells), jnp.bfloat16),
+            pltpu.VMEM((count, quarter, cells), jnp.float32),
+            pltpu.SemaphoreType.DMA((count,)),
+            pltpu.SemaphoreType.DMA((count,)),
+        ],
+        compiler_params=pltpu.CompilerParams(vmem_limit_bytes=40 * 2**20),
+        cost_estimate=COST,
+        name="spread",
+    )(me.reshape(1), *pieces)
+    return jnp.transpose(out, (1, 2, 0))
+
+
+def join_kernel(count, me_ref, *rest):
+    pieces, out, held, sems = rest[:count], *rest[count:]
+    slot = pl.program_id(0)
+
+    def arrive(k):
+        rows = pl.ds(0, held.shape[1])
+        return pltpu.make_async_copy(pieces[k].at[rows, :], held.at[k], sems.at[k])
+
+    @pl.when(slot == 0)
+    def _():
+        for k in range(count):
+            arrive(k).start()
+        for k in range(count):
+            arrive(k).wait()
+
+    source = jnp.bitwise_xor(me_ref[0], slot)
+
+    @pl.loop(0, out.shape[0] // ROWS)
+    def _(step):
+        rows = pl.ds(pl.multiple_of(step * ROWS, ROWS), ROWS)
+        out[rows, :] = held[source, rows, :].astype(out.dtype)
+
+
+def join_parts(pieces, me, quarter, genes, dtype):
+    count = len(pieces)
+    cells = pieces[0].shape[1]
+    return pl.pallas_call(
+        functools.partial(join_kernel, count),
+        grid=(count,),
+        out_shape=jax.ShapeDtypeStruct((genes, cells), dtype),
+        in_specs=[pl.BlockSpec(memory_space=pltpu.SMEM)]
+        + [pl.BlockSpec(memory_space=pl.ANY)] * count,
+        out_specs=pl.BlockSpec((quarter, cells), lambda slot: (slot, 0)),
+        scratch_shapes=[
+            pltpu.VMEM((count, quarter, cells), jnp.bfloat16),
+            pltpu.SemaphoreType.DMA((count,)),
+        ],
+        compiler_params=pltpu.CompilerParams(vmem_limit_bytes=40 * 2**20),
+        cost_estimate=COST,
+        name="join",
+    )(me.reshape(1), *pieces)
+
+
+def turn_kernel(count, *refs):
+    out = refs[-1]
+    for k in range(count):
+        height = refs[k].shape[1]
+        out[k * height : (k + 1) * height, :] = jnp.transpose(refs[k][...])
+
+
+def turn_parts(parts):
+    count = len(parts)
+    quarter, cells = parts[0].shape
+    return pl.pallas_call(
+        functools.partial(turn_kernel, count),
+        grid=(quarter // WIDE,),
+        out_shape=jax.ShapeDtypeStruct((count * cells, quarter), jnp.bfloat16),
+        in_specs=[pl.BlockSpec((WIDE, cells), lambda step: (step, 0))] * count,
+        out_specs=pl.BlockSpec((count * cells, WIDE), lambda step: (0, step)),
+        compiler_params=pltpu.CompilerParams(vmem_limit_bytes=40 * 2**20),
+        cost_estimate=COST,
+        name="turn_parts",
+    )(*parts)
+
+
+def scores_kernel(rows, table, *refs):
+    outs, total = refs[:-1], refs[-1]
+    step = pl.program_id(0)
+    product = jnp.dot(rows[...], table[...], preferred_element_type=jnp.float32)
+
+    @pl.when(step == 0)
+    def _():
+        total[...] = product
+
+    @pl.when(step > 0)
+    def _():
+        total[...] += product
+
+    @pl.when(step == pl.num_programs(0) - 1)
+    def _():
+        height = outs[0].shape[0]
+        for k in range(len(outs)):
+            outs[k][...] = total[k * height : (k + 1) * height, :].astype(outs[k].dtype)
+
+
+def embed_cells(rows, table, count):
+    height, quarter = rows.shape
+    width = table.shape[1]
+    return pl.pallas_call(
+        scores_kernel,
+        grid=(quarter // WIDE,),
+        out_shape=[
+            jax.ShapeDtypeStruct((height // count, width), jnp.float32 if k == 0 else jnp.bfloat16)
+            for k in range(count)
+        ],
+        in_specs=[
+            pl.BlockSpec((height, WIDE), lambda step: (0, step)),
+            pl.BlockSpec((WIDE, width), lambda step: (step, 0)),
+        ],
+        out_specs=[pl.BlockSpec((height // count, width), lambda step: (0, 0))] * count,
+        scratch_shapes=[pltpu.VMEM((height, width), jnp.float32)],
+        compiler_params=pltpu.CompilerParams(vmem_limit_bytes=58 * 2**20),
+        cost_estimate=COST,
+        name="embed_cells",
+    )(rows, table)
+
+
+def latents_kernel(count, table, *refs):
+    cots, outs, total = refs[:count], refs[count:-1], refs[-1]
+    step = pl.program_id(0)
+    product = jnp.dot(
+        table[...],
+        jnp.concatenate([one[...] for one in cots], axis=1),
+        preferred_element_type=jnp.float32,
+    )
+
+    @pl.when(step == 0)
+    def _():
+        total[...] = product
+
+    @pl.when(step > 0)
+    def _():
+        total[...] += product
+
+    @pl.when(step == pl.num_programs(0) - 1)
+    def _():
+        cells = outs[0].shape[0]
+        for k in range(count):
+            outs[k][...] = jnp.transpose(total[:, k * cells : (k + 1) * cells]).astype(
+                outs[k].dtype
+            )
+
+
+def cots_to_latents(cots, table):
+    count = len(cots)
+    width, quarter = table.shape
+    cells = cots[0].shape[1]
+    return pl.pallas_call(
+        functools.partial(latents_kernel, count),
+        grid=(quarter // WIDE,),
+        out_shape=[
+            jax.ShapeDtypeStruct((cells, width), jnp.float32 if k == 0 else jnp.bfloat16)
+            for k in range(count)
+        ],
+        in_specs=[pl.BlockSpec((width, WIDE), lambda step: (0, step))]
+        + [pl.BlockSpec((WIDE, cells), lambda step: (step, 0))] * count,
+        out_specs=[pl.BlockSpec((cells, width), lambda step: (0, 0))] * count,
+        scratch_shapes=[pltpu.VMEM((width, count * cells), jnp.float32)],
+        compiler_params=pltpu.CompilerParams(vmem_limit_bytes=40 * 2**20),
+        cost_estimate=COST,
+        name="cots_to_latents",
+    )(table, *cots)
+
+
+def decode_kernel(count, table, *refs):
+    rows, outs = refs[:count], refs[count:]
+    cells = rows[0].shape[0]
+    product = jnp.dot(
+        jnp.concatenate([one[...] for one in rows], axis=0),
+        table[...],
+        preferred_element_type=jnp.float32,
+    ).astype(jnp.bfloat16)
+    for k in range(count):
+        outs[k][...] = jnp.transpose(product[k * cells : (k + 1) * cells, :])
+
+
+def decode_genes(latents, table):
+    count = len(latents)
+    width, quarter = table.shape
+    cells = latents[0].shape[0]
+    return pl.pallas_call(
+        functools.partial(decode_kernel, count),
+        grid=(quarter // WIDE,),
+        out_shape=[jax.ShapeDtypeStruct((quarter, cells), jnp.bfloat16)] * count,
+        in_specs=[pl.BlockSpec((width, WIDE), lambda step: (0, step))]
+        + [pl.BlockSpec((cells, width), lambda step: (0, 0))] * count,
+        out_specs=[pl.BlockSpec((WIDE, cells), lambda step: (step, 0))] * count,
+        compiler_params=pltpu.CompilerParams(vmem_limit_bytes=40 * 2**20),
+        cost_estimate=COST,
+        name="decode_genes",
+    )(table, *latents)
+
+
+def genes_kernel(count, table, *refs):
+    rows, outs, stacked = refs[:count], refs[count : 2 * count], refs[-1]
+    cells = rows[0].shape[0]
+
+    @pl.when(pl.program_id(0) == 0)
+    def _():
+        for k in range(count):
+            stacked[:, k * cells : (k + 1) * cells] = jnp.transpose(rows[k][...])
+
+    product = jnp.dot(table[...], stacked[...], preferred_element_type=jnp.float32)
+    for k in range(count):
+        outs[k][...] = product[:, k * cells : (k + 1) * cells].astype(outs[k].dtype)
+
+
+def cells_to_genes(table, rows, quarter):
+    count = len(rows)
+    cells, width = rows[0].shape
+    return pl.pallas_call(
+        functools.partial(genes_kernel, count),
+        grid=(quarter // TALL,),
+        out_shape=[jax.ShapeDtypeStruct((quarter, cells), jnp.bfloat16)] * count,
+        in_specs=[pl.BlockSpec((TALL, width), lambda step: (step, 0))]
+        + [pl.BlockSpec((cells, width), lambda step: (0, 0))] * count,
+        out_specs=[pl.BlockSpec((TALL, cells), lambda step: (step, 0))] * count,
+        scratch_shapes=[pltpu.VMEM((width, count * cells), jnp.bfloat16)],
+        compiler_params=pltpu.CompilerParams(vmem_limit_bytes=58 * 2**20),
+        cost_estimate=COST,
+        name="cells_to_genes",
+    )(table, *rows)
+
+
+def embed_kernel(count, *refs):
+    parts, rows = refs[:count], refs[count : 2 * count]
+    small, out, stacked, results, sems = refs[2 * count :]
+    steps = parts[0].shape[0] // ROWS
+    height = rows[0].shape[0]
+    blocks, _, block = out.shape
+    for k in range(count):
+        stacked[k * height : (k + 1) * height, :] = rows[k][...]
+
+    def leave(slot, step):
+        start = pl.multiple_of(step * ROWS, ROWS)
+        return pltpu.make_async_copy(
+            results.at[slot], out.at[:, pl.ds(start, ROWS), :], sems.at[slot]
+        )
+
+    last = pltpu.make_async_copy(
+        small, out.at[:, pl.ds(steps * ROWS, small.shape[1]), :], sems.at[2]
+    )
+    last.start()
+
+    @pl.loop(0, steps)
+    def _(step):
+        slot = lax.rem(step, 2)
+
+        @pl.when(step >= 2)
+        def _():
+            leave(slot, step - 2).wait()
+
+        here = pl.ds(pl.multiple_of(step * ROWS, ROWS), ROWS)
+        product = jnp.dot(
+            jnp.concatenate([part[here, :] for part in parts], axis=1),
+            stacked[...],
+            preferred_element_type=jnp.float32,
+        ).astype(results.dtype)
+        for k in range(blocks):
+            results[slot, k] = product[:, k * block : (k + 1) * block]
+        leave(slot, step).start()
+
+    for step in range(max(steps - 2, 0), steps):
+        leave(step % 2, step).wait()
+    last.wait()
+
+
+def embed_products(parts, rows, small):
+    count = len(parts)
+    quarter, cells = parts[0].shape
+    width = rows[0].shape[1]
+    blocks, extra, block = small.shape
+    return pl.pallas_call(
+        functools.partial(embed_kernel, count),
+        out_shape=jax.ShapeDtypeStruct((blocks, quarter + extra, block), jnp.bfloat16),
+        in_specs=[pl.BlockSpec(memory_space=pltpu.VMEM)] * (2 * count + 1),
+        out_specs=pl.BlockSpec(memory_space=pltpu.HBM),
+        scratch_shapes=[
+            pltpu.VMEM((count * cells, width), jnp.bfloat16),
+            pltpu.VMEM((2, blocks, ROWS, block), jnp.bfloat16),
+            pltpu.SemaphoreType.DMA((3,)),
+        ],
+        compiler_params=pltpu.CompilerParams(vmem_limit_bytes=40 * 2**20),
+        cost_estimate=COST,
+        name="embed_products",
+    )(*parts, *rows, small)
+
+
+def products_kernel(count, *refs):
+    out = refs[-1]
+    spot = 0
+    for k in range(count):
+        rows = jnp.transpose(refs[2 * k][...])
+        columns = refs[2 * k + 1]
+        width = columns.shape[1]
+        for start in range(0, width, 256):
+            out[:, spot + start : spot + start + 256] = jnp.dot(
+                rows, columns[:, start : start + 256], preferred_element_type=jnp.float32
+            ).astype(out.dtype)
+        spot += width
+
+
+def row_products(pairs):
+    operands = [one for pair in pairs for one in pair]
+    height = pairs[0][0].shape[1]
+    width = sum(b.shape[1] for _, b in pairs)
+    return pl.pallas_call(
+        functools.partial(products_kernel, len(pairs)),
+        out_shape=jax.ShapeDtypeStruct((height, width), jnp.bfloat16),
+        in_specs=[pl.BlockSpec(memory_space=pltpu.VMEM)] * len(operands),
+        out_specs=pl.BlockSpec(memory_space=pltpu.VMEM),
+        compiler_params=pltpu.CompilerParams(vmem_limit_bytes=48 * 2**20),
+        cost_estimate=COST,
+        name="row_products",
+    )(*operands)
+
+
+def decoder_kernel(count, *refs):
+    rows, cots, out, turned = refs[:count], refs[count : 2 * count], refs[-2], refs[-1]
+    cells = rows[0].shape[0]
+
+    @pl.when(pl.program_id(0) == 0)
+    def _():
+        for k in range(count):
+            turned[:, k * cells : (k + 1) * cells] = jnp.transpose(rows[k][...])
+
+    out[...] = lax.dot_general(
+        turned[...],
+        jnp.concatenate([one[...] for one in cots], axis=1),
+        (((1,), (1,)), ((), ())),
+        preferred_element_type=jnp.float32,
+    ).astype(out.dtype)
+
+
+def decoder_products(latents, cots):
+    count = len(latents)
+    cells, width = latents[0].shape
+    quarter = cots[0].shape[0]
+    step_rows = math.gcd(quarter, 1152)
+    return pl.pallas_call(
+        functools.partial(decoder_kernel, count),
+        grid=(quarter // step_rows,),
+        out_shape=jax.ShapeDtypeStruct((width, quarter), jnp.bfloat16),
+        in_specs=[pl.BlockSpec((cells, width), lambda step: (0, 0))] * count
+        + [pl.BlockSpec((step_rows, cells), lambda step: (step, 0))] * count,
+        out_specs=pl.BlockSpec((width, step_rows), lambda step: (0, step)),
+        scratch_shapes=[pltpu.VMEM((width, count * cells), jnp.bfloat16)],
+        compiler_params=pltpu.CompilerParams(vmem_limit_bytes=40 * 2**20),
+        cost_estimate=COST,
+        name="decoder_products",
+    )(*latents, *cots)
+
+
+def head_probs(keys, queries, scaling):
+    scores = (
+        lax.dot_general(keys, queries, (((1,), (1,)), ((), ())), preferred_element_type=jnp.float32)
+        * scaling
+    )
+    scores = jnp.exp(scores - jnp.max(scores, axis=0, keepdims=True))
+    return scores * (1.0 / jnp.sum(scores, axis=0, keepdims=True))
+
+
+def attend_kernel(heads, width, rows_ref, out, turned):
+    step = pl.program_id(0)
+    height = out.shape[0]
+    group = heads * width
+
+    @pl.when(step == 0)
+    def _():
+        turned[...] = jnp.transpose(rows_ref[:, 2 * group : 3 * group])
+
+    block = rows_ref[pl.ds(pl.multiple_of(step * height, height), height), :group]
+    results = []
+    for h in range(heads):
+        probs = head_probs(
+            rows_ref[:, group + h * width : group + (h + 1) * width],
+            block[:, h * width : (h + 1) * width],
+            width ** (-0.5),
+        ).astype(jnp.bfloat16)
+        results.append(
+            jnp.dot(turned[h * width : (h + 1) * width, :], probs, preferred_element_type=jnp.float32)
+        )
+    out[...] = jnp.transpose(jnp.concatenate(results, axis=0)).astype(out.dtype)
+
+
+def attend(rows, heads):
+    cells, total = rows.shape
+    group = total // 3
+    height = math.gcd(cells, 256)
+    return pl.pallas_call(
+        functools.partial(attend_kernel, heads, group // heads),
+        grid=(cells // height,),
+        out_shape=jax.ShapeDtypeStruct((cells, group), jnp.bfloat16),
+        in_specs=[pl.BlockSpec((cells, total), lambda step: (0, 0))],
+        out_specs=pl.BlockSpec((height, group), lambda step: (step, 0)),
+        scratch_shapes=[pltpu.VMEM((group, cells), jnp.bfloat16)],
+        compiler_params=pltpu.CompilerParams(vmem_limit_bytes=40 * 2**20),
+        cost_estimate=COST,
+        name="attend",
+    )(rows)
+
+
+def attend_back_kernel(heads, width, rows_ref, cot_ref, out, turned, key_sum, value_sum):
+    step = pl.program_id(0)
+    group = heads * width
+    height = rows_ref.shape[0] // pl.num_programs(0)
+    scaling = width ** (-0.5)
+
+    @pl.when(step == 0)
+    def _():
+        turned[...] = jnp.transpose(rows_ref[:, group : 2 * group])
+        key_sum[...] = jnp.zeros_like(key_sum)
+        value_sum[...] = jnp.zeros_like(value_sum)
+
+    here = pl.ds(pl.multiple_of(step * height, height), height)
+    block = rows_ref[here, :group]
+    cots = cot_ref[here, :]
+    results = []
+    for h in range(heads):
+        columns = slice(h * width, (h + 1) * width)
+        queries = block[:, columns]
+        cot = cots[:, columns]
+        probs = head_probs(
+            rows_ref[:, group + h * width : group + (h + 1) * width], queries, scaling
+        )
+        prob_grad = lax.dot_general(
+            rows_ref[:, 2 * group + h * width : 2 * group + (h + 1) * width],
+            cot,
+            (((1,), (1,)), ((), ())),
+            preferred_element_type=jnp.float32,
+        )
+        delta = jnp.sum(probs * prob_grad, axis=0, keepdims=True)
+        score_grad = (probs * (prob_grad - delta)).astype(jnp.bfloat16)
+        results.append(
+            jnp.dot(turned[columns, :], score_grad, preferred_element_type=jnp.float32) * scaling
+        )
+        key_sum[:, columns] += jnp.dot(score_grad, queries, preferred_element_type=jnp.float32)
+        value_sum[:, columns] += jnp.dot(
+            probs.astype(jnp.bfloat16), cot, preferred_element_type=jnp.float32
+        )
+    out[here, :group] = jnp.transpose(jnp.concatenate(results, axis=0)).astype(out.dtype)
+
+    @pl.when(step == pl.num_programs(0) - 1)
+    def _():
+        out[:, group : 2 * group] = (key_sum[...] * scaling).astype(out.dtype)
+        out[:, 2 * group :] = value_sum[...].astype(out.dtype)
+
+
+def attend_back(rows, cot, heads):
+    cells, total = rows.shape
+    group = total // 3
+    height = math.gcd(cells, 256)
+    return pl.pallas_call(
+        functools.partial(attend_back_kernel, heads, group // heads),
+        grid=(cells // height,),
+        out_shape=jax.ShapeDtypeStruct((cells, total), jnp.bfloat16),
+        in_specs=[
+            pl.BlockSpec((cells, total), lambda step: (0, 0)),
+            pl.BlockSpec((cells, group), lambda step: (0, 0)),
+        ],
+        out_specs=pl.BlockSpec((cells, total), lambda step: (0, 0)),
+        scratch_shapes=[
+            pltpu.VMEM((group, cells), jnp.bfloat16),
+            pltpu.VMEM((cells, group), jnp.float32),
+            pltpu.VMEM((cells, group), jnp.float32),
+        ],
+        compiler_params=pltpu.CompilerParams(vmem_limit_bytes=40 * 2**20),
+        cost_estimate=COST,
+        name="attend_back",
+    )(rows, cot)
 
 
 def split_model(
@@ -409,62 +1001,87 @@
     own_rows = w_qkv.shape[0]
     latent_width = w_decode.shape[0] * blocks
     mixture_count = comp_means.shape[1]
-    quarter = -(-genes // (slides * 128)) * 128
+    quarter = -(-genes // (slides * ROWS)) * ROWS
     padded = quarter * slides
     head_part = model_width // slides
     pair = model_width // blocks
     pairs = head_part // pair
     ff_part = up_bias.shape[0] // slides
-    scaling = HEAD_DIM ** (-0.5)
-
-    def gene_part(rows, place):
-        return lax.dynamic_slice_in_dim(rows, place * quarter, quarter, 1)
-
-    def pad_genes(rows):
-        return jnp.pad(rows, ((0, 0), (0, padded - genes)))
+    latent_part = model_width // slides
 
     def place_of(k):
         return jnp.bitwise_xor(me, k)
 
-    embedding = gather_blk(gene_part(pad_genes(embed_t), me))
-    qkv_part = lax.dynamic_index_in_dim(
-        w_qkv.reshape(own_rows, 3, slides, pairs, pair), me, 2, keepdims=False
-    )
-    qkv_part = jnp.transpose(qkv_part, (0, 2, 1, 3)).reshape(own_rows, pairs * 3 * pair)
+    def column_part(rows, width, place):
+        return lax.dynamic_slice_in_dim(rows, place * width, width, 1)
+
+    def whole(piece, axis):
+        return in_order(share(piece, slides), me, axis)
+
+    def wide(piece):
+        return piece.astype(jnp.float32)
+
+    embed_part = lax.dynamic_slice_in_dim(
+        jnp.pad(embed_t.T, ((0, padded - genes), (0, 0))), me * quarter, quarter, 0
+    )
     bias_part = lax.dynamic_slice_in_dim(up_bias, me * ff_part, ff_part, 0)
     mean_cols = comp_means.size // own_rows
     small = jnp.concatenate(
         [norm_params, comp_means.reshape(own_rows, mean_cols), bias_part.reshape(own_rows, -1)],
         axis=1,
-    )
-    small_cols = small.shape[1]
-    small = jnp.pad(small, ((0, 0), (0, 128 - small_cols)))
-    first = gather_blk(jnp.concatenate([qkv_part, small], axis=1))
-    weight_qkv = first[:, : pairs * 3 * pair].reshape(model_width, pairs, 3 * pair)
-    small_all = first[:, pairs * 3 * pair :]
-    norm_float = small_all[:, :4].astype(jnp.float32)
-    centres = small_all[:, 4 : 4 + mean_cols].reshape(latent_width, mixture_count)
-    bias_up = small_all[:, 4 + mean_cols : small_cols].reshape(-1).astype(jnp.float32)
-    weight_out = gather_blk(w_attn_out)
-    up_part = lax.dynamic_index_in_dim(
-        w_up.reshape(own_rows, blocks, slides, ff_part), me, 2, keepdims=False
-    ).reshape(own_rows, blocks * ff_part)
-    weight_up = gather_blk(up_part)
-    weight_down = gather_blk(lax.dynamic_slice_in_dim(w_down, me * ff_part, ff_part, 0))
-    weight_latent = gather_blk(w_latent)
-    weight_decode = gather_blk(gene_part(pad_genes(w_decode), me))
-
-    expression = jnp.log1p(
-        counts[0].astype(jnp.float32) * 10000.0 / library[0].astype(jnp.float32)[:, None]
-    )
-    expression_low = pad_genes(expression.astype(jnp.bfloat16))
-    expr_parts = swap([gene_part(expression_low, place_of(k)) for k in range(slides)])
-    h_zero = collect([contract_cols(part, embedding) for part in expr_parts])
+    ).T
+    small_rows = small.shape[0]
+    small = jnp.pad(small, ((0, SMALL - small_rows), (0, 0)))
+    qkv_width = pairs * 3 * pair
+    qkv_part = [
+        lax.dynamic_slice_in_dim(w_qkv, k * model_width + me * head_part, head_part, 1)
+        for k in range(3)
+    ]
+    qkv_part = jnp.concatenate(
+        [part[:, j * pair : (j + 1) * pair] for j in range(pairs) for part in qkv_part], axis=1
+    ).T
+    embedding = gather_blk(jnp.concatenate([embed_part, small, qkv_part], axis=0), 1)
+    small_all = embedding[quarter : quarter + SMALL]
+    weight_qkv = embedding[quarter + SMALL :].reshape(pairs, 3 * pair, model_width)
+    norm_float = small_all[:4].astype(jnp.float32)
+    centres = small_all[4 : 4 + mean_cols].T.reshape(latent_width, mixture_count)
+    bias_up = small_all[4 + mean_cols : small_rows].T.reshape(-1).astype(jnp.float32)
+    expr_parts = swap(expression_parts(counts, library, me, slides, quarter))
+
+    cot_all = jnp.pad(decoded_cot[0].T, ((0, padded - genes), (0, 0)))
+    cot_first = [
+        lax.dynamic_slice_in_dim(cot_all, place_of(k) * quarter, quarter, 0)
+        for k in range(slides)
+    ]
+    cot_parts = swap([after(piece, *expr_parts[1:]) for piece in cot_first])
+    up_part = jnp.concatenate(
+        [
+            lax.dynamic_slice_in_dim(w_up, (k * slides + me) * ff_part, ff_part, 1)
+            for k in range(blocks)
+        ],
+        axis=1,
+    )
+    down_part = lax.dynamic_slice_in_dim(w_down, me * ff_part, ff_part, 0)
+    expr_rows = turn_parts(expr_parts)
+    middle = gather_blk(
+        after(
+            jnp.concatenate([w_attn_out, up_part, down_part, w_latent], axis=1),
+            embedding,
+            expr_rows,
+            *cot_parts[1:],
+        )
+    )
+    weight_out, weight_up, weight_down, weight_latent = jnp.split(middle, 4, axis=1)
+    decode_part = lax.dynamic_slice_in_dim(
+        jnp.pad(w_decode, ((0, 0), (0, padded - genes))), me * quarter, quarter, 1
+    )
+
+    h_zero = collect(embed_cells(expr_rows, embedding, slides))
     h_zero = h_zero + spatial_code(coords[0], model_width)
-    normed_one, norm_one_back = jax.vjp(layer_norm, h_zero, norm_float[:, 0], norm_float[:, 1])
+    normed_one, norm_one_back = jax.vjp(layer_norm, h_zero, norm_float[0], norm_float[1])
     normed_one_all = jnp.concatenate(share(normed_one.astype(jnp.bfloat16), slides), axis=0)
     projected = jnp.einsum(
-        "ck,kpf->pcf", normed_one_all, weight_qkv, preferred_element_type=jnp.float32
+        "ck,pfk->pcf", normed_one_all, weight_qkv, preferred_element_type=jnp.float32
     ).astype(jnp.bfloat16)
 
     def to_heads(rows):
@@ -474,35 +1091,19 @@
 
     head_rows = to_heads(projected)
     per_pair = pair // HEAD_DIM
-
-    def heads_of(rows):
-        return jnp.transpose(rows.reshape(blocks * cells, per_pair, HEAD_DIM), (1, 0, 2))
-
-    queries = heads_of(head_rows[:, :pair])
-    key_rows = heads_of(head_rows[:, pair : 2 * pair])
-    value_rows = heads_of(head_rows[:, 2 * pair :])
-    scores = (
-        jnp.einsum("htd,hkd->htk", queries, key_rows, preferred_element_type=jnp.float32)
-        * scaling
-    )
-    probs = jax.nn.softmax(scores, axis=-1)
-    probs_low = probs.astype(jnp.bfloat16)
-    head_out = jnp.einsum(
-        "htk,hkd->thd", probs_low, value_rows, preferred_element_type=jnp.float32
-    ).astype(jnp.bfloat16)
-    own_heads = to_heads(head_out.reshape(blocks * cells, pair)).reshape(
-        pairs, slides, cells, pair
-    )
+    own_heads = to_heads(attend(head_rows, per_pair)).reshape(pairs, slides, cells, pair)
+    weight_decode = gather_blk(after(decode_part, middle, own_heads))
     attended_parts = swap(
         [
-            jnp.transpose(own_heads[:, k], (1, 0, 2)).reshape(cells, head_part)
+            jnp.concatenate([own_heads[j, k] for j in range(pairs)], axis=1)
             for k in range(slides)
         ]
     )
     attended_low = in_order(attended_parts, me, 1)
     h_one = h_zero + jnp.dot(attended_low, weight_out, preferred_element_type=jnp.float32)
-    normed_two, norm_two_back = jax.vjp(layer_norm, h_one, norm_float[:, 2], norm_float[:, 3])
-    normed_two_all = jnp.concatenate(share(normed_two.astype(jnp.bfloat16), slides), axis=0)
+    normed_two, norm_two_back = jax.vjp(layer_norm, h_one, norm_float[2], norm_float[3])
+    normed_two_low = normed_two.astype(jnp.bfloat16)
+    normed_two_all = jnp.concatenate(share(normed_two_low, slides), axis=0)
     hidden_pre = (
         jnp.dot(normed_two_all, weight_up, preferred_element_type=jnp.float32) + bias_up
     )
@@ -517,148 +1118,159 @@
     latent = latent_pre[:, :latent_width] + spread * noise[0]
     prior, prior_back = jax.vjp(mixture_term, latent, centres.astype(jnp.float32))
 
-    cot_all = pad_genes(decoded_cot[0])
-    cot_parts = swap([gene_part(cot_all, place_of(k)) for k in range(slides)])
-    latent_from_decode = collect([contract_cols(part, weight_decode) for part in cot_parts])
+    latent_from_decode = collect(cots_to_latents(cot_parts, weight_decode))
     latent_from_prior, centre_grad = prior_back(prior_cot[0])
     latent_total = latent_from_decode + latent_from_prior
     pre_grad = jnp.concatenate(
         [latent_total, latent_total * noise[0] * spread * 0.5], axis=-1
     ).astype(jnp.bfloat16)
-    pre_grad_all = jnp.concatenate(share(pre_grad, slides), axis=0)
+    latent_parts = share(latent.astype(jnp.bfloat16), slides)
+    pre_grad_all = jnp.concatenate(share(after(pre_grad, *latent_parts[1:]), slides), axis=0)
+    decode_local = decoder_products(latent_parts, cot_parts)
+    pre_grad_all = after(pre_grad_all, decode_local)
+    decode_own = scatter_blk(decode_local)
     h_two_grad_all = contract_cols(pre_grad_all, weight_latent)
     down_input = h_two_grad_all.astype(jnp.bfloat16)
     hidden_grad = contract_cols(down_input, weight_down)
     pre_hidden_grad = gelu_back(hidden_grad)[0].astype(jnp.bfloat16)
-    normed_two_grad = collect(split_rows(contract_cols(pre_hidden_grad, weight_up), slides))
+    h_two_all = jnp.concatenate(share(after(h_two_low, pre_grad_all), slides), axis=0)
+    normed_two_parts = split_rows(contract_cols(pre_hidden_grad, weight_up), slides)
+    normed_two_grad = collect(normed_two_parts)
+    middle_local = row_products(
+        [
+            (hidden_low, after(down_input, normed_two_parts[-1])),
+            (normed_two_all, pre_hidden_grad),
+            (h_two_all, column_part(pre_grad_all, latent_part, me)),
+        ]
+    )
+    normed_two_grad = after(normed_two_grad, middle_local)
+    middle_grad = scatter_blk(after(middle_local, decode_own))
     h_one_part, gain_two_grad, shift_two_grad = norm_two_back(normed_two_grad)
     h_one_grad = h_two_grad_all[:cells] + h_one_part
     out_input = h_one_grad.astype(jnp.bfloat16)
     attended_grad = contract_cols(out_input, weight_out).astype(jnp.bfloat16)
 
-    def column_part(rows, width, place):
-        return lax.dynamic_slice_in_dim(rows, place * width, width, 1)
-
     grad_parts = swap([column_part(attended_grad, head_part, place_of(k)) for k in range(slides)])
-    grad_pairs = jnp.stack([part.reshape(cells, pairs, pair) for part in grad_parts])
-    grad_pairs = jnp.transpose(grad_pairs, (2, 0, 1, 3))
-    out_heads = heads_of(to_heads(grad_pairs))
-    prob_grad = jnp.einsum(
-        "htd,hkd->htk", out_heads, value_rows, preferred_element_type=jnp.float32
-    )
-    row_delta = jnp.sum(probs * prob_grad, axis=-1, keepdims=True)
-    score_grad = (probs * (prob_grad - row_delta)).astype(jnp.bfloat16)
-    query_grad = (
-        jnp.einsum("htk,hkd->thd", score_grad, key_rows, preferred_element_type=jnp.float32)
-        * scaling
-    )
-    key_grad = (
-        jnp.einsum("htk,htd->khd", score_grad, queries, preferred_element_type=jnp.float32)
-        * scaling
-    )
-    value_grad = jnp.einsum(
-        "htk,htd->khd", probs_low, out_heads, preferred_element_type=jnp.float32
-    )
-    head_grads = jnp.concatenate(
+    grad_pairs = jnp.stack(
+        [part[:, j * pair : (j + 1) * pair] for j in range(pairs) for part in grad_parts]
+    )
+    out_heads = to_heads(grad_pairs)
+
+    decoded_rows = decode_genes(
+        [after(rows, *grad_parts[1:]) for rows in latent_parts], weight_decode
+    )
+    out_heads = after(out_heads, *decoded_rows)
+    decoded_parts = swap(decoded_rows)
+    attended_all = jnp.concatenate(share(after(attended_low, *grad_parts[1:]), slides), axis=0)
+    head_grads = attend_back(head_rows, out_heads, per_pair)
+    out_parts = swap(
         [
-            part.reshape(blocks * cells, pair).astype(jnp.bfloat16)
-            for part in (query_grad, key_grad, value_grad)
-        ],
-        axis=1,
-    )
+            after(column_part(out_input, head_part, place_of(k)), *grad_parts[1:])
+            for k in range(slides)
+        ]
+    )
+    decode_shares = share(after(decode_own, *grad_parts[1:]), slides)
     projected_grad = to_heads(head_grads).reshape(pairs, slides * cells, 3 * pair)
+    projected_grad = after(projected_grad, attended_all, *out_parts[1:], *decoded_parts[1:])
     normed_one_grad = collect(
         split_rows(
             jnp.einsum(
-                "pcf,kpf->ck", projected_grad, weight_qkv, preferred_element_type=jnp.float32
+                "pcf,pfk->ck", projected_grad, weight_qkv, preferred_element_type=jnp.float32
             ),
             slides,
         )
     )
+    last_local = row_products(
+        [
+            (normed_one_all, jnp.concatenate(list(projected_grad), axis=1)),
+            (attended_all, jnp.concatenate(out_parts, axis=0)),
+        ]
+    )
+    normed_one_grad = after(normed_one_grad, last_local, *decode_shares[1:])
+    last_grad = scatter_blk(after(last_local, middle_grad))
     h_zero_part, gain_one_grad, shift_one_grad = norm_one_back(normed_one_grad)
     h_zero_low = (h_one_grad + h_zero_part).astype(jnp.bfloat16)
     h_zero_parts = share(h_zero_low, slides)
-    expr_grad_parts = swap(
-        [
-            jnp.dot(part, embedding, preferred_element_type=jnp.float32).astype(jnp.bfloat16)
-            for part in h_zero_parts
-        ]
-    )
-    expr_grad = in_order(expr_grad_parts, me, 1)[:, :genes].astype(jnp.float32)
-
-    latent_all = jnp.concatenate(share(latent.astype(jnp.bfloat16), slides), axis=0)
-    decoded_rows = jnp.dot(latent_all, weight_decode, preferred_element_type=jnp.float32)
-    decoded = in_order(swap(split_rows(decoded_rows.astype(jnp.bfloat16), slides)), me, 1)
-    decoded = decoded[:, :genes]
-
-    def whole(piece, axis):
-        return in_order(share(piece, slides), me, axis)
-
-    cot_stack = jnp.concatenate(cot_parts, axis=0)
-    decode_grad = whole(scatter_blk(contract_rows(latent_all, cot_stack)), 1)[:, :genes]
-    h_two_all = jnp.concatenate(share(h_two_low, slides), axis=0)
-    latent_part = model_width // slides
-    latent_grad = whole(
-        scatter_blk(contract_rows(h_two_all, column_part(pre_grad_all, latent_part, me))), 1
-    )
-    down_grad = whole(scatter_blk(contract_rows(hidden_low, down_input)), 0)
-    up_grad = scatter_blk(contract_rows(normed_two_all, pre_hidden_grad))
-    up_grad = whole(up_grad.reshape(own_rows, blocks, 1, ff_part), 2)
-    attended_all = jnp.concatenate(share(attended_low, slides), axis=0)
-    out_parts = swap([column_part(out_input, head_part, place_of(k)) for k in range(slides)])
-    attn_out_grad = whole(
-        scatter_blk(contract_rows(attended_all, jnp.concatenate(out_parts, axis=0))), 1
-    )
-    qkv_grad = jnp.einsum(
-        "ck,pcf->kpf", normed_one_all, projected_grad, preferred_element_type=jnp.float32
-    ).reshape(model_width, pairs * 3 * pair)
+
     up_bias_grad = jnp.sum(pre_hidden_grad.astype(jnp.float32), axis=0)
     small_grad = jnp.concatenate(
         [
-            jnp.stack([gain_one_grad, shift_one_grad, gain_two_grad, shift_two_grad], axis=1),
-            centre_grad.reshape(model_width, mean_cols),
-            up_bias_grad.reshape(model_width, -1),
-        ],
-        axis=1,
-    )
-    small_grad = jnp.pad(small_grad, ((0, 0), (0, 128 - small_cols)))
-    first_grad = scatter_blk(jnp.concatenate([qkv_grad, small_grad], axis=1))
-    first_parts = share(first_grad, slides)
+            jnp.stack([gain_one_grad, shift_one_grad, gain_two_grad, shift_two_grad], axis=0),
+            centre_grad.reshape(model_width, mean_cols).T,
+            up_bias_grad.reshape(model_width, -1).T,
+        ],
+        axis=0,
+    )
+    small_grad = jnp.pad(small_grad, ((0, SMALL - small_rows), (0, 0))).astype(jnp.bfloat16)
+    small_grad = jnp.transpose(small_grad.reshape(SMALL, blocks, own_rows), (1, 0, 2))
+    embed_local = embed_products(expr_parts, h_zero_parts, small_grad)
+    gene_rows = cells_to_genes(
+        embedding, [after(part, embed_local) for part in h_zero_parts], quarter
+    )
+    embed_own = scatter_blk(after(embed_local, last_grad))[0]
+    middle_parts = share(after(middle_grad, embed_local), slides)
+    gene_parts = swap(gene_rows)
+    last_parts = share(after(last_grad, embed_local), slides)
+    expr_grad = spread_parts(gene_parts, me, genes)
+    decoded = join_parts(
+        [after(part, *gene_rows[1:]) for part in decoded_parts], me, quarter, genes, jnp.bfloat16
+    ).T
+    middle_parts = [after(part, *gene_rows[1:]) for part in middle_parts]
+    up_end = model_width + blocks * ff_part
+    down_grad = in_order([part[:, :model_width] for part in middle_parts], me, 0)
+    up_grad = in_order(
+        [
+            part[:, model_width:up_end].reshape(own_rows, blocks, 1, ff_part)
+            for part in middle_parts
+        ],
+        me,
+        2,
+    )
+    latent_grad = in_order([part[:, up_end:] for part in middle_parts], me, 1)
+    decode_grad = in_order([after(part, *gene_rows[1:]) for part in decode_shares], me, 1)
+    decode_grad = decode_grad[:, :genes]
     qkv_grad = in_order(
         [
             jnp.transpose(
-                part[:, : pairs * 3 * pair].reshape(own_rows, pairs, 3, 1, pair), (0, 2, 3, 1, 4)
+                part[:, :qkv_width].reshape(own_rows, pairs, 3, 1, pair), (0, 2, 3, 1, 4)
             )
-            for part in first_parts
+            for part in last_parts
         ],
         me,
         2,
     ).reshape(own_rows, 3 * model_width)
-    small_parts = [part[:, pairs * 3 * pair :] for part in first_parts]
+    attn_out_grad = in_order([part[:, qkv_width:] for part in last_parts], me, 1)
+
+    outs = [
+        wide(one)
+        for one in (
+            decode_grad,
+            qkv_grad,
+            attn_out_grad,
+            up_grad.reshape(own_rows, -1),
+            down_grad,
+            latent_grad,
+        )
+    ]
+    embed_shares = share(after(embed_own, expr_grad, *outs), slides)
+    embed_grad = join_parts(embed_shares, me, quarter, genes, jnp.float32).T
+    small_parts = [part[quarter : quarter + small_rows].T for part in embed_shares]
     summed = sum(part.astype(jnp.float32) for part in small_parts)
-    up_bias_out = in_order(
-        [part[:, 4 + mean_cols : small_cols].reshape(-1) for part in small_parts], me, 0
-    )
-    embed_grad = whole(
-        scatter_blk(contract_rows(jnp.concatenate(h_zero_parts, axis=0), jnp.concatenate(expr_parts, axis=0))),
-        1,
-    )[:, :genes]
-
-    def wide(piece):
-        return piece.astype(jnp.float32)
+    up_bias_out = in_order([part[:, 4 + mean_cols :].reshape(-1) for part in small_parts], me, 0)
+
 
     return (
         decoded[None],
         prior[None],
-        expr_grad[None],
-        wide(embed_grad),
-        wide(qkv_grad),
-        wide(attn_out_grad),
-        wide(up_grad.reshape(own_rows, -1)),
+        expr_grad,
+        embed_grad,
+        outs[1],
+        outs[2],
+        outs[3],
         wide(up_bias_out),
-        wide(down_grad),
-        wide(latent_grad),
-        wide(decode_grad),
+        outs[4],
+        outs[5],
+        outs[0],
         summed[:, 4 : 4 + mean_cols].reshape(comp_means.shape),
         summed[:, :4],
     )

time: 781 us -> 703 us (0.900)
  matrix products: 122 us -> 27.1 us
  Pallas kernels: 0 us -> 86.3 us
  waiting for transfers between devices: 378 us -> 307 us
  blocking collectives: 0 us -> 48.4 us
  other arithmetic: 55.1 us -> 22.1 us
  starting transfers between devices: 111 us -> 92.8 us
    pallas_call x0 -> x15, Pallas kernels: none -> 86.3 us  [the longest x1 13.5 us: attend_back(): pl.pallas_call(functools.partial(attend_back_kernel, heads, group // head...]
    all_gather x7 -> x3, waiting for transfers between devices: 80 us -> 0.02 us  [gather_blk(): return lax.all_gather(piece, 'blk', axis=axis, tiled=True)]
    ppermute x78 -> x69, waiting for transfers between devices: 222 us -> 294 us  [swap(): lax.ppermute(pieces[k], 'slide', peers(k, count))]
    dot_general x19 -> x2, matrix products: 70.3 us -> 3.15 us  [the longest x1 2.14 us: split_model(): jnp.einsum('pcf,pfk->ck', projected_grad, weight_qkv, preferred_element_t...]
    all_to_all x4 -> x3, waiting for transfers between devices: 75.8 us -> 13.3 us  [to_heads(): lax.all_to_all(rows.reshape(blocks, cells, rows.shape[-1]), 'blk', 0, 0,...]
    all_to_all x0 -> x1, blocking collectives: none -> 48.4 us  [to_heads(): lax.all_to_all(rows.reshape(blocks, cells, rows.shape[-1]), 'blk', 0, 0,...]
    dot_general x12 -> x4, matrix products: 33.1 us -> 14.4 us  [contract_cols(): lax.dot_general(former, latter, (((1,), (1,)), ((), ())), preferred_eleme...]
    ppermute x78 -> x69, starting transfers between devices: 95.4 us -> 80.7 us  [swap(): lax.ppermute(pieces[k], 'slide', peers(k, count))]
  transfers between devices with their start and end apart: 96 -> 79, of which waited for: 49 -> 48; matrix products, arithmetic and copies ran while one was open for 29% -> 14% of each run, Pallas kernels for 0% -> 12%
where the time goes in v2:
time: 703 us; the launch traced here: 693 us
  waiting for transfers between devices  307 us (44%)
  starting transfers between devices  92.8 us (13%)
  local copies, waits for them, and re-layouts  92.6 us (13%)
  Pallas kernels  86.3 us (12%)
  blocking collectives  48.4 us (7%)
  matrix products  27.1 us (4%)
  other arithmetic  22.1 us (3%)
  between operations  16.5 us (2%)
    ppermute x69, waiting for transfers between devices, swap(): lax.ppermute(pieces[k], 'slide', peers(k, count))  294 us
    ppermute x69, starting transfers between devices, swap(): lax.ppermute(pieces[k], 'slide', peers(k, count))  80.7 us
    unnamed x276, local copies, waits for them, and re-layouts  60.4 us
    all_to_all x1, blocking collectives, to_heads(): lax.all_to_all(rows.reshape(blocks, cells, rows.shape[-1]), 'blk', 0, 0,...  48.4 us
    dot_general x4, matrix products, contract_cols(): lax.dot_general(former, latter, (((1,), (1,)), ((), ())), preferred_eleme...  14.4 us
  transfers between devices with their start and end apart: 79, of which 48 were waited for; matrix products, arithmetic and copies ran while one was open for 14% of the time, Pallas kernels for 12%

profile of v2, /device:TPU:0, one launch (start us, length us, event | category | flops | bytes accessed | tf_op | source)
XLA Modules:
  0.0 692.8 jit_solution(4597695250856562375)
XLA Ops:
  15.7 6.6 expression.1
  35.0 11.0 %collective-permute-done.refs_1_ = bf16[3456,128]{1,0:T(8,128)(2,1)S(1)} collective-permute-done((bf16[3456,128]{1,0:T(8,128)(2,1)}, bf16[3456,128]{1,0:T(8,128)(2,1)S(1)}, u32[]{:S(2)}, u32[]{:S(2)}) %collective-permute-start) | collective-permute-done | bytes 884768 | tf_op jit(solution)/shard_map/ppermute | solution.py:346
  45.9 19.6 %collective-permute-done.1.refs_2_ = bf16[3456,128]{1,0:T(8,128)(2,1)S(1)} collective-permute-done((bf16[3456,128]{1,0:T(8,128)(2,1)}, bf16[3456,128]{1,0:T(8,128)(2,1)S(1)}, u32[]{:S(2)}, u32[]{:S(2)}) %collective-permute-start.1) | collective-permute-done | bytes 884768 | tf_op jit(solution)/shard_map/ppermute | solution.py:346
  88.4 17.9 %collective-permute-done.4.refs_2_.refs_6_ = bf16[3456,128]{1,0:T(8,128)(2,1)} collective-permute-done((bf16[3456,128]{1,0:T(8,128)(2,1)}, bf16[3456,128]{1,0:T(8,128)(2,1)}, u32[]{:S(2)}, u32[]{:S(2)}) %collective-permute-start.4) | collective-permute-done | bytes 884768 | tf_op jit(solution)/shard_map/ppermute | solution.py:346
  107.4 9.0 %embed_cells.1 = (f32[128,1024]{1,0:T(8,128)}, bf16[128,1024]{1,0:T(8,128)(2,1)}, bf16[128,1024]{1,0:T(8,128)(2,1)}, bf16[128,1024]{1,0:T(8,128)(2,1)}) custom-call(bf16[512,3456]{1,0:T(8,128)(2,1)} %copy-done.3, bf16[4240,1024]{1,0:T(8,128)(2,1)} %all-gather.4.cloned.1.call-done.table), custom_call_target="tpu_custom_call" | custom-call | tf_op jit(solution)/shard_map/embed_cells/pallas_call | solution.py:603
  144.4 48.4 %all_to_all.20 = bf16[8,128,384]{2,1,0:T(8,128)(2,1)S(1)} all-to-all(bf16[8,128,384]{2,1,0:T(8,128)(2,1)S(1)} %bitcast.316), channel_id=1, replica_groups=mesh['slide'=4,'blk'=8] {'blk'}, dimensions={0} | all-to-all | bytes 1572864 | tf_op jit(solution)/shard_map/all_to_all | solution.py:1088
  192.8 8.2 %attend.1 = bf16[1024,128]{1,0:T(8,128)(2,1)} custom-call(bf16[1024,384]{1,0:T(8,128)(2,1)S(1)} %bitcast.300), custom_call_target="tpu_custom_call" | custom-call | tf_op jit(solution)/shard_map/attend/pallas_call | solution.py:894
  207.2 7.7 %all-to-all-done.1 = bf16[8,128,128]{2,1,0:T(8,128)(2,1)S(1)} async-done(((bf16[8,128,128]{2,1,0:T(8,128)(2,1)}), bf16[8,128,128]{2,1,0:T(8,128)(2,1)S(1)}, u32[]{:S(2)}, u32[]{:S(2)}) %all-to-all-start.1) | async-done | bytes 262176 | tf_op jit(solution)/shard_map/all_to_all | solution.py:1088
  230.3 5.8 collective-permute-done.17
  305.6 7.1 %collective-permute-done.28 = bf16[128,1024]{1,0:T(8,128)(2,1)S(1)} collective-permute-done((bf16[128,1024]{1,0:T(8,128)(2,1)S(1)}, bf16[128,1024]{1,0:T(8,128)(2,1)S(1)}, u32[]{:S(2)}, u32[]{:S(2)}) %collective-permute-start.28) | collective-permute-done | bytes 262176 | tf_op jit(solution)/shard_map/ppermute | solution.py:346
  385.3 13.5 %attend_back.1 = bf16[1024,384]{1,0:T(8,128)(2,1)} custom-call(bf16[1024,384]{1,0:T(8,128)(2,1)S(1)} %bitcast.301, bf16[1024,128]{1,0:T(8,128)(2,1)} %bitcast.50.cot_ref), custom_call_target="tpu_custom_call" | custom-call | tf_op jit(solution)/shard_map/attend_back/pallas_call | solution.py:957
  408.1 37.5 %collective-permute-done.42 = bf16[128,256]{1,0:T(8,128)(2,1)S(1)} collective-permute-done((bf16[128,256]{1,0:T(8,128)(2,1)S(1)}, bf16[128,256]{1,0:T(8,128)(2,1)S(1)}, u32[]{:S(2)}, u32[]{:S(2)}) %collective-permute-start.42) | collective-permute-done | bytes 65568 | tf_op jit(solution)/shard_map/ppermute | solution.py:346
  447.8 6.9 %collective-permute-done.44 = bf16[128,256]{1,0:T(8,128)(2,1)S(1)} collective-permute-done((bf16[128,256]{1,0:T(8,128)(2,1)S(1)}, bf16[128,256]{1,0:T(8,128)(2,1)S(1)}, u32[]{:S(2)}, u32[]{:S(2)}) %collective-permute-start.44) | collective-permute-done | bytes 65568 | tf_op jit(solution)/shard_map/ppermute | solution.py:346
  457.0 9.8 %collective-permute-done.40 = bf16[128,1024]{1,0:T(8,128)(2,1)S(1)} collective-permute-done((bf16[128,1024]{1,0:T(8,128)(2,1)S(1)}, bf16[128,1024]{1,0:T(8,128)(2,1)S(1)}, u32[]{:S(2)}, u32[]{:S(2)}) %collective-permute-start.40) | collective-permute-done | bytes 262176 | tf_op jit(solution)/shard_map/ppermute | solution.py:346
  487.2 5.9 collective-permute-done.50
  493.1 10.8 %collective-permute-done.49 = bf16[128,1024]{1,0:T(8,128)(2,1)S(1)} collective-permute-done((bf16[128,1024]{1,0:T(8,128)(2,1)S(1)}, bf16[128,1024]{1,0:T(8,128)(2,1)S(1)}, u32[]{:S(2)}, u32[]{:S(2)}) %collective-permute-start.49) | collective-permute-done | bytes 262176 | tf_op jit(solution)/shard_map/ppermute | solution.py:346
  504.1 6.9 collective-permute-done.52
  525.7 7.0 %embed_products.1 = bf16[8,3472,128]{2,1,0:T(8,128)(2,1)S(1)} custom-call(bf16[3456,128]{1,0:T(8,128)(2,1)S(1)} %copy-done.10, bf16[3456,128]{1,0:T(8,128)(2,1)S(1)} %copy-done.12, bf16[3456,128]{1,0:T(8,128)(2,1)S(1)} %copy-done.14, bf16[3456,128]{1,0:T(8,128)(2,1)} %collective-permute-done.2.refs_3_, ...), custom_call_target="tpu_custom_call" | custom-call | tf_op jit(solution)/shard_map/embed_products/pallas_call | solution.py:777
  535.7 8.0 %cells_to_genes.1 = (bf16[3456,128]{1,0:T(8,128)(2,1)}, bf16[3456,128]{1,0:T(8,128)(2,1)}, bf16[3456,128]{1,0:T(8,128)(2,1)}, bf16[3456,128]{1,0:T(8,128)(2,1)}) custom-call(bf16[4240,1024]{1,0:T(8,128)(2,1)} %all-gather.4.cloned.1.call-done.table, bf16[128,1024]{1,0:T(8,128)(2,1)} %copy-done.15, bf16[128,1024]{1,0:T(8,128)(2,1)} %collective-permute-done.54.refs_5_.refs_1_, ...), custom_call_target="tpu_custom_call" | custom-call | tf_op jit(solution)/shard_map/cells_to_genes/pallas_call | solution.py:715
  551.0 15.5 %collective-permute-done.57.rest_1_ = bf16[3456,128]{1,0:T(8,128)(2,1)S(1)} collective-permute-done((bf16[3456,128]{1,0:T(8,128)(2,1)}, bf16[3456,128]{1,0:T(8,128)(2,1)S(1)}, u32[]{:S(2)}, u32[]{:S(2)}) %collective-permute-start.57) | collective-permute-done | bytes 884768 | tf_op jit(solution)/shard_map/ppermute | solution.py:346
  569.5 29.6 %collective-permute-done.58.rest_2_ = bf16[3456,128]{1,0:T(8,128)(2,1)S(1)} collective-permute-done((bf16[3456,128]{1,0:T(8,128)(2,1)}, bf16[3456,128]{1,0:T(8,128)(2,1)S(1)}, u32[]{:S(2)}, u32[]{:S(2)}) %collective-permute-start.58) | collective-permute-done | bytes 884768 | tf_op jit(solution)/shard_map/ppermute | solution.py:346
  603.0 7.0 %collective-permute-done.64 = bf16[128,2304]{1,0:T(8,128)(2,1)S(1)} collective-permute-done((bf16[128,2304]{1,0:T(8,128)(2,1)S(1)}, bf16[128,2304]{1,0:T(8,128)(2,1)S(1)}, u32[]{:S(2)}, u32[]{:S(2)}) %collective-permute-start.64) | collective-permute-done | bytes 589856 | tf_op jit(solution)/shard_map/ppermute | solution.py:346
  650.7 8.4 %collective-permute-done.68.rest_3_ = bf16[3472,128]{1,0:T(8,128)(2,1)S(1)} collective-permute-done((bf16[3472,128]{1,0:T(8,128)(2,1)}, bf16[3472,128]{1,0:T(8,128)(2,1)S(1)}, u32[]{:S(2)}, u32[]{:S(2)}) %collective-permute-start.68) | collective-permute-done | bytes 888864 | tf_op jit(solution)/shard_map/ppermute | solution.py:346
  659.0 17.7 %collective-permute-done.67.rest_2_ = bf16[3472,128]{1,0:T(8,128)(2,1)S(1)} collective-permute-done((bf16[3472,128]{1,0:T(8,128)(2,1)}, bf16[3472,128]{1,0:T(8,128)(2,1)S(1)}, u32[]{:S(2)}, u32[]{:S(2)}) %collective-permute-start.67) | collective-permute-done | bytes 888864 | tf_op jit(solution)/shard_map/ppermute | solution.py:346
  (595 shorter events, 350.7 us)
Async XLA Ops:
  7.2 99.2 %all-gather.4.cloned.1.call-start = ((), (), s32[]{:S(2)}) async-start(), calls=%async_computation.8 | async-start | bytes 9768960 | tf_op jit(solution)/shard_map/all_gather | solution.py:378
  12.6 202.3 %all-gather.6.cloned.1.call-start = ((), (), s32[]{:S(2)}) async-start(), calls=%async_computation.9 | async-start | bytes 9437184 | tf_op jit(solution)/shard_map/all_gather | solution.py:378
  25.3 40.3 %collective-permute-start.1 = (bf16[3456,128]{1,0:T(8,128)(2,1)}, bf16[3456,128]{1,0:T(8,128)(2,1)S(1)}, u32[]{:S(2)}, u32[]{:S(2)}) collective-permute-start(bf16[3456,128]{1,0:T(8,128)(2,1)} %get-tuple-element.81), channel_id=1, source_target_pairs={{0,16},{8,24},{16,0},{24,8},{1,17},{9,25},{17,1},{25,9},{2,18},{10... | collective-permute-start | bytes 2654216 | tf_op jit(solution)/shard_map/ppermute | solution.py:346
  26.7 38.8 %collective-permute-start.2 = (bf16[3456,128]{1,0:T(8,128)(2,1)}, bf16[3456,128]{1,0:T(8,128)(2,1)}, u32[]{:S(2)}, u32[]{:S(2)}) collective-permute-start(bf16[3456,128]{1,0:T(8,128)(2,1)} %get-tuple-element.82), channel_id=1, source_target_pairs={{0,24},{8,16},{16,8},{24,0},{1,25},{9,17},{17,9},{25,1},{2,26},{10... | collective-permute-start | bytes 2654216 | tf_op jit(solution)/shard_map/ppermute | solution.py:346
  66.8 39.5 %collective-permute-start.4 = (bf16[3456,128]{1,0:T(8,128)(2,1)}, bf16[3456,128]{1,0:T(8,128)(2,1)}, u32[]{:S(2)}, u32[]{:S(2)}) collective-permute-start(bf16[3456,128]{1,0:T(8,128)(2,1)} %get-tuple-element.84), channel_id=1, source_target_pairs={{0,16},{8,24},{16,0},{24,8},{1,17},{9,25},{17,1},{25,9},{2,18},{10... | collective-permute-start | bytes 2654216 | tf_op jit(solution)/shard_map/ppermute | solution.py:346
  67.6 38.8 %collective-permute-start.5 = (bf16[3456,128]{1,0:T(8,128)(2,1)}, bf16[3456,128]{1,0:T(8,128)(2,1)}, u32[]{:S(2)}, u32[]{:S(2)}) collective-permute-start(bf16[3456,128]{1,0:T(8,128)(2,1)} %get-tuple-element.85), channel_id=1, source_target_pairs={{0,24},{8,16},{16,8},{24,0},{1,25},{9,17},{17,9},{25,1},{2,26},{10... | collective-permute-start | bytes 2654216 | tf_op jit(solution)/shard_map/ppermute | solution.py:346
  205.3 76.2 %all-gather.8.cloned.1.call-start = ((), (), s32[]{:S(2)}) async-start(), calls=%async_computation.10 | async-start | bytes 3981312 | tf_op jit(solution)/shard_map/all_gather | solution.py:378
  215.0 115.3 %reduce-scatter.5.cloned.1.call-start = ((), (), s32[]{:S(2)}) async-start(), calls=%async_computation.11 | async-start | bytes 3981312 | tf_op jit(solution)/shard_map/reduce_scatter | solution.py:382
  277.5 196.1 %reduce-scatter.7.cloned.1.call-start = ((), (), s32[]{:S(2)}) async-start(), calls=%async_computation.12 | async-start | bytes 5308416 | tf_op jit(solution)/shard_map/reduce_scatter | solution.py:382
  398.8 70.9 %all-to-all-start.3 = ((bf16[8,128,384]{2,1,0:T(8,128)(2,1)}), bf16[8,128,384]{2,1,0:T(8,128)(2,1)}, u32[]{:S(2)}, u32[]{:S(2)}) async-start(bf16[8,128,384]{2,1,0:T(8,128)(2,1)} %bitcast.51), calls=%async_computation.3 | async-start | bytes 1572864 | tf_op jit(solution)/shard_map/all_to_all | solution.py:1088
  403.0 132.6 %reduce-scatter.9.cloned.1.call-start = ((), (), s32[]{:S(2)}) async-start(), calls=%async_computation.13 | async-start | bytes 2359296 | tf_op jit(solution)/shard_map/reduce_scatter | solution.py:382
  403.1 63.7 %collective-permute-start.45 = (bf16[3456,128]{1,0:T(8,128)(2,1)}, bf16[3456,128]{1,0:T(8,128)(2,1)S(1)}, u32[]{:S(2)}, u32[]{:S(2)}) collective-permute-start(bf16[3456,128]{1,0:T(8,128)(2,1)} %get-tuple-element.107), channel_id=1, source_target_pairs={{0,8},{8,0},{16,24},{24,16},{1,9},{9,1},{17,25},{25,17},{2,10},{10... | collective-permute-start | bytes 2654216 | tf_op jit(solution)/shard_map/ppermute | solution.py:346
  403.5 64.3 %collective-permute-start.46 = (bf16[3456,128]{1,0:T(8,128)(2,1)}, bf16[3456,128]{1,0:T(8,128)(2,1)S(1)}, u32[]{:S(2)}, u32[]{:S(2)}) collective-permute-start(bf16[3456,128]{1,0:T(8,128)(2,1)} %get-tuple-element.108), channel_id=1, source_target_pairs={{0,16},{8,24},{16,0},{24,8},{1,17},{9,25},{17,1},{25,9},{2,18},{10... | collective-permute-start | bytes 2654216 | tf_op jit(solution)/shard_map/ppermute | solution.py:346
  404.4 64.2 %collective-permute-start.47 = (bf16[3456,128]{1,0:T(8,128)(2,1)S(1)}, bf16[3456,128]{1,0:T(8,128)(2,1)S(1)}, u32[]{:S(2)}, u32[]{:S(2)}) collective-permute-start(bf16[3456,128]{1,0:T(8,128)(2,1)S(1)} %copy-done.38), channel_id=1, source_target_pairs={{0,24},{8,16},{16,8},{24,0},{1,25},{9,17},{17,9},{25,1},{2,26},{10... | collective-permute-start | bytes 2654216 | tf_op jit(solution)/shard_map/ppermute | solution.py:346
  406.7 38.9 %collective-permute-start.42 = (bf16[128,256]{1,0:T(8,128)(2,1)S(1)}, bf16[128,256]{1,0:T(8,128)(2,1)S(1)}, u32[]{:S(2)}, u32[]{:S(2)}) collective-permute-start(bf16[128,256]{1,0:T(8,128)(2,1)S(1)} %get-tuple-element.112), channel_id=1, source_target_pairs={{0,8},{8,0},{16,24},{24,16},{1,9},{9,1},{17,25},{25,17},{2,10},{10... | collective-permute-start | bytes 196616 | tf_op jit(solution)/shard_map/ppermute | solution.py:346
  407.1 38.8 %collective-permute-start.43 = (bf16[128,256]{1,0:T(8,128)(2,1)S(1)}, bf16[128,256]{1,0:T(8,128)(2,1)S(1)}, u32[]{:S(2)}, u32[]{:S(2)}) collective-permute-start(bf16[128,256]{1,0:T(8,128)(2,1)S(1)} %get-tuple-element.113), channel_id=1, source_target_pairs={{0,16},{8,24},{16,0},{24,8},{1,17},{9,25},{17,1},{25,9},{2,18},{10... | collective-permute-start | bytes 196616 | tf_op jit(solution)/shard_map/ppermute | solution.py:346
  473.6 161.7 %reduce-scatter.11.cloned.1.call-start = ((), (), s32[]{:S(2)}) async-start(), calls=%async_computation.14 | async-start | bytes 7999488 | tf_op jit(solution)/shard_map/reduce_scatter | solution.py:382
  544.7 54.4 %collective-permute-start.58 = (bf16[3456,128]{1,0:T(8,128)(2,1)}, bf16[3456,128]{1,0:T(8,128)(2,1)S(1)}, u32[]{:S(2)}, u32[]{:S(2)}) collective-permute-start(bf16[3456,128]{1,0:T(8,128)(2,1)} %get-tuple-element.124), channel_id=1, source_target_pairs={{0,16},{8,24},{16,0},{24,8},{1,17},{9,25},{17,1},{25,9},{2,18},{10... | collective-permute-start | bytes 2654216 | tf_op jit(solution)/shard_map/ppermute | solution.py:346
  545.4 53.8 %collective-permute-start.59 = (bf16[3456,128]{1,0:T(8,128)(2,1)}, bf16[3456,128]{1,0:T(8,128)(2,1)S(1)}, u32[]{:S(2)}, u32[]{:S(2)}) collective-permute-start(bf16[3456,128]{1,0:T(8,128)(2,1)} %get-tuple-element.125), channel_id=1, source_target_pairs={{0,24},{8,16},{16,8},{24,0},{1,25},{9,17},{17,9},{25,1},{2,26},{10... | collective-permute-start | bytes 2654216 | tf_op jit(solution)/shard_map/ppermute | solution.py:346
  548.5 54.5 %collective-permute-start.65 = (bf16[128,2304]{1,0:T(8,128)(2,1)S(1)}, bf16[128,2304]{1,0:T(8,128)(2,1)S(1)}, u32[]{:S(2)}, u32[]{:S(2)}) collective-permute-start(bf16[128,2304]{1,0:T(8,128)(2,1)S(1)} %copy-done.57), channel_id=1, source_target_pairs={{0,24},{8,16},{16,8},{24,0},{1,25},{9,17},{17,9},{25,1},{2,26},{10... | collective-permute-start | bytes 1769480 | tf_op jit(solution)/shard_map/ppermute | solution.py:346
  549.6 60.3 %collective-permute-start.64 = (bf16[128,2304]{1,0:T(8,128)(2,1)S(1)}, bf16[128,2304]{1,0:T(8,128)(2,1)S(1)}, u32[]{:S(2)}, u32[]{:S(2)}) collective-permute-start(bf16[128,2304]{1,0:T(8,128)(2,1)S(1)} %copy-done.57), channel_id=1, source_target_pairs={{0,16},{8,24},{16,0},{24,8},{1,17},{9,25},{17,1},{25,9},{2,18},{10... | collective-permute-start | bytes 1769480 | tf_op jit(solution)/shard_map/ppermute | solution.py:346
  566.5 43.7 %collective-permute-start.63 = (bf16[128,2304]{1,0:T(8,128)(2,1)S(1)}, bf16[128,2304]{1,0:T(8,128)(2,1)S(1)}, u32[]{:S(2)}, u32[]{:S(2)}) collective-permute-start(bf16[128,2304]{1,0:T(8,128)(2,1)S(1)} %copy-done.57), channel_id=1, source_target_pairs={{0,8},{8,0},{16,24},{24,16},{1,9},{9,1},{17,25},{25,17},{2,10},{10... | collective-permute-start | bytes 1769480 | tf_op jit(solution)/shard_map/ppermute | solution.py:346
  637.0 39.7 %collective-permute-start.67 = (bf16[3472,128]{1,0:T(8,128)(2,1)}, bf16[3472,128]{1,0:T(8,128)(2,1)S(1)}, u32[]{:S(2)}, u32[]{:S(2)}) collective-permute-start(bf16[3472,128]{1,0:T(8,128)(2,1)} %bitcast.304), channel_id=1, source_target_pairs={{0,16},{8,24},{16,0},{24,8},{1,17},{9,25},{17,1},{25,9},{2,18},{10... | collective-permute-start | bytes 2666504 | tf_op jit(solution)/shard_map/ppermute | solution.py:346
  638.3 39.0 %collective-permute-start.66 = (bf16[3472,128]{1,0:T(8,128)(2,1)}, bf16[3472,128]{1,0:T(8,128)(2,1)}, u32[]{:S(2)}, u32[]{:S(2)}) collective-permute-start(bf16[3472,128]{1,0:T(8,128)(2,1)} %bitcast.305), channel_id=1, source_target_pairs={{0,8},{8,0},{16,24},{24,16},{1,9},{9,1},{17,25},{25,17},{2,10},{10... | collective-permute-start | bytes 2666504 | tf_op jit(solution)/shard_map/ppermute | solution.py:346
  (172 other events, 2006.6 us)
Sparse Core Ops, SparseCore 0:
  12.8 87.5 all-gather.3
  106.5 98.7 all-gather.5
  215.1 40.1 all-gather.7
  277.6 42.1 reduce-scatter.4
  330.5 57.6 reduce-scatter.6
  473.7 35.5 reduce-scatter.8
  535.8 77.4 reduce-scatter.10

commit v3 on v2

--- a/solution.py
+++ b/solution.py
@@ -366,8 +366,12 @@
     )
 
 
+def lowered(partials):
+    return [partials[0]] + [piece.astype(jnp.bfloat16) for piece in partials[1:]]
+
+
 def collect(partials):
-    arrived = swap([partials[0]] + [piece.astype(jnp.bfloat16) for piece in partials[1:]])
+    arrived = swap(partials)
     total = arrived[0]
     for piece in arrived[1:]:
         total = total + piece.astype(jnp.float32)
@@ -577,6 +581,66 @@
     )(*parts)
 
 
+def finish_kernel(count, quarter, mean_cols, folds, me_ref, *refs):
+    pieces = refs[:count]
+    out, norm, means, bias, held, sems = refs[count:]
+    slot = pl.program_id(0)
+
+    def arrive(k):
+        place = jnp.bitwise_xor(me_ref[0], k)
+        return pltpu.make_async_copy(pieces[k], held.at[place], sems.at[k])
+
+    @pl.when(slot == 0)
+    def _():
+        for k in range(count):
+            arrive(k).start()
+        for k in range(count):
+            arrive(k).wait()
+        small = [held[q, quarter:, :].astype(jnp.float32) for q in range(count)]
+        total = sum(small[1:], small[0])
+        norm[...] = total[:4, :]
+        width = means.shape[1]
+        for k in range(folds):
+            means[k * mean_cols : (k + 1) * mean_cols, :] = total[
+                4 : 4 + mean_cols, k * width : (k + 1) * width
+            ]
+        bias[...] = jnp.concatenate(
+            [one[4 + mean_cols : 5 + mean_cols, :] for one in small], axis=0
+        )
+
+    out[...] = held[slot, :quarter, :].astype(out.dtype)
+
+
+def finish(pieces, me, quarter, genes, mean_cols, folds):
+    count = len(pieces)
+    height, cells = pieces[0].shape
+    return pl.pallas_call(
+        functools.partial(finish_kernel, count, quarter, mean_cols, folds),
+        grid=(count,),
+        out_shape=[
+            jax.ShapeDtypeStruct((genes, cells), jnp.float32),
+            jax.ShapeDtypeStruct((4, cells), jnp.float32),
+            jax.ShapeDtypeStruct((folds * mean_cols, cells // folds), jnp.float32),
+            jax.ShapeDtypeStruct((count, cells), jnp.float32),
+        ],
+        in_specs=[pl.BlockSpec(memory_space=pltpu.SMEM)]
+        + [pl.BlockSpec(memory_space=pl.ANY)] * count,
+        out_specs=[
+            pl.BlockSpec((quarter, cells), lambda slot: (slot, 0)),
+            pl.BlockSpec((4, cells), lambda slot: (0, 0)),
+            pl.BlockSpec((folds * mean_cols, cells // folds), lambda slot: (0, 0)),
+            pl.BlockSpec((count, cells), lambda slot: (0, 0)),
+        ],
+        scratch_shapes=[
+            pltpu.VMEM((count, height, cells), jnp.bfloat16),
+            pltpu.SemaphoreType.DMA((count,)),
+        ],
+        compiler_params=pltpu.CompilerParams(vmem_limit_bytes=40 * 2**20),
+        cost_estimate=COST,
+        name="finish",
+    )(me.reshape(1), *pieces)
+
+
 def scores_kernel(rows, table, *refs):
     outs, total = refs[:-1], refs[-1]
     step = pl.program_id(0)
@@ -666,6 +730,76 @@
     )(table, *cots)
 
 
+def gelu_slope(rows):
+    scale = math.sqrt(2.0 / math.pi)
+    squares = rows * rows
+    bent = jnp.tanh(scale * (rows + 0.044715 * (squares * rows)))
+    inner = scale * (1.0 + (3.0 * 0.044715) * squares)
+    return 0.5 * (1.0 + bent) + 0.5 * rows * (1.0 - bent * bent) * inner
+
+
+def feed_back_kernel(count, latent, down, up, pre, *refs):
+    parts = refs[:count]
+    own, down_input, pre_grad, bias, *outs = refs[count:]
+    cells = own.shape[0]
+    width = own.shape[1]
+    h_grad = jnp.dot(
+        jnp.concatenate([part[:, : latent.shape[0]] for part in parts], axis=0),
+        latent[...],
+        preferred_element_type=jnp.float32,
+    )
+    own[...] = h_grad[:cells, :]
+    down_input[...] = h_grad.astype(jnp.bfloat16)
+    step = 256
+    for start in range(0, pre.shape[1], step):
+        columns = slice(start, start + step)
+        hidden_grad = lax.dot_general(
+            down_input[...],
+            down[columns, :],
+            (((1,), (1,)), ((), ())),
+            preferred_element_type=jnp.float32,
+        )
+        low = (hidden_grad * gelu_slope(pre[:, columns])).astype(jnp.bfloat16)
+        pre_grad[:, columns] = low
+        bias[:, columns] = jnp.sum(low.astype(jnp.float32), axis=0, keepdims=True)
+    product = lax.dot_general(
+        pre_grad[...], up[...], (((1,), (1,)), ((), ())), preferred_element_type=jnp.float32
+    )
+    for k in range(count):
+        outs[k][...] = product[k * cells : (k + 1) * cells, :].astype(outs[k].dtype)
+
+
+def feed_back(parts, latent, down, up, pre):
+    count = len(parts)
+    cells = parts[0].shape[0]
+    width = latent.shape[1]
+    units = pre.shape[1]
+
+    def whole(array):
+        return pl.BlockSpec(array.shape, lambda step: (0,) * len(array.shape))
+
+    shapes = [
+        jax.ShapeDtypeStruct((cells, width), jnp.float32),
+        jax.ShapeDtypeStruct((count * cells, width), jnp.bfloat16),
+        jax.ShapeDtypeStruct((count * cells, units), jnp.bfloat16),
+        jax.ShapeDtypeStruct((1, units), jnp.float32),
+    ] + [
+        jax.ShapeDtypeStruct((cells, width), jnp.float32 if k == 0 else jnp.bfloat16)
+        for k in range(count)
+    ]
+    operands = [latent, down, up, pre, *parts]
+    return pl.pallas_call(
+        functools.partial(feed_back_kernel, count),
+        grid=(1,),
+        out_shape=shapes,
+        in_specs=[whole(one) for one in operands],
+        out_specs=[whole(one) for one in shapes],
+        compiler_params=pltpu.CompilerParams(vmem_limit_bytes=56 * 2**20),
+        cost_estimate=COST,
+        name="feed_back",
+    )(*operands)
+
+
 def decode_kernel(count, table, *refs):
     rows, outs = refs[:count], refs[count:]
     cells = rows[0].shape[0]
@@ -680,19 +814,167 @@
 
 def decode_genes(latents, table):
     count = len(latents)
-    width, quarter = table.shape
-    cells = latents[0].shape[0]
+    cells, width = latents[0].shape
+    quarter = table.shape[1]
     return pl.pallas_call(
         functools.partial(decode_kernel, count),
-        grid=(quarter // WIDE,),
+        grid=(1,),
         out_shape=[jax.ShapeDtypeStruct((quarter, cells), jnp.bfloat16)] * count,
-        in_specs=[pl.BlockSpec((width, WIDE), lambda step: (0, step))]
+        in_specs=[pl.BlockSpec((width, quarter), lambda step: (0, 0))]
         + [pl.BlockSpec((cells, width), lambda step: (0, 0))] * count,
-        out_specs=[pl.BlockSpec((WIDE, cells), lambda step: (step, 0))] * count,
+        out_specs=[pl.BlockSpec((quarter, cells), lambda step: (0, 0))] * count,
         compiler_params=pltpu.CompilerParams(vmem_limit_bytes=40 * 2**20),
         cost_estimate=COST,
         name="decode_genes",
     )(table, *latents)
+
+
+def last_kernel(count, first, me_ref, normed, projected, both, *refs):
+    pre_grads, cots, out = refs[:count], refs[count : 2 * count], refs[-1]
+    cells = cots[0].shape[0]
+
+    width = normed.shape[1]
+
+    def by_offset(first):
+        return jnp.concatenate(
+            [
+                both[
+                    pl.ds(pl.multiple_of(jnp.bitwise_xor(me_ref[0], k) * cells, cells), cells),
+                    first : first + width,
+                ]
+                for k in range(count)
+            ],
+            axis=0,
+        )
+
+    spot = 0
+    for rows, columns in (
+        (normed[...], [projected[k] for k in range(projected.shape[0])]),
+        (by_offset(0), [jnp.concatenate([one[:, first:] for one in cots], axis=0)]),
+        (by_offset(width), [jnp.concatenate([one[...] for one in pre_grads], axis=0)]),
+    ):
+        turned = jnp.transpose(rows)
+        for one in columns:
+            size = one.shape[1]
+            out[:, spot : spot + size] = jnp.dot(
+                turned, one, preferred_element_type=jnp.float32
+            ).astype(out.dtype)
+            spot += size
+
+
+def last_products(normed, projected, pre_grads, both, cots, first, me):
+    count = len(cots)
+    height = normed.shape[1]
+    width = projected.shape[0] * projected.shape[2] + 2 * pre_grads[0].shape[1]
+    return pl.pallas_call(
+        functools.partial(last_kernel, count, first),
+        out_shape=jax.ShapeDtypeStruct((height, width), jnp.bfloat16),
+        in_specs=[pl.BlockSpec(memory_space=pltpu.SMEM)]
+        + [pl.BlockSpec(memory_space=pltpu.VMEM)] * (3 + 2 * count),
+        out_specs=pl.BlockSpec(memory_space=pltpu.VMEM),
+        compiler_params=pltpu.CompilerParams(vmem_limit_bytes=40 * 2**20),
+        cost_estimate=COST,
+        name="last_products",
+    )(me.reshape(1), normed, projected, both, *pre_grads, *cots)
+
+
+def pair_kernel(count, *refs):
+    parts, out = refs[:count], refs[-1]
+    width = out.shape[2]
+    for j in range(out.shape[0] // count):
+        for k in range(count):
+            out[j * count + k] = parts[k][:, j * width : (j + 1) * width]
+
+
+def pair_up(parts, pairs):
+    count = len(parts)
+    cells, width = parts[0].shape
+    return pl.pallas_call(
+        functools.partial(pair_kernel, count),
+        out_shape=jax.ShapeDtypeStruct((pairs * count, cells, width // pairs), parts[0].dtype),
+        in_specs=[pl.BlockSpec(memory_space=pltpu.VMEM)] * count,
+        out_specs=pl.BlockSpec(memory_space=pltpu.VMEM),
+        cost_estimate=COST,
+        name="pair_up",
+    )(*parts)
+
+
+def assemble_kernel(count, sizes, me_ref, *refs):
+    parts, decoder = refs[:count], refs[count : 2 * count]
+    down, up, qkv, attn, latent, decode, held, halves, sems = refs[2 * count :]
+    blocks, pairs, pair, quarter, half = sizes
+
+    def arrive(k):
+        place = jnp.bitwise_xor(me_ref[0], k)
+        return (
+            pltpu.make_async_copy(parts[k], held.at[place], sems.at[0, k]),
+            pltpu.make_async_copy(decoder[k], halves.at[place], sems.at[1, k]),
+        )
+
+    for k in range(count):
+        for one in arrive(k):
+            one.start()
+    for k in range(count):
+        for one in arrive(k):
+            one.wait()
+    rows, width = attn.shape
+    part = width // count
+    ff = up.shape[1] // (count * blocks)
+    latents, genes = decode.shape
+
+    def piece(q, spot, size):
+        return held[q, :, spot : spot + size].astype(jnp.float32)
+
+    for q in range(count):
+        down[q * rows : (q + 1) * rows, :] = piece(q, 0, width)
+        spot = width
+        for b in range(blocks):
+            up[:, (b * count + q) * ff : (b * count + q + 1) * ff] = piece(q, spot, ff)
+            spot += ff
+        for j in range(pairs):
+            for t in range(3):
+                first = t * width + q * part + j * pair
+                qkv[:, first : first + pair] = piece(q, spot, pair)
+                spot += pair
+        for out in (attn, latent):
+            out[:, q * part : (q + 1) * part] = piece(q, spot, part)
+            spot += part
+        for side in range(2):
+            first = q * quarter + side * half
+            size = min(half, quarter - side * half, genes - first)
+            if size > 0:
+                decode[:, first : first + size] = halves[
+                    q, side * latents : (side + 1) * latents, :size
+                ].astype(jnp.float32)
+
+
+def assemble(parts, decoder, me, genes, quarter, half, latents, blocks, pairs, pair):
+    count = len(parts)
+    rows = parts[0].shape[0]
+    width = blocks * rows
+    shapes = [
+        (count * rows, width),
+        (rows, count * width),
+        (rows, 3 * width),
+        (rows, width),
+        (rows, width),
+        (latents, genes),
+    ]
+    return pl.pallas_call(
+        functools.partial(assemble_kernel, count, (blocks, pairs, pair, quarter, half)),
+        out_shape=[jax.ShapeDtypeStruct(shape, jnp.float32) for shape in shapes],
+        in_specs=[pl.BlockSpec(memory_space=pltpu.SMEM)]
+        + [pl.BlockSpec(memory_space=pl.ANY)] * (2 * count),
+        out_specs=[pl.BlockSpec(memory_space=pltpu.VMEM)] * len(shapes),
+        scratch_shapes=[
+            pltpu.VMEM((count,) + parts[0].shape, jnp.bfloat16),
+            pltpu.VMEM((count,) + decoder[0].shape, jnp.bfloat16),
+            pltpu.SemaphoreType.DMA((2, count)),
+        ],
+        compiler_params=pltpu.CompilerParams(vmem_limit_bytes=48 * 2**20),
+        cost_estimate=COST,
+        name="assemble",
+    )(me.reshape(1), *parts, *decoder)
 
 
 def genes_kernel(count, table, *refs):
@@ -784,7 +1066,7 @@
             pltpu.VMEM((2, blocks, ROWS, block), jnp.bfloat16),
             pltpu.SemaphoreType.DMA((3,)),
         ],
-        compiler_params=pltpu.CompilerParams(vmem_limit_bytes=40 * 2**20),
+        compiler_params=pltpu.CompilerParams(vmem_limit_bytes=58 * 2**20),
         cost_estimate=COST,
         name="embed_products",
     )(*parts, *rows, small)
@@ -1026,10 +1308,18 @@
     )
     bias_part = lax.dynamic_slice_in_dim(up_bias, me * ff_part, ff_part, 0)
     mean_cols = comp_means.size // own_rows
+    folds = mixture_count // mean_cols
+    own_latents = w_decode.shape[0]
     small = jnp.concatenate(
-        [norm_params, comp_means.reshape(own_rows, mean_cols), bias_part.reshape(own_rows, -1)],
-        axis=1,
-    ).T
+        [
+            norm_params.T,
+            jnp.concatenate(
+                [comp_means.T[k * mean_cols : (k + 1) * mean_cols] for k in range(folds)], axis=1
+            ),
+            bias_part.reshape(-1, own_rows),
+        ],
+        axis=0,
+    )
     small_rows = small.shape[0]
     small = jnp.pad(small, ((0, SMALL - small_rows), (0, 0)))
     qkv_width = pairs * 3 * pair
@@ -1040,12 +1330,24 @@
     qkv_part = jnp.concatenate(
         [part[:, j * pair : (j + 1) * pair] for j in range(pairs) for part in qkv_part], axis=1
     ).T
-    embedding = gather_blk(jnp.concatenate([embed_part, small, qkv_part], axis=0), 1)
+    out_latent = jnp.concatenate(
+        [
+            lax.dynamic_slice_in_dim(weight, me * head_part, head_part, 1)
+            for weight in (w_attn_out, w_latent)
+        ],
+        axis=1,
+    ).T
+    embedding = gather_blk(
+        jnp.concatenate([embed_part, small, qkv_part, out_latent], axis=0), 1
+    )
     small_all = embedding[quarter : quarter + SMALL]
-    weight_qkv = embedding[quarter + SMALL :].reshape(pairs, 3 * pair, model_width)
+    qkv_end = quarter + SMALL + qkv_width
+    weight_qkv = embedding[quarter + SMALL : qkv_end].reshape(pairs, 3 * pair, model_width)
+    out_latent = embedding[qkv_end:]
     norm_float = small_all[:4].astype(jnp.float32)
-    centres = small_all[4 : 4 + mean_cols].T.reshape(latent_width, mixture_count)
-    bias_up = small_all[4 + mean_cols : small_rows].T.reshape(-1).astype(jnp.float32)
+    centres = small_all[4 : 4 + mean_cols].reshape(mean_cols, blocks, folds, own_latents)
+    centres = jnp.transpose(centres, (1, 3, 2, 0)).reshape(latent_width, mixture_count)
+    bias_up = small_all[4 + mean_cols].astype(jnp.float32)
     expr_parts = swap(expression_parts(counts, library, me, slides, quarter))
 
     cot_all = jnp.pad(decoded_cot[0].T, ((0, padded - genes), (0, 0)))
@@ -1063,17 +1365,30 @@
     )
     down_part = lax.dynamic_slice_in_dim(w_down, me * ff_part, ff_part, 0)
     expr_rows = turn_parts(expr_parts)
+    half = -(-quarter // 256) * 128
+    decode_part = lax.dynamic_slice_in_dim(
+        jnp.pad(w_decode, ((0, 0), (0, padded - genes))), me * quarter, quarter, 1
+    )
+    decode_part = jnp.concatenate(
+        [decode_part[:, :half], jnp.pad(decode_part[:, half:], ((0, 0), (0, 2 * half - quarter)))],
+        axis=0,
+    )
     middle = gather_blk(
         after(
-            jnp.concatenate([w_attn_out, up_part, down_part, w_latent], axis=1),
+            jnp.concatenate([up_part, decode_part], axis=1),
             embedding,
             expr_rows,
             *cot_parts[1:],
         )
     )
-    weight_out, weight_up, weight_down, weight_latent = jnp.split(middle, 4, axis=1)
-    decode_part = lax.dynamic_slice_in_dim(
-        jnp.pad(w_decode, ((0, 0), (0, padded - genes))), me * quarter, quarter, 1
+    weight_up, halves = jnp.split(middle, [model_width], axis=1)
+    halves = halves.reshape(blocks, 2, own_latents, half)
+    weight_decode = jnp.concatenate(
+        [
+            halves[:, 0].reshape(latent_width, half),
+            halves[:, 1].reshape(latent_width, half)[:, : quarter - half],
+        ],
+        axis=1,
     )
 
     h_zero = collect(embed_cells(expr_rows, embedding, slides))
@@ -1089,10 +1404,16 @@
             rows.reshape(blocks, cells, rows.shape[-1]), "blk", 0, 0, tiled=True
         ).reshape(blocks * cells, rows.shape[-1])
 
-    head_rows = to_heads(projected)
+    out_shares = share(after(out_latent[:head_part], normed_one_all), slides)
+    head_rows = after(to_heads(projected), *out_shares[1:])
     per_pair = pair // HEAD_DIM
+    weight_down = gather_blk(after(down_part, middle, head_rows))
+    latent_shares = share(after(out_latent[head_part:], head_rows), slides)
+    weight_out = in_order(out_shares, me, 0)
+    weight_latent = in_order(latent_shares, me, 0)
     own_heads = to_heads(attend(head_rows, per_pair)).reshape(pairs, slides, cells, pair)
-    weight_decode = gather_blk(after(decode_part, middle, own_heads))
+    latent_cots = cots_to_latents(cot_parts, weight_decode)
+    own_heads = after(own_heads, latent_cots[-1], *latent_shares[1:])
     attended_parts = swap(
         [
             jnp.concatenate([own_heads[j, k] for j in range(pairs)], axis=1)
@@ -1100,79 +1421,89 @@
         ]
     )
     attended_low = in_order(attended_parts, me, 1)
-    h_one = h_zero + jnp.dot(attended_low, weight_out, preferred_element_type=jnp.float32)
+    h_one = h_zero + contract_cols(attended_low, weight_out)
     normed_two, norm_two_back = jax.vjp(layer_norm, h_one, norm_float[2], norm_float[3])
     normed_two_low = normed_two.astype(jnp.bfloat16)
     normed_two_all = jnp.concatenate(share(normed_two_low, slides), axis=0)
     hidden_pre = (
         jnp.dot(normed_two_all, weight_up, preferred_element_type=jnp.float32) + bias_up
     )
-    hidden_act, gelu_back = jax.vjp(jax.nn.gelu, hidden_pre)
-    hidden_low = hidden_act.astype(jnp.bfloat16)
-    h_two = h_one + collect(
-        split_rows(jnp.dot(hidden_low, weight_down, preferred_element_type=jnp.float32), slides)
-    )
+    hidden_low = jax.nn.gelu(hidden_pre).astype(jnp.bfloat16)
+    h_two_sum = collect(
+        lowered(
+            split_rows(
+                jnp.dot(hidden_low, weight_down, preferred_element_type=jnp.float32), slides
+            )
+        )
+    )
+    latent_from_decode = collect(latent_cots)
+    h_two = h_one + after(h_two_sum, latent_from_decode)
     h_two_low = h_two.astype(jnp.bfloat16)
-    latent_pre = jnp.dot(h_two_low, weight_latent, preferred_element_type=jnp.float32)
+    both_rows = lax.all_gather(
+        jnp.concatenate([attended_low, h_two_low], axis=1), "slide", axis=0, tiled=True
+    )
+    latent_pre = contract_cols(h_two_low, weight_latent)
     spread = jnp.exp(0.5 * latent_pre[:, latent_width:])
     latent = latent_pre[:, :latent_width] + spread * noise[0]
     prior, prior_back = jax.vjp(mixture_term, latent, centres.astype(jnp.float32))
 
-    latent_from_decode = collect(cots_to_latents(cot_parts, weight_decode))
     latent_from_prior, centre_grad = prior_back(prior_cot[0])
     latent_total = latent_from_decode + latent_from_prior
     pre_grad = jnp.concatenate(
         [latent_total, latent_total * noise[0] * spread * 0.5], axis=-1
     ).astype(jnp.bfloat16)
-    latent_parts = share(latent.astype(jnp.bfloat16), slides)
-    pre_grad_all = jnp.concatenate(share(after(pre_grad, *latent_parts[1:]), slides), axis=0)
+    both_parts = share(
+        jnp.concatenate([pre_grad, latent.astype(jnp.bfloat16)], axis=1), slides
+    )
+    h_two_grad, down_input, pre_hidden_grad, up_bias_grad, *normed_two_parts = feed_back(
+        both_parts, weight_latent, weight_down, weight_up, hidden_pre
+    )
+    normed_two_grad = collect(normed_two_parts)
+    latent_parts = [part[:, model_width:] for part in both_parts]
+    latent_parts = [after(part, normed_two_parts[-1]) for part in latent_parts]
     decode_local = decoder_products(latent_parts, cot_parts)
-    pre_grad_all = after(pre_grad_all, decode_local)
-    decode_own = scatter_blk(decode_local)
-    h_two_grad_all = contract_cols(pre_grad_all, weight_latent)
-    down_input = h_two_grad_all.astype(jnp.bfloat16)
-    hidden_grad = contract_cols(down_input, weight_down)
-    pre_hidden_grad = gelu_back(hidden_grad)[0].astype(jnp.bfloat16)
-    h_two_all = jnp.concatenate(share(after(h_two_low, pre_grad_all), slides), axis=0)
-    normed_two_parts = split_rows(contract_cols(pre_hidden_grad, weight_up), slides)
-    normed_two_grad = collect(normed_two_parts)
+    decoded_rows = decode_genes(latent_parts, weight_decode)
+    normed_two_grad = after(normed_two_grad, decode_local, decoded_rows[-1])
+    decode_own = scatter_blk(after(decode_local, both_rows))
+    h_one_part, gain_two_grad, shift_two_grad = norm_two_back(normed_two_grad)
+    h_one_grad = h_two_grad + h_one_part
+    out_input = h_one_grad.astype(jnp.bfloat16)
+    attended_grad = jnp.dot(out_input, weight_out, preferred_element_type=jnp.float32).astype(jnp.bfloat16)
+    grad_parts = swap([column_part(attended_grad, head_part, place_of(k)) for k in range(slides)])
+    out_heads = to_heads(pair_up(grad_parts, pairs))
+
     middle_local = row_products(
         [
-            (hidden_low, after(down_input, normed_two_parts[-1])),
+            (hidden_low, after(down_input, *grad_parts[1:])),
             (normed_two_all, pre_hidden_grad),
-            (h_two_all, column_part(pre_grad_all, latent_part, me)),
         ]
     )
-    normed_two_grad = after(normed_two_grad, middle_local)
-    middle_grad = scatter_blk(after(middle_local, decode_own))
-    h_one_part, gain_two_grad, shift_two_grad = norm_two_back(normed_two_grad)
-    h_one_grad = h_two_grad_all[:cells] + h_one_part
-    out_input = h_one_grad.astype(jnp.bfloat16)
-    attended_grad = contract_cols(out_input, weight_out).astype(jnp.bfloat16)
-
-    grad_parts = swap([column_part(attended_grad, head_part, place_of(k)) for k in range(slides)])
-    grad_pairs = jnp.stack(
-        [part[:, j * pair : (j + 1) * pair] for j in range(pairs) for part in grad_parts]
-    )
-    out_heads = to_heads(grad_pairs)
-
-    decoded_rows = decode_genes(
-        [after(rows, *grad_parts[1:]) for rows in latent_parts], weight_decode
-    )
-    out_heads = after(out_heads, *decoded_rows)
-    decoded_parts = swap(decoded_rows)
-    attended_all = jnp.concatenate(share(after(attended_low, *grad_parts[1:]), slides), axis=0)
+    out_heads = after(out_heads, middle_local)
+    decoded_parts = swap(
+        [after(one, *grad_parts[1:]) for one in decoded_rows[:-1]]
+        + [after(decoded_rows[-1], out_heads)]
+    )
+    out_heads = after(out_heads, *decoded_parts[1:-1])
     head_grads = attend_back(head_rows, out_heads, per_pair)
-    out_parts = swap(
+    middle_grad = scatter_blk(after(middle_local, decode_own, head_grads))
+    decode_half = jnp.concatenate(
+        [decode_own[:, :half], jnp.pad(decode_own[:, half:], ((0, 0), (0, 2 * half - quarter)))],
+        axis=0,
+    )
+    more_parts = swap(
         [
-            after(column_part(out_input, head_part, place_of(k)), *grad_parts[1:])
+            after(
+                jnp.concatenate(
+                    [decode_half, column_part(out_input, head_part, place_of(k))], axis=1
+                ),
+                head_grads,
+            )
             for k in range(slides)
         ]
     )
-    decode_shares = share(after(decode_own, *grad_parts[1:]), slides)
     projected_grad = to_heads(head_grads).reshape(pairs, slides * cells, 3 * pair)
-    projected_grad = after(projected_grad, attended_all, *out_parts[1:], *decoded_parts[1:])
-    normed_one_grad = collect(
+    projected_grad = after(projected_grad, decoded_parts[-1], *more_parts[1:])
+    normed_one_parts = lowered(
         split_rows(
             jnp.einsum(
                 "pcf,pfk->ck", projected_grad, weight_qkv, preferred_element_type=jnp.float32
@@ -1180,24 +1511,29 @@
             slides,
         )
     )
-    last_local = row_products(
-        [
-            (normed_one_all, jnp.concatenate(list(projected_grad), axis=1)),
-            (attended_all, jnp.concatenate(out_parts, axis=0)),
-        ]
-    )
-    normed_one_grad = after(normed_one_grad, last_local, *decode_shares[1:])
+    normed_one_grad = collect(normed_one_parts)
+    last_local = last_products(
+        normed_one_all,
+        after(projected_grad, normed_one_parts[-1]),
+        [column_part(part, latent_part, me) for part in both_parts],
+        both_rows,
+        more_parts,
+        half,
+        me,
+    )
+    normed_one_grad = after(normed_one_grad, last_local)
     last_grad = scatter_blk(after(last_local, middle_grad))
     h_zero_part, gain_one_grad, shift_one_grad = norm_one_back(normed_one_grad)
     h_zero_low = (h_one_grad + h_zero_part).astype(jnp.bfloat16)
     h_zero_parts = share(h_zero_low, slides)
 
-    up_bias_grad = jnp.sum(pre_hidden_grad.astype(jnp.float32), axis=0)
     small_grad = jnp.concatenate(
         [
             jnp.stack([gain_one_grad, shift_one_grad, gain_two_grad, shift_two_grad], axis=0),
-            centre_grad.reshape(model_width, mean_cols).T,
-            up_bias_grad.reshape(model_width, -1).T,
+            jnp.transpose(
+                centre_grad.reshape(blocks, own_latents, folds, mean_cols), (3, 0, 2, 1)
+            ).reshape(mean_cols, model_width),
+            up_bias_grad,
         ],
         axis=0,
     )
@@ -1208,71 +1544,34 @@
         embedding, [after(part, embed_local) for part in h_zero_parts], quarter
     )
     embed_own = scatter_blk(after(embed_local, last_grad))[0]
-    middle_parts = share(after(middle_grad, embed_local), slides)
     gene_parts = swap(gene_rows)
-    last_parts = share(after(last_grad, embed_local), slides)
+    grad_shares = share(
+        after(jnp.concatenate([middle_grad, last_grad], axis=1), embed_local), slides
+    )
+    embed_shares = share(after(embed_own, *gene_parts[1:], *grad_shares[1:]), slides)
     expr_grad = spread_parts(gene_parts, me, genes)
-    decoded = join_parts(
-        [after(part, *gene_rows[1:]) for part in decoded_parts], me, quarter, genes, jnp.bfloat16
-    ).T
-    middle_parts = [after(part, *gene_rows[1:]) for part in middle_parts]
-    up_end = model_width + blocks * ff_part
-    down_grad = in_order([part[:, :model_width] for part in middle_parts], me, 0)
-    up_grad = in_order(
-        [
-            part[:, model_width:up_end].reshape(own_rows, blocks, 1, ff_part)
-            for part in middle_parts
-        ],
-        me,
-        2,
-    )
-    latent_grad = in_order([part[:, up_end:] for part in middle_parts], me, 1)
-    decode_grad = in_order([after(part, *gene_rows[1:]) for part in decode_shares], me, 1)
-    decode_grad = decode_grad[:, :genes]
-    qkv_grad = in_order(
-        [
-            jnp.transpose(
-                part[:, :qkv_width].reshape(own_rows, pairs, 3, 1, pair), (0, 2, 3, 1, 4)
-            )
-            for part in last_parts
-        ],
-        me,
-        2,
-    ).reshape(own_rows, 3 * model_width)
-    attn_out_grad = in_order([part[:, qkv_width:] for part in last_parts], me, 1)
-
-    outs = [
-        wide(one)
-        for one in (
-            decode_grad,
-            qkv_grad,
-            attn_out_grad,
-            up_grad.reshape(own_rows, -1),
-            down_grad,
-            latent_grad,
-        )
-    ]
-    embed_shares = share(after(embed_own, expr_grad, *outs), slides)
-    embed_grad = join_parts(embed_shares, me, quarter, genes, jnp.float32).T
-    small_parts = [part[quarter : quarter + small_rows].T for part in embed_shares]
-    summed = sum(part.astype(jnp.float32) for part in small_parts)
-    up_bias_out = in_order([part[:, 4 + mean_cols :].reshape(-1) for part in small_parts], me, 0)
-
+    decoded = join_parts(decoded_parts, me, quarter, genes, jnp.bfloat16).T
+    down_grad, up_grad, qkv_grad, attn_out_grad, latent_grad, decode_grad = assemble(
+        grad_shares, more_parts, me, genes, quarter, half, own_latents, blocks, pairs, pair
+    )
+    embed_grad, norm_grad, means_grad, up_bias_grad = finish(
+        embed_shares, me, quarter, genes, mean_cols, folds
+    )
 
     return (
         decoded[None],
         prior[None],
         expr_grad,
-        embed_grad,
-        outs[1],
-        outs[2],
-        outs[3],
-        wide(up_bias_out),
-        outs[4],
-        outs[5],
-        outs[0],
-        summed[:, 4 : 4 + mean_cols].reshape(comp_means.shape),
-        summed[:, :4],
+        embed_grad.T,
+        qkv_grad,
+        attn_out_grad,
+        up_grad,
+        up_bias_grad.reshape(-1),
+        down_grad,
+        latent_grad,
+        decode_grad,
+        means_grad.T,
+        norm_grad.T,
     )
 
 

time: 703 us -> 648 us (0.922)
  blocking collectives: 48.4 us -> 0 us
  local copies, waits for them, and re-layouts: 92.6 us -> 70.3 us
  Pallas kernels: 86.3 us -> 105 us
  matrix products: 27.1 us -> 16.2 us
  waiting for transfers between devices: 307 us -> 316 us
    all_to_all x1 -> x0, blocking collectives: 48.4 us -> none  [to_heads(): lax.all_to_all(rows.reshape(blocks, cells, rows.shape[-1]), 'blk', 0, 0,...]
    unnamed x276 -> x291, local copies, waits for them, and re-layouts: 60.4 us -> 35.1 us
    pallas_call x1 -> x6, Pallas kernels: 3.3 us -> 27.3 us  [the longest x1 9.56 us: feed_back(): pl.pallas_call(functools.partial(feed_back_kernel, count), grid=(1,), out...]
    dot_general x4 -> x2, matrix products: 14.4 us -> 3.37 us  [contract_cols(): lax.dot_general(former, latter, (((1,), (1,)), ((), ())), preferred_eleme...]
    ppermute x69 -> x60, starting transfers between devices: 80.7 us -> 73.1 us  [swap(): lax.ppermute(pieces[k], 'slide', peers(k, count))]
    all_to_all x3 -> x4, starting transfers between devices: 11.7 us -> 16.9 us  [to_heads(): lax.all_to_all(rows.reshape(blocks, cells, rows.shape[-1]), 'blk', 0, 0,...]
    all_to_all x3 -> x4, waiting for transfers between devices: 13.3 us -> 15.8 us  [to_heads(): lax.all_to_all(rows.reshape(blocks, cells, rows.shape[-1]), 'blk', 0, 0,...]
    ppermute x69 -> x60, waiting for transfers between devices: 294 us -> 294 us  [swap(): lax.ppermute(pieces[k], 'slide', peers(k, count))]
  transfers between devices with their start and end apart: 79 -> 72, of which waited for: 48 -> 44; matrix products, arithmetic and copies ran while one was open for 14% -> 11% of each run, Pallas kernels for 12% -> 16%
where the time goes in v3:
time: 648 us; the launch traced here: 637 us
  waiting for transfers between devices  316 us (49%)
  Pallas kernels  105 us (16%)
  starting transfers between devices  91 us (14%)
  local copies, waits for them, and re-layouts  70.3 us (11%)
  other arithmetic  21.9 us (3%)
  between operations  16.3 us (3%)
  matrix products  16.2 us (2%)
    ppermute x60, waiting for transfers between devices, swap(): lax.ppermute(pieces[k], 'slide', peers(k, count))  294 us
    ppermute x60, starting transfers between devices, swap(): lax.ppermute(pieces[k], 'slide', peers(k, count))  73.1 us
    unnamed x291, local copies, waits for them, and re-layouts  35.1 us
    all_to_all x4, starting transfers between devices, to_heads(): lax.all_to_all(rows.reshape(blocks, cells, rows.shape[-1]), 'blk', 0, 0,...  16.9 us
    all_to_all x4, waiting for transfers between devices, to_heads(): lax.all_to_all(rows.reshape(blocks, cells, rows.shape[-1]), 'blk', 0, 0,...  15.8 us
  transfers between devices with their start and end apart: 72, of which 44 were waited for; matrix products, arithmetic and copies ran while one was open for 11% of the time, Pallas kernels for 16%

profile of v3, /device:TPU:0, one launch (start us, length us, event | category | flops | bytes accessed | tf_op | source)
XLA Modules:
  0.0 636.8 jit_solution(6081912956474942839)
XLA Ops:
  38.2 9.5 %collective-permute-done.refs_1_ = bf16[3456,128]{1,0:T(8,128)(2,1)S(1)} collective-permute-done((bf16[3456,128]{1,0:T(8,128)(2,1)}, bf16[3456,128]{1,0:T(8,128)(2,1)S(1)}, u32[]{:S(2)}, u32[]{:S(2)}) %collective-permute-start) | collective-permute-done | bytes 884768 | tf_op jit(solution)/shard_map/ppermute | solution.py:346
  47.7 19.7 %collective-permute-done.1.refs_2_ = bf16[3456,128]{1,0:T(8,128)(2,1)} collective-permute-done((bf16[3456,128]{1,0:T(8,128)(2,1)}, bf16[3456,128]{1,0:T(8,128)(2,1)}, u32[]{:S(2)}, u32[]{:S(2)}) %collective-permute-start.1) | collective-permute-done | bytes 884768 | tf_op jit(solution)/shard_map/ppermute | solution.py:346
  77.1 13.2 %collective-permute-done.3.refs_1_.refs_5_ = bf16[3456,128]{1,0:T(8,128)(2,1)} collective-permute-done((bf16[3456,128]{1,0:T(8,128)(2,1)}, bf16[3456,128]{1,0:T(8,128)(2,1)}, u32[]{:S(2)}, u32[]{:S(2)}) %collective-permute-start.3) | collective-permute-done | bytes 884768 | tf_op jit(solution)/shard_map/ppermute | solution.py:346
  90.3 17.8 %collective-permute-done.4.refs_2_.refs_6_ = bf16[3456,128]{1,0:T(8,128)(2,1)} collective-permute-done((bf16[3456,128]{1,0:T(8,128)(2,1)}, bf16[3456,128]{1,0:T(8,128)(2,1)}, u32[]{:S(2)}, u32[]{:S(2)}) %collective-permute-start.4) | collective-permute-done | bytes 884768 | tf_op jit(solution)/shard_map/ppermute | solution.py:346
  111.9 9.0 %embed_cells.1 = (f32[128,1024]{1,0:T(8,128)}, bf16[128,1024]{1,0:T(8,128)(2,1)}, bf16[128,1024]{1,0:T(8,128)(2,1)}, bf16[128,1024]{1,0:T(8,128)(2,1)}) custom-call(bf16[512,3456]{1,0:T(8,128)(2,1)} %copy-done.2, bf16[4752,1024]{1,0:T(8,128)(2,1)} %all-gather.5.cloned.1.call-done.table), custom_call_target="tpu_custom_call" | custom-call | tf_op jit(solution)/shard_map/embed_cells/pallas_call | solution.py:667
  166.0 11.5 %collective-permute-done.14 = bf16[256,1024]{1,0:T(8,128)(2,1)S(1)} collective-permute-done((bf16[256,1024]{1,0:T(8,128)(2,1)S(1)}, bf16[256,1024]{1,0:T(8,128)(2,1)S(1)}, u32[]{:S(2)}, u32[]{:S(2)}) %collective-permute-start.14) | collective-permute-done | bytes 524320 | tf_op jit(solution)/shard_map/ppermute | solution.py:346
  177.5 10.7 %collective-permute-done.13 = bf16[256,1024]{1,0:T(8,128)(2,1)S(1)} collective-permute-done((bf16[256,1024]{1,0:T(8,128)(2,1)S(1)}, bf16[256,1024]{1,0:T(8,128)(2,1)S(1)}, u32[]{:S(2)}, u32[]{:S(2)}) %collective-permute-start.13) | collective-permute-done | bytes 524320 | tf_op jit(solution)/shard_map/ppermute | solution.py:346
  190.9 8.2 %attend.1 = bf16[1024,128]{1,0:T(8,128)(2,1)} custom-call(bf16[1024,384]{1,0:T(8,128)(2,1)S(1)} %bitcast.165), custom_call_target="tpu_custom_call" | custom-call | tf_op jit(solution)/shard_map/attend/pallas_call | solution.py:1176
  217.2 8.2 %collective-permute-done.16 = bf16[256,1024]{1,0:T(8,128)(2,1)} collective-permute-done((bf16[256,1024]{1,0:T(8,128)(2,1)}, bf16[256,1024]{1,0:T(8,128)(2,1)}, u32[]{:S(2)}, u32[]{:S(2)}) %collective-permute-start.16) | collective-permute-done | bytes 524320 | tf_op jit(solution)/shard_map/ppermute | solution.py:346
  295.1 10.0 %collective-permute-done.32.refs_3_ = bf16[128,1536]{1,0:T(8,128)(2,1)S(1)} collective-permute-done((bf16[128,1536]{1,0:T(8,128)(2,1)S(1)}, bf16[128,1536]{1,0:T(8,128)(2,1)S(1)}, u32[]{:S(2)}, u32[]{:S(2)}) %collective-permute-start.32) | collective-permute-done | bytes 393248 | tf_op jit(solution)/shard_map/ppermute | solution.py:346
  305.1 6.7 %collective-permute-done.31.refs_2_ = bf16[128,1536]{1,0:T(8,128)(2,1)S(1)} collective-permute-done((bf16[128,1536]{1,0:T(8,128)(2,1)S(1)}, bf16[128,1536]{1,0:T(8,128)(2,1)S(1)}, u32[]{:S(2)}, u32[]{:S(2)}) %collective-permute-start.31) | collective-permute-done | bytes 393248 | tf_op jit(solution)/shard_map/ppermute | solution.py:346
  312.7 9.6 %feed_back.1 = (f32[128,1024]{1,0:T(8,128)}, bf16[512,1024]{1,0:T(8,128)(2,1)}, bf16[512,1024]{1,0:T(8,128)(2,1)}, f32[1,1024]{1,0:T(1,128)}, f32[128,1024]{1,0:...) custom-call(bf16[1024,1024]{1,0:T(8,128)(2,1)} %copy-done.43, ...), custom_call_target="tpu_custom_call" | custom-call | tf_op jit(solution)/shard_map/feed_back/pallas_call | solution.py:791
  373.1 6.7 %all-to-all-done.2 = bf16[8,128,128]{2,1,0:T(8,128)(2,1)S(1)} async-done(((bf16[8,128,128]{2,1,0:T(8,128)(2,1)}), bf16[8,128,128]{2,1,0:T(8,128)(2,1)S(1)}, u32[]{:S(2)}, u32[]{:S(2)}) %all-to-all-start.2) | async-done | bytes 262176 | tf_op jit(solution)/shard_map/all_to_all | solution.py:1403
  379.8 12.3 %attend_back.1 = bf16[1024,384]{1,0:T(8,128)(2,1)} custom-call(bf16[1024,384]{1,0:T(8,128)(2,1)S(1)} %bitcast.166, bf16[1024,128]{1,0:T(8,128)(2,1)S(1)} %bitcast.170), custom_call_target="tpu_custom_call" | custom-call | tf_op jit(solution)/shard_map/attend_back/pallas_call | solution.py:1239
  406.2 13.5 %collective-permute-done.41.rest_3_ = bf16[3456,128]{1,0:T(8,128)(2,1)} collective-permute-done((bf16[3456,128]{1,0:T(8,128)(2,1)}, bf16[3456,128]{1,0:T(8,128)(2,1)}, u32[]{:S(2)}, u32[]{:S(2)}) %collective-permute-start.41) | collective-permute-done | bytes 884768 | tf_op jit(solution)/shard_map/ppermute | solution.py:346
  419.7 9.0 %all-to-all-done.3 = bf16[8,128,384]{2,1,0:T(8,128)(2,1)S(1)} async-done(((bf16[8,128,384]{2,1,0:T(8,128)(2,1)}), bf16[8,128,384]{2,1,0:T(8,128)(2,1)S(1)}, u32[]{:S(2)}, u32[]{:S(2)}) %all-to-all-start.3) | async-done | bytes 786464 | tf_op jit(solution)/shard_map/all_to_all | solution.py:1403
  430.9 10.5 %collective-permute-done.44.refs_7_ = bf16[128,2048]{1,0:T(8,128)(2,1)S(1)} collective-permute-done((bf16[128,2048]{1,0:T(8,128)(2,1)}, bf16[128,2048]{1,0:T(8,128)(2,1)S(1)}, u32[]{:S(2)}, u32[]{:S(2)}) %collective-permute-start.44) | collective-permute-done | bytes 524320 | tf_op jit(solution)/shard_map/ppermute | solution.py:346
  457.7 11.3 %collective-permute-done.45 = bf16[128,1024]{1,0:T(8,128)(2,1)S(1)} collective-permute-done((bf16[128,1024]{1,0:T(8,128)(2,1)S(1)}, bf16[128,1024]{1,0:T(8,128)(2,1)S(1)}, u32[]{:S(2)}, u32[]{:S(2)}) %collective-permute-start.45) | collective-permute-done | bytes 262176 | tf_op jit(solution)/shard_map/ppermute | solution.py:346
  487.4 9.3 %embed_products.1 = bf16[8,3472,128]{2,1,0:T(8,128)(2,1)} custom-call(bf16[3456,128]{1,0:T(8,128)(2,1)} %copy-done.10, bf16[3456,128]{1,0:T(8,128)(2,1)} %copy-done.11, bf16[3456,128]{1,0:T(8,128)(2,1)} %collective-permute-done.1.refs_2_, bf16[3456,128]{1,0:T(8,128)(2,1)} %collective-permute-done.2.refs_3_, bf16[128,1024]{1,0:T(8,128)(2,1)} %copy-done.55, ...), custom_call_target="tpu_custom_call" | custom-call | tf_op jit(solution)/shard_map/embed_products/pallas_call | solution.py:1059
  496.8 7.9 %cells_to_genes.1 = (bf16[3456,128]{1,0:T(8,128)(2,1)}, bf16[3456,128]{1,0:T(8,128)(2,1)}, bf16[3456,128]{1,0:T(8,128)(2,1)}, bf16[3456,128]{1,0:T(8,128)(2,1)}) custom-call(bf16[4752,1024]{1,0:T(8,128)(2,1)} %all-gather.5.cloned.1.call-done.table, bf16[128,1024]{1,0:T(8,128)(2,1)} %copy-done.55, bf16[128,1024]{1,0:T(8,128)(2,1)} %copy-done.67, ...), custom_call_target="tpu_custom_call" | custom-call | tf_op jit(solution)/shard_map/cells_to_genes/pallas_call | solution.py:997
  511.0 16.4 %collective-permute-done.51.rest_1_ = bf16[3456,128]{1,0:T(8,128)(2,1)S(1)} collective-permute-done((bf16[3456,128]{1,0:T(8,128)(2,1)}, bf16[3456,128]{1,0:T(8,128)(2,1)S(1)}, u32[]{:S(2)}, u32[]{:S(2)}) %collective-permute-start.51) | collective-permute-done | bytes 884768 | tf_op jit(solution)/shard_map/ppermute | solution.py:346
  528.6 37.3 %collective-permute-done.52.rest_2_ = bf16[3456,128]{1,0:T(8,128)(2,1)S(1)} collective-permute-done((bf16[3456,128]{1,0:T(8,128)(2,1)}, bf16[3456,128]{1,0:T(8,128)(2,1)S(1)}, u32[]{:S(2)}, u32[]{:S(2)}) %collective-permute-start.52) | collective-permute-done | bytes 884768 | tf_op jit(solution)/shard_map/ppermute | solution.py:346
  568.6 14.4 %collective-permute-done.55.refs_2_ = bf16[128,3328]{1,0:T(8,128)(2,1)S(1)} collective-permute-done((bf16[128,3328]{1,0:T(8,128)(2,1)S(1)}, bf16[128,3328]{1,0:T(8,128)(2,1)S(1)}, u32[]{:S(2)}, u32[]{:S(2)}) %collective-permute-start.55) | collective-permute-done | bytes 852000 | tf_op jit(solution)/shard_map/ppermute | solution.py:346
  608.7 17.0 %collective-permute-done.58.refs_2_ = bf16[3472,128]{1,0:T(8,128)(2,1)S(1)} collective-permute-done((bf16[3472,128]{1,0:T(8,128)(2,1)}, bf16[3472,128]{1,0:T(8,128)(2,1)S(1)}, u32[]{:S(2)}, u32[]{:S(2)}) %collective-permute-start.58) | collective-permute-done | bytes 888864 | tf_op jit(solution)/shard_map/ppermute | solution.py:346
  (558 shorter events, 321.0 us)
Async XLA Ops:
  7.2 103.7 %all-gather.5.cloned.1.call-start = ((), (), s32[]{:S(2)}) async-start(), calls=%async_computation.8 | async-start | bytes 10948608 | tf_op jit(solution)/shard_map/all_gather | solution.py:382
  14.4 193.0 %all-gather.7.cloned.1.call-start = ((), (), s32[]{:S(2)}) async-start(), calls=%async_computation.9 | async-start | bytes 6488064 | tf_op jit(solution)/shard_map/all_gather | solution.py:382
  27.0 40.4 %collective-permute-start.1 = (bf16[3456,128]{1,0:T(8,128)(2,1)}, bf16[3456,128]{1,0:T(8,128)(2,1)}, u32[]{:S(2)}, u32[]{:S(2)}) collective-permute-start(bf16[3456,128]{1,0:T(8,128)(2,1)} %get-tuple-element.93), channel_id=1, source_target_pairs={{0,16},{8,24},{16,0},{24,8},{1,17},{9,25},{17,1},{25,9},{2,18},{10... | collective-permute-start | bytes 2654216 | tf_op jit(solution)/shard_map/ppermute | solution.py:346
  28.5 38.9 %collective-permute-start.2 = (bf16[3456,128]{1,0:T(8,128)(2,1)}, bf16[3456,128]{1,0:T(8,128)(2,1)}, u32[]{:S(2)}, u32[]{:S(2)}) collective-permute-start(bf16[3456,128]{1,0:T(8,128)(2,1)} %get-tuple-element.94), channel_id=1, source_target_pairs={{0,24},{8,16},{16,8},{24,0},{1,25},{9,17},{17,9},{25,1},{2,26},{10... | collective-permute-start | bytes 2654216 | tf_op jit(solution)/shard_map/ppermute | solution.py:346
  68.6 39.5 %collective-permute-start.4 = (bf16[3456,128]{1,0:T(8,128)(2,1)}, bf16[3456,128]{1,0:T(8,128)(2,1)}, u32[]{:S(2)}, u32[]{:S(2)}) collective-permute-start(bf16[3456,128]{1,0:T(8,128)(2,1)} %get-tuple-element.96), channel_id=1, source_target_pairs={{0,16},{8,24},{16,0},{24,8},{1,17},{9,25},{17,1},{25,9},{2,18},{10... | collective-permute-start | bytes 2654216 | tf_op jit(solution)/shard_map/ppermute | solution.py:346
  69.5 38.7 %collective-permute-start.5 = (bf16[3456,128]{1,0:T(8,128)(2,1)}, bf16[3456,128]{1,0:T(8,128)(2,1)}, u32[]{:S(2)}, u32[]{:S(2)}) collective-permute-start(bf16[3456,128]{1,0:T(8,128)(2,1)} %get-tuple-element.97), channel_id=1, source_target_pairs={{0,24},{8,16},{16,8},{24,0},{1,25},{9,17},{17,9},{25,1},{2,26},{10... | collective-permute-start | bytes 2654216 | tf_op jit(solution)/shard_map/ppermute | solution.py:346
  154.9 36.0 %all-to-all-start = ((bf16[8,128,384]{2,1,0:T(8,128)(2,1)}), bf16[8,128,384]{2,1,0:T(8,128)(2,1)S(1)}, u32[]{:S(2)}, u32[]{:S(2)}) async-start(bf16[8,128,384]{2,1,0:T(8,128)(2,1)} %bitcast.21), calls=%async_computation | async-start | bytes 1572864 | tf_op jit(solution)/shard_map/all_to_all | solution.py:1403
  207.4 50.6 %all-gather.9.cloned.1.call-start = ((), (), s32[]{:S(2)}) async-start(), calls=%async_computation.10 | async-start | bytes 2359296 | tf_op jit(solution)/shard_map/all_gather | solution.py:382
  208.1 124.0 %all-gather.11.cloned.1.call-start = ((), (), s32[]{:S(2)}) async-start(), calls=%async_computation.11 | async-start | bytes 2621440 | tf_op jit(solution)/shard_map/all_gather | solution.py:1442
  278.5 113.6 %reduce-scatter.5.cloned.1.call-start = ((), (), s32[]{:S(2)}) async-start(), calls=%async_computation.12 | async-start | bytes 3981312 | tf_op jit(solution)/shard_map/reduce_scatter | solution.py:386
  366.0 87.7 %reduce-scatter.7.cloned.1.call-start = ((), (), s32[]{:S(2)}) async-start(), calls=%async_computation.13 | async-start | bytes 4718592 | tf_op jit(solution)/shard_map/reduce_scatter | solution.py:386
  392.2 36.5 %all-to-all-start.3 = ((bf16[8,128,384]{2,1,0:T(8,128)(2,1)}), bf16[8,128,384]{2,1,0:T(8,128)(2,1)S(1)}, u32[]{:S(2)}, u32[]{:S(2)}) async-start(bf16[8,128,384]{2,1,0:T(8,128)(2,1)} %bitcast.68), calls=%async_computation.3 | async-start | bytes 1572864 | tf_op jit(solution)/shard_map/all_to_all | solution.py:1403
  395.9 100.8 %reduce-scatter.9.cloned.1.call-start = ((), (), s32[]{:S(2)}) async-start(), calls=%async_computation.14 | async-start | bytes 2949120 | tf_op jit(solution)/shard_map/reduce_scatter | solution.py:386
  399.3 31.6 %collective-permute-start.42 = (bf16[128,2048]{1,0:T(8,128)(2,1)}, bf16[128,2048]{1,0:T(8,128)(2,1)S(1)}, u32[]{:S(2)}, u32[]{:S(2)}) collective-permute-start(bf16[128,2048]{1,0:T(8,128)(2,1)} %get-tuple-element.138), channel_id=1, source_target_pairs={{0,8},{8,0},{16,24},{24,16},{1,9},{9,1},{17,25},{25,17},{2,10},{10... | collective-permute-start | bytes 1572872 | tf_op jit(solution)/shard_map/ppermute | solution.py:346
  400.4 41.0 %collective-permute-start.44 = (bf16[128,2048]{1,0:T(8,128)(2,1)}, bf16[128,2048]{1,0:T(8,128)(2,1)S(1)}, u32[]{:S(2)}, u32[]{:S(2)}) collective-permute-start(bf16[128,2048]{1,0:T(8,128)(2,1)} %get-tuple-element.140), channel_id=1, source_target_pairs={{0,24},{8,16},{16,8},{24,0},{1,25},{9,17},{17,9},{25,1},{2,26},{10... | collective-permute-start | bytes 1572872 | tf_op jit(solution)/shard_map/ppermute | solution.py:346
  401.6 39.9 %collective-permute-start.43 = (bf16[128,2048]{1,0:T(8,128)(2,1)}, bf16[128,2048]{1,0:T(8,128)(2,1)S(1)}, u32[]{:S(2)}, u32[]{:S(2)}) collective-permute-start(bf16[128,2048]{1,0:T(8,128)(2,1)} %get-tuple-element.139), channel_id=1, source_target_pairs={{0,16},{8,24},{16,0},{24,8},{1,17},{9,25},{17,1},{25,9},{2,18},{10... | collective-permute-start | bytes 1572872 | tf_op jit(solution)/shard_map/ppermute | solution.py:346
  453.7 131.1 %reduce-scatter.11.cloned.1.call-start = ((), (), s32[]{:S(2)}) async-start(), calls=%async_computation.15 | async-start | bytes 7999488 | tf_op jit(solution)/shard_map/reduce_scatter | solution.py:386
  505.9 60.0 %collective-permute-start.52 = (bf16[3456,128]{1,0:T(8,128)(2,1)}, bf16[3456,128]{1,0:T(8,128)(2,1)S(1)}, u32[]{:S(2)}, u32[]{:S(2)}) collective-permute-start(bf16[3456,128]{1,0:T(8,128)(2,1)} %get-tuple-element.152), channel_id=1, source_target_pairs={{0,16},{8,24},{16,0},{24,8},{1,17},{9,25},{17,1},{25,9},{2,18},{10... | collective-permute-start | bytes 2654216 | tf_op jit(solution)/shard_map/ppermute | solution.py:346
  507.0 59.8 %collective-permute-start.53 = (bf16[3456,128]{1,0:T(8,128)(2,1)}, bf16[3456,128]{1,0:T(8,128)(2,1)S(1)}, u32[]{:S(2)}, u32[]{:S(2)}) collective-permute-start(bf16[3456,128]{1,0:T(8,128)(2,1)} %get-tuple-element.153), channel_id=1, source_target_pairs={{0,24},{8,16},{16,8},{24,0},{1,25},{9,17},{17,9},{25,1},{2,26},{10... | collective-permute-start | bytes 2654216 | tf_op jit(solution)/shard_map/ppermute | solution.py:346
  508.3 59.5 %collective-permute-start.56 = (bf16[128,3328]{1,0:T(8,128)(2,1)S(1)}, bf16[128,3328]{1,0:T(8,128)(2,1)S(1)}, u32[]{:S(2)}, u32[]{:S(2)}) collective-permute-start(bf16[128,3328]{1,0:T(8,128)(2,1)S(1)} %pad_maximum_fusion.8.refs_0_), channel_id=1, source_target_pairs={{0,24},{8,16},{16,8},{24,0},{1,25},{9,17},{17,9},{25,1},{2,26},{10... | collective-permute-start | bytes 2555912 | tf_op jit(solution)/shard_map/ppermute | solution.py:346
  510.1 73.0 %collective-permute-start.55 = (bf16[128,3328]{1,0:T(8,128)(2,1)S(1)}, bf16[128,3328]{1,0:T(8,128)(2,1)S(1)}, u32[]{:S(2)}, u32[]{:S(2)}) collective-permute-start(bf16[128,3328]{1,0:T(8,128)(2,1)S(1)} %pad_maximum_fusion.8.refs_0_), channel_id=1, source_target_pairs={{0,16},{8,24},{16,0},{24,8},{1,17},{9,25},{17,1},{25,9},{2,18},{10... | collective-permute-start | bytes 2555912 | tf_op jit(solution)/shard_map/ppermute | solution.py:346
  527.4 56.5 %collective-permute-start.54 = (bf16[128,3328]{1,0:T(8,128)(2,1)S(1)}, bf16[128,3328]{1,0:T(8,128)(2,1)S(1)}, u32[]{:S(2)}, u32[]{:S(2)}) collective-permute-start(bf16[128,3328]{1,0:T(8,128)(2,1)S(1)} %pad_maximum_fusion.8.refs_0_), channel_id=1, source_target_pairs={{0,8},{8,0},{16,24},{24,16},{1,9},{9,1},{17,25},{25,17},{2,10},{10... | collective-permute-start | bytes 2555912 | tf_op jit(solution)/shard_map/ppermute | solution.py:346
  586.6 39.1 %collective-permute-start.58 = (bf16[3472,128]{1,0:T(8,128)(2,1)}, bf16[3472,128]{1,0:T(8,128)(2,1)S(1)}, u32[]{:S(2)}, u32[]{:S(2)}) collective-permute-start(bf16[3472,128]{1,0:T(8,128)(2,1)} %bitcast.172), channel_id=1, source_target_pairs={{0,16},{8,24},{16,0},{24,8},{1,17},{9,25},{17,1},{25,9},{2,18},{10... | collective-permute-start | bytes 2666504 | tf_op jit(solution)/shard_map/ppermute | solution.py:346
  587.1 38.5 %collective-permute-start.57 = (bf16[3472,128]{1,0:T(8,128)(2,1)}, bf16[3472,128]{1,0:T(8,128)(2,1)S(1)}, u32[]{:S(2)}, u32[]{:S(2)}) collective-permute-start(bf16[3472,128]{1,0:T(8,128)(2,1)} %bitcast.173), channel_id=1, source_target_pairs={{0,8},{8,0},{16,24},{24,16},{1,9},{9,1},{17,25},{25,17},{2,10},{10... | collective-permute-start | bytes 2666504 | tf_op jit(solution)/shard_map/ppermute | solution.py:346
  (184 other events, 2193.3 us)
Sparse Core Ops, SparseCore 0:
  14.5 96.2 all-gather.4
  113.1 65.4 all-gather.6
  210.4 29.5 all-gather.8
  278.6 48.2 all-gather.10
  332.2 47.6 reduce-scatter.4
  392.3 61.3 reduce-scatter.6
  456.7 38.9 reduce-scatter.8
  498.1 77.0 reduce-scatter.10

commit v4 on v3

--- a/solution.py
+++ b/solution.py
@@ -366,6 +366,16 @@
     )
 
 
+def exact_dot(former, latter, left, right):
+    return lax.dot_general(
+        former,
+        latter,
+        (((left,), (right,)), ((), ())),
+        precision=lax.Precision.HIGHEST,
+        preferred_element_type=jnp.float32,
+    )
+
+
 def lowered(partials):
     return [partials[0]] + [piece.astype(jnp.bfloat16) for piece in partials[1:]]
 
@@ -386,12 +396,23 @@
     return lax.psum_scatter(piece, "blk", scatter_dimension=axis, tiled=True)
 
 
+def to_core(rows):
+    count = lax.axis_size("blk")
+    return lax.ppermute(rows, "blk", [(place, place ^ 1) for place in range(count)])
+
+
+def to_chip(rows, offset):
+    count = lax.axis_size("blk")
+    return lax.ppermute(rows, "blk", [(place, place ^ (2 * offset)) for place in range(count)])
+
+
 def split_rows(rows, count):
     height = rows.shape[0] // count
     return [rows[k * height : (k + 1) * height] for k in range(count)]
 
 
 ROWS = 432
+STEP = 864
 TALL = 1728
 WIDE = 3456
 CHUNKS = 2
@@ -641,42 +662,29 @@
     )(me.reshape(1), *pieces)
 
 
-def scores_kernel(rows, table, *refs):
-    outs, total = refs[:-1], refs[-1]
-    step = pl.program_id(0)
+def scores_kernel(rows, table, *outs):
     product = jnp.dot(rows[...], table[...], preferred_element_type=jnp.float32)
-
-    @pl.when(step == 0)
-    def _():
-        total[...] = product
-
-    @pl.when(step > 0)
-    def _():
-        total[...] += product
-
-    @pl.when(step == pl.num_programs(0) - 1)
-    def _():
-        height = outs[0].shape[0]
-        for k in range(len(outs)):
-            outs[k][...] = total[k * height : (k + 1) * height, :].astype(outs[k].dtype)
+    height = outs[0].shape[0]
+    for k in range(len(outs)):
+        outs[k][...] = product[k * height : (k + 1) * height, :].astype(outs[k].dtype)
 
 
 def embed_cells(rows, table, count):
     height, quarter = rows.shape
     width = table.shape[1]
+    block = math.gcd(width, 512)
     return pl.pallas_call(
         scores_kernel,
-        grid=(quarter // WIDE,),
+        grid=(width // block,),
         out_shape=[
             jax.ShapeDtypeStruct((height // count, width), jnp.float32 if k == 0 else jnp.bfloat16)
             for k in range(count)
         ],
         in_specs=[
-            pl.BlockSpec((height, WIDE), lambda step: (0, step)),
-            pl.BlockSpec((WIDE, width), lambda step: (step, 0)),
-        ],
-        out_specs=[pl.BlockSpec((height // count, width), lambda step: (0, 0))] * count,
-        scratch_shapes=[pltpu.VMEM((height, width), jnp.float32)],
+            pl.BlockSpec((height, quarter), lambda step: (0, 0)),
+            pl.BlockSpec((quarter, block), lambda step: (0, step)),
+        ],
+        out_specs=[pl.BlockSpec((height // count, block), lambda step: (0, step))] * count,
         compiler_params=pltpu.CompilerParams(vmem_limit_bytes=58 * 2**20),
         cost_estimate=COST,
         name="embed_cells",
@@ -814,14 +822,15 @@
 
 def decode_genes(latents, table):
     count = len(latents)
-    cells, width = latents[0].shape
-    quarter = table.shape[1]
+    cells = latents[0].shape[0]
+    width, quarter = table.shape
+    last = latents[0].shape[1] // width - 1
     return pl.pallas_call(
         functools.partial(decode_kernel, count),
         grid=(1,),
         out_shape=[jax.ShapeDtypeStruct((quarter, cells), jnp.bfloat16)] * count,
         in_specs=[pl.BlockSpec((width, quarter), lambda step: (0, 0))]
-        + [pl.BlockSpec((cells, width), lambda step: (0, 0))] * count,
+        + [pl.BlockSpec((cells, width), lambda step: (0, last))] * count,
         out_specs=[pl.BlockSpec((quarter, cells), lambda step: (0, 0))] * count,
         compiler_params=pltpu.CompilerParams(vmem_limit_bytes=40 * 2**20),
         cost_estimate=COST,
@@ -829,17 +838,28 @@
     )(table, *latents)
 
 
-def last_kernel(count, first, me_ref, normed, projected, both, *refs):
-    pre_grads, cots, out = refs[:count], refs[count : 2 * count], refs[-1]
+def chip_offsets(chips):
+    order = [0]
+    bit = chips // 2
+    while bit:
+        order = order + [one + bit for one in order]
+        bit //= 2
+    return order
+
+
+def last_kernel(count, first, offsets, places, normed, projected, both, *refs):
+    pre_grads, cots = refs[:count], refs[count : 2 * count]
+    kept, sent, turned = refs[2 * count :]
+    me, place = places[0], places[1]
     cells = cots[0].shape[0]
-
     width = normed.shape[1]
+    block = kept.shape[0] // len(offsets)
 
     def by_offset(first):
         return jnp.concatenate(
             [
                 both[
-                    pl.ds(pl.multiple_of(jnp.bitwise_xor(me_ref[0], k) * cells, cells), cells),
+                    pl.ds(pl.multiple_of(jnp.bitwise_xor(me, k) * cells, cells), cells),
                     first : first + width,
                 ]
                 for k in range(count)
@@ -848,34 +868,72 @@
         )
 
     spot = 0
-    for rows, columns in (
-        (normed[...], [projected[k] for k in range(projected.shape[0])]),
-        (by_offset(0), [jnp.concatenate([one[:, first:] for one in cots], axis=0)]),
-        (by_offset(width), [jnp.concatenate([one[...] for one in pre_grads], axis=0)]),
+    for group, (rows, columns) in enumerate(
+        (
+            (normed[...], [projected[k] for k in range(projected.shape[0])]),
+            (by_offset(0), [jnp.concatenate([one[:, first:] for one in cots], axis=0)]),
+            (by_offset(width), [jnp.concatenate([one[...] for one in pre_grads], axis=0)]),
+        )
     ):
-        turned = jnp.transpose(rows)
+        turned[group] = jnp.transpose(rows)
         for one in columns:
             size = one.shape[1]
-            out[:, spot : spot + size] = jnp.dot(
-                turned, one, preferred_element_type=jnp.float32
-            ).astype(out.dtype)
+            for out, core in ((kept, place % 2), (sent, 1 - place % 2)):
+                owners = [jnp.bitwise_xor(place // 2, k) * 2 + core for k in offsets]
+                ordered = jnp.concatenate(
+                    [
+                        turned[group, pl.ds(pl.multiple_of(owner * block, block), block), :]
+                        for owner in owners
+                    ],
+                    axis=0,
+                )
+                out[:, spot : spot + size] = jnp.dot(
+                    ordered, one, preferred_element_type=jnp.float32
+                ).astype(out.dtype)
             spot += size
 
 
-def last_products(normed, projected, pre_grads, both, cots, first, me):
+def last_products(normed, projected, pre_grads, both, cots, first, me, place):
     count = len(cots)
     height = normed.shape[1]
+    offsets = chip_offsets(lax.axis_size("blk") // 2)
     width = projected.shape[0] * projected.shape[2] + 2 * pre_grads[0].shape[1]
     return pl.pallas_call(
-        functools.partial(last_kernel, count, first),
-        out_shape=jax.ShapeDtypeStruct((height, width), jnp.bfloat16),
+        functools.partial(last_kernel, count, first, offsets),
+        out_shape=[
+            jax.ShapeDtypeStruct((height // 2, width), jnp.float32),
+            jax.ShapeDtypeStruct((height // 2, width), jnp.bfloat16),
+        ],
         in_specs=[pl.BlockSpec(memory_space=pltpu.SMEM)]
         + [pl.BlockSpec(memory_space=pltpu.VMEM)] * (3 + 2 * count),
-        out_specs=pl.BlockSpec(memory_space=pltpu.VMEM),
+        out_specs=[pl.BlockSpec(memory_space=pltpu.VMEM)] * 2,
+        scratch_shapes=[pltpu.VMEM((3, height, normed.shape[0]), jnp.bfloat16)],
         compiler_params=pltpu.CompilerParams(vmem_limit_bytes=40 * 2**20),
         cost_estimate=COST,
         name="last_products",
-    )(me.reshape(1), normed, projected, both, *pre_grads, *cots)
+    )(jnp.stack([me, place]), normed, projected, both, *pre_grads, *cots)
+
+
+def half_kernel(kept, other, stay, go):
+    height = stay.shape[0]
+    stay[...] = kept[:height, :] + other[:height, :].astype(jnp.float32)
+    go[...] = (kept[height:, :] + other[height:, :].astype(jnp.float32)).astype(go.dtype)
+
+
+def merge_half(kept, other):
+    height, width = kept.shape
+    return pl.pallas_call(
+        half_kernel,
+        out_shape=[
+            jax.ShapeDtypeStruct((height // 2, width), jnp.float32),
+            jax.ShapeDtypeStruct((height // 2, width), jnp.bfloat16),
+        ],
+        in_specs=[pl.BlockSpec(memory_space=pltpu.VMEM)] * 2,
+        out_specs=[pl.BlockSpec(memory_space=pltpu.VMEM)] * 2,
+        compiler_params=pltpu.CompilerParams(vmem_limit_bytes=40 * 2**20),
+        cost_estimate=COST,
+        name="merge_half",
+    )(kept, other)
 
 
 def pair_kernel(count, *refs):
@@ -1011,20 +1069,20 @@
 def embed_kernel(count, *refs):
     parts, rows = refs[:count], refs[count : 2 * count]
     small, out, stacked, results, sems = refs[2 * count :]
-    steps = parts[0].shape[0] // ROWS
+    steps = parts[0].shape[0] // STEP
     height = rows[0].shape[0]
     blocks, _, block = out.shape
     for k in range(count):
         stacked[k * height : (k + 1) * height, :] = rows[k][...]
 
     def leave(slot, step):
-        start = pl.multiple_of(step * ROWS, ROWS)
+        start = pl.multiple_of(step * STEP, STEP)
         return pltpu.make_async_copy(
-            results.at[slot], out.at[:, pl.ds(start, ROWS), :], sems.at[slot]
+            results.at[slot], out.at[:, pl.ds(start, STEP), :], sems.at[slot]
         )
 
     last = pltpu.make_async_copy(
-        small, out.at[:, pl.ds(steps * ROWS, small.shape[1]), :], sems.at[2]
+        small, out.at[:, pl.ds(steps * STEP, small.shape[1]), :], sems.at[2]
     )
     last.start()
 
@@ -1036,7 +1094,7 @@
         def _():
             leave(slot, step - 2).wait()
 
-        here = pl.ds(pl.multiple_of(step * ROWS, ROWS), ROWS)
+        here = pl.ds(pl.multiple_of(step * STEP, STEP), STEP)
         product = jnp.dot(
             jnp.concatenate([part[here, :] for part in parts], axis=1),
             stacked[...],
@@ -1063,7 +1121,7 @@
         out_specs=pl.BlockSpec(memory_space=pltpu.HBM),
         scratch_shapes=[
             pltpu.VMEM((count * cells, width), jnp.bfloat16),
-            pltpu.VMEM((2, blocks, ROWS, block), jnp.bfloat16),
+            pltpu.VMEM((2, blocks, STEP, block), jnp.bfloat16),
             pltpu.SemaphoreType.DMA((3,)),
         ],
         compiler_params=pltpu.CompilerParams(vmem_limit_bytes=58 * 2**20),
@@ -1118,16 +1176,17 @@
     ).astype(out.dtype)
 
 
-def decoder_products(latents, cots):
+def decoder_products(latents, cots, width):
     count = len(latents)
-    cells, width = latents[0].shape
+    cells = latents[0].shape[0]
+    last = latents[0].shape[1] // width - 1
     quarter = cots[0].shape[0]
     step_rows = math.gcd(quarter, 1152)
     return pl.pallas_call(
         functools.partial(decoder_kernel, count),
         grid=(quarter // step_rows,),
         out_shape=jax.ShapeDtypeStruct((width, quarter), jnp.bfloat16),
-        in_specs=[pl.BlockSpec((cells, width), lambda step: (0, 0))] * count
+        in_specs=[pl.BlockSpec((cells, width), lambda step: (0, last))] * count
         + [pl.BlockSpec((step_rows, cells), lambda step: (step, 0))] * count,
         out_specs=pl.BlockSpec((width, step_rows), lambda step: (0, step)),
         scratch_shapes=[pltpu.VMEM((width, count * cells), jnp.bfloat16)],
@@ -1172,7 +1231,7 @@
 def attend(rows, heads):
     cells, total = rows.shape
     group = total // 3
-    height = math.gcd(cells, 256)
+    height = math.gcd(cells, 1024)
     return pl.pallas_call(
         functools.partial(attend_kernel, heads, group // heads),
         grid=(cells // height,),
@@ -1235,7 +1294,7 @@
 def attend_back(rows, cot, heads):
     cells, total = rows.shape
     group = total // 3
-    height = math.gcd(cells, 256)
+    height = math.gcd(cells, 1024)
     return pl.pallas_call(
         functools.partial(attend_back_kernel, heads, group // heads),
         grid=(cells // height,),
@@ -1405,15 +1464,15 @@
         ).reshape(blocks * cells, rows.shape[-1])
 
     out_shares = share(after(out_latent[:head_part], normed_one_all), slides)
-    head_rows = after(to_heads(projected), *out_shares[1:])
+    latent_cots = cots_to_latents(cot_parts, weight_decode)
+    head_rows = after(to_heads(projected), latent_cots[-1], *out_shares[1:])
     per_pair = pair // HEAD_DIM
     weight_down = gather_blk(after(down_part, middle, head_rows))
     latent_shares = share(after(out_latent[head_part:], head_rows), slides)
     weight_out = in_order(out_shares, me, 0)
     weight_latent = in_order(latent_shares, me, 0)
     own_heads = to_heads(attend(head_rows, per_pair)).reshape(pairs, slides, cells, pair)
-    latent_cots = cots_to_latents(cot_parts, weight_decode)
-    own_heads = after(own_heads, latent_cots[-1], *latent_shares[1:])
+    own_heads = after(own_heads, *latent_shares[1:])
     attended_parts = swap(
         [
             jnp.concatenate([own_heads[j, k] for j in range(pairs)], axis=1)
@@ -1425,6 +1484,11 @@
     normed_two, norm_two_back = jax.vjp(layer_norm, h_one, norm_float[2], norm_float[3])
     normed_two_low = normed_two.astype(jnp.bfloat16)
     normed_two_all = jnp.concatenate(share(normed_two_low, slides), axis=0)
+    centres_float = centres.astype(jnp.float32)
+    half_norms = 0.5 * jnp.sum(centres_float * centres_float, axis=0)
+    normed_two_all, half_norms, centres_float = lax.optimization_barrier(
+        (after(normed_two_all, weight_latent), half_norms, centres_float)
+    )
     hidden_pre = (
         jnp.dot(normed_two_all, weight_up, preferred_element_type=jnp.float32) + bias_up
     )
@@ -1445,9 +1509,18 @@
     latent_pre = contract_cols(h_two_low, weight_latent)
     spread = jnp.exp(0.5 * latent_pre[:, latent_width:])
     latent = latent_pre[:, :latent_width] + spread * noise[0]
-    prior, prior_back = jax.vjp(mixture_term, latent, centres.astype(jnp.float32))
-
-    latent_from_prior, centre_grad = prior_back(prior_cot[0])
+    mixing = latent_width ** (-0.5)
+    mix = (exact_dot(latent, centres_float, 1, 0) - half_norms) * mixing
+    mix_max = jnp.max(mix, axis=-1, keepdims=True)
+    mix_exp = jnp.exp(mix - mix_max)
+    mix_sum = jnp.sum(mix_exp, axis=-1, keepdims=True)
+    prior = -(mix_max + jnp.log(mix_sum))[:, 0]
+    shares = prior_cot[0][:, None] * (mix_exp / mix_sum)
+    latent_from_prior = exact_dot(shares, centres_float, 1, 1) * -mixing
+    centre_grad = (
+        centres_float * jnp.sum(shares, axis=0) - exact_dot(latent, shares, 0, 0)
+    ) * mixing
+
     latent_total = latent_from_decode + latent_from_prior
     pre_grad = jnp.concatenate(
         [latent_total, latent_total * noise[0] * spread * 0.5], axis=-1
@@ -1459,12 +1532,11 @@
         both_parts, weight_latent, weight_down, weight_up, hidden_pre
     )
     normed_two_grad = collect(normed_two_parts)
-    latent_parts = [part[:, model_width:] for part in both_parts]
-    latent_parts = [after(part, normed_two_parts[-1]) for part in latent_parts]
-    decode_local = decoder_products(latent_parts, cot_parts)
+    latent_parts = [after(part, normed_two_parts[-1]) for part in both_parts]
+    decode_local = decoder_products(latent_parts, cot_parts, latent_width)
     decoded_rows = decode_genes(latent_parts, weight_decode)
     normed_two_grad = after(normed_two_grad, decode_local, decoded_rows[-1])
-    decode_own = scatter_blk(after(decode_local, both_rows))
+    decode_own = scatter_blk(after(decode_local, both_rows, normed_two_grad))
     h_one_part, gain_two_grad, shift_two_grad = norm_two_back(normed_two_grad)
     h_one_grad = h_two_grad + h_one_part
     out_input = h_one_grad.astype(jnp.bfloat16)
@@ -1512,7 +1584,7 @@
         )
     )
     normed_one_grad = collect(normed_one_parts)
-    last_local = last_products(
+    last_kept, last_sent = last_products(
         normed_one_all,
         after(projected_grad, normed_one_parts[-1]),
         [column_part(part, latent_part, me) for part in both_parts],
@@ -1520,12 +1592,19 @@
         more_parts,
         half,
         me,
-    )
-    normed_one_grad = after(normed_one_grad, last_local)
-    last_grad = scatter_blk(after(last_local, middle_grad))
+        lax.axis_index("blk"),
+    )
+    last_kept, last_sent = merge_half(last_kept, to_core(last_sent))
+    normed_one_grad = after(normed_one_grad, last_sent)
     h_zero_part, gain_one_grad, shift_one_grad = norm_one_back(normed_one_grad)
     h_zero_low = (h_one_grad + h_zero_part).astype(jnp.bfloat16)
     h_zero_parts = share(h_zero_low, slides)
+    bit = 1
+    while last_kept.shape[0] > own_rows:
+        last_kept, last_sent = merge_half(last_kept, to_chip(last_sent, bit))
+        bit *= 2
+    h_zero_parts = [after(h_zero_parts[0], last_sent)] + h_zero_parts[1:]
+    last_grad = last_kept + to_chip(last_sent, bit).astype(jnp.float32)
 
     small_grad = jnp.concatenate(
         [
@@ -1543,10 +1622,10 @@
     gene_rows = cells_to_genes(
         embedding, [after(part, embed_local) for part in h_zero_parts], quarter
     )
-    embed_own = scatter_blk(after(embed_local, last_grad))[0]
+    embed_own = scatter_blk(after(embed_local, middle_grad))[0]
     gene_parts = swap(gene_rows)
     grad_shares = share(
-        after(jnp.concatenate([middle_grad, last_grad], axis=1), embed_local), slides
+        after(jnp.concatenate([middle_grad, last_grad.astype(jnp.bfloat16)], axis=1), embed_local), slides
     )
     embed_shares = share(after(embed_own, *gene_parts[1:], *grad_shares[1:]), slides)
     expr_grad = spread_parts(gene_parts, me, genes)

time: 648 us -> 629 us (0.971)
  waiting for transfers between devices: 316 us -> 289 us
  starting transfers between devices: 91 us -> 101 us
    ppermute x60, waiting for transfers between devices: 294 us -> 226 us  [swap(): lax.ppermute(pieces[k], 'slide', peers(k, count))]
    ppermute x0 -> x3, waiting for transfers between devices: none -> 28.9 us  [the longest x2 28.8 us: to_chip(): lax.ppermute(rows, 'blk', [(place, place ^ 2 * offset) for place in range...]
    all_gather x3, waiting for transfers between devices: 2.74 us -> 17.3 us  [gather_blk(): return lax.all_gather(piece, 'blk', axis=axis, tiled=True)]
    unnamed x291 -> x243, local copies, waits for them, and re-layouts: 35.1 us -> 34.9 us
  transfers between devices with their start and end apart: 72 -> 74, of which waited for: 44 -> 37; matrix products, arithmetic and copies ran while one was open for 11% -> 12% of each run, Pallas kernels for 16% -> 15%
where the time goes in v4:
time: 629 us; the launch traced here: 618 us
  waiting for transfers between devices  289 us (46%)
  starting transfers between devices  101 us (16%)
  Pallas kernels  99.2 us (16%)
  local copies, waits for them, and re-layouts  71.2 us (11%)
  other arithmetic  25.1 us (4%)
  matrix products  16.9 us (3%)
  between operations  16.4 us (3%)
    ppermute x60, waiting for transfers between devices, swap(): lax.ppermute(pieces[k], 'slide', peers(k, count))  226 us
    ppermute x60, starting transfers between devices, swap(): lax.ppermute(pieces[k], 'slide', peers(k, count))  78.7 us
    unnamed x243, local copies, waits for them, and re-layouts  34.9 us
    ppermute x2, waiting for transfers between devices, to_chip(): lax.ppermute(rows, 'blk', [(place, place ^ 2 * offset) for place in range...  28.8 us
    all_gather x3, waiting for transfers between devices, gather_blk(): return lax.all_gather(piece, 'blk', axis=axis, tiled=True)  17.3 us
    all_to_all x4, starting transfers between devices, to_heads(): lax.all_to_all(rows.reshape(blocks, cells, rows.shape[-1]), 'blk', 0, 0,...  16.7 us
    all_to_all x4, waiting for transfers between devices, to_heads(): lax.all_to_all(rows.reshape(blocks, cells, rows.shape[-1]), 'blk', 0, 0,...  14.1 us
  transfers between devices with their start and end apart: 74, of which 37 were waited for; matrix products, arithmetic and copies ran while one was open for 12% of the time, Pallas kernels for 15%

profile of v4, /device:TPU:0, one launch (start us, length us, event | category | flops | bytes accessed | tf_op | source)
XLA Modules:
  0.0 618.5 jit_solution(7150763596767164133)
XLA Ops:
  17.5 6.6 %expression.1 = (bf16[3456,128]{1,0:T(8,128)(2,1)S(1)}, bf16[3456,128]{1,0:T(8,128)(2,1)}, bf16[3456,128]{1,0:T(8,128)(2,1)}, bf16[3456,128]{1,0:T(8,128)(2,1)}) custom-call(s32[1]{0:T(128)} %bitcast.me_ref, s32[1,128]{1,0:T(1,128)S(1)} %copy-done.47, s32[13500,1,128]{2,1,0:T(1,128)S(1)} %bitcast.159), custom_call_target="tpu_custom_call" | custom-call | tf_op jit(solution)/shard_map/expression/pallas_call | solution.py:468
  38.2 9.5 %collective-permute-done.refs_1_ = bf16[3456,128]{1,0:T(8,128)(2,1)S(1)} collective-permute-done((bf16[3456,128]{1,0:T(8,128)(2,1)}, bf16[3456,128]{1,0:T(8,128)(2,1)S(1)}, u32[]{:S(2)}, u32[]{:S(2)}) %collective-permute-start) | collective-permute-done | bytes 884768 | tf_op jit(solution)/shard_map/ppermute | solution.py:346
  47.7 19.7 %collective-permute-done.1.refs_2_ = bf16[3456,128]{1,0:T(8,128)(2,1)} collective-permute-done((bf16[3456,128]{1,0:T(8,128)(2,1)}, bf16[3456,128]{1,0:T(8,128)(2,1)}, u32[]{:S(2)}, u32[]{:S(2)}) %collective-permute-start.1) | collective-permute-done | bytes 884768 | tf_op jit(solution)/shard_map/ppermute | solution.py:346
  77.1 13.2 %collective-permute-done.3.refs_1_.refs_5_ = bf16[3456,128]{1,0:T(8,128)(2,1)} collective-permute-done((bf16[3456,128]{1,0:T(8,128)(2,1)}, bf16[3456,128]{1,0:T(8,128)(2,1)}, u32[]{:S(2)}, u32[]{:S(2)}) %collective-permute-start.3) | collective-permute-done | bytes 884768 | tf_op jit(solution)/shard_map/ppermute | solution.py:346
  90.3 17.8 %collective-permute-done.4.refs_2_.refs_6_ = bf16[3456,128]{1,0:T(8,128)(2,1)} collective-permute-done((bf16[3456,128]{1,0:T(8,128)(2,1)}, bf16[3456,128]{1,0:T(8,128)(2,1)}, u32[]{:S(2)}, u32[]{:S(2)}) %collective-permute-start.4) | collective-permute-done | bytes 884768 | tf_op jit(solution)/shard_map/ppermute | solution.py:346
  112.6 8.0 %embed_cells.1 = (f32[128,1024]{1,0:T(8,128)}, bf16[128,1024]{1,0:T(8,128)(2,1)}, bf16[128,1024]{1,0:T(8,128)(2,1)}, bf16[128,1024]{1,0:T(8,128)(2,1)}) custom-call(bf16[512,3456]{1,0:T(8,128)(2,1)} %copy-done.2, bf16[4752,1024]{1,0:T(8,128)(2,1)} %all-gather.5.cloned.1.call-done.table), custom_call_target="tpu_custom_call" | custom-call | tf_op jit(solution)/shard_map/embed_cells/pallas_call | solution.py:676
  130.0 6.1 collective-permute-done.10
  164.4 14.6 %all-gather.7.cloned.1.call-done = bf16[1024,2816]{1,0:T(8,128)(2,1)} async-done(((bf16[128,2816]{1,0:T(8,128)(2,1)}), bf16[1024,2816]{1,0:T(8,128)(2,1)}) %all-gather.7.cloned.1.call-update) | async-done | bytes 5767184 | tf_op jit(solution)/shard_map/all_gather | solution.py:392
  192.9 8.2 %collective-permute-start.20 = (bf16[256,1024]{1,0:T(8,128)(2,1)}, bf16[256,1024]{1,0:T(8,128)(2,1)}, u32[]{:S(2)}, u32[]{:S(2)}) collective-permute-start(bf16[256,1024]{1,0:T(8,128)(2,1)} %get-tuple-element.120), channel_id=1, source_target_pairs={{0,24},{8,16},{16,8},{24,0},{1,25},{9,17},{17,9},{25,1},{2,26},{10... | collective-permute-start | bytes 1572872 | tf_op jit(solution)/shard_map/ppermute | solution.py:346
  285.2 11.9 %collective-permute-done.32.refs_3_ = bf16[128,1536]{1,0:T(8,128)(2,1)S(1)} collective-permute-done((bf16[128,1536]{1,0:T(8,128)(2,1)S(1)}, bf16[128,1536]{1,0:T(8,128)(2,1)S(1)}, u32[]{:S(2)}, u32[]{:S(2)}) %collective-permute-start.32) | collective-permute-done | bytes 393248 | tf_op jit(solution)/shard_map/ppermute | solution.py:346
  303.3 9.6 %feed_back.1 = (f32[128,1024]{1,0:T(8,128)}, bf16[512,1024]{1,0:T(8,128)(2,1)}, bf16[512,1024]{1,0:T(8,128)(2,1)}, f32[1,1024]{1,0:T(1,128)}, f32[128,1024]{1,0:...) custom-call(bf16[1024,1024]{1,0:T(8,128)(2,1)} %pad_maximum_fusion.4.latent, ...), custom_call_target="tpu_custom_call" | custom-call | tf_op jit(solution)/shard_map/feed_back/pallas_call | solution.py:799
  323.8 5.7 decoder_products.1
  357.2 8.4 %all-to-all-done.2 = bf16[8,128,128]{2,1,0:T(8,128)(2,1)S(1)} async-done(((bf16[8,128,128]{2,1,0:T(8,128)(2,1)}), bf16[8,128,128]{2,1,0:T(8,128)(2,1)S(1)}, u32[]{:S(2)}, u32[]{:S(2)}) %all-to-all-start.2) | async-done | bytes 262176 | tf_op jit(solution)/shard_map/all_to_all | solution.py:1462
  365.6 10.5 %attend_back.1 = bf16[1024,384]{1,0:T(8,128)(2,1)} custom-call(bf16[1024,384]{1,0:T(8,128)(2,1)} %bitcast.23.rows_ref, bf16[1024,128]{1,0:T(8,128)(2,1)S(1)} %bitcast.162), custom_call_target="tpu_custom_call" | custom-call | tf_op jit(solution)/shard_map/attend_back/pallas_call | solution.py:1298
  393.0 13.0 %collective-permute-done.41.rest_3_ = bf16[3456,128]{1,0:T(8,128)(2,1)S(1)} collective-permute-done((bf16[3456,128]{1,0:T(8,128)(2,1)}, bf16[3456,128]{1,0:T(8,128)(2,1)S(1)}, u32[]{:S(2)}, u32[]{:S(2)}) %collective-permute-start.41) | collective-permute-done | bytes 884768 | tf_op jit(solution)/shard_map/ppermute | solution.py:346
  417.1 10.8 %collective-permute-done.44.refs_7_ = bf16[128,2048]{1,0:T(8,128)(2,1)S(1)} collective-permute-done((bf16[128,2048]{1,0:T(8,128)(2,1)}, bf16[128,2048]{1,0:T(8,128)(2,1)S(1)}, u32[]{:S(2)}, u32[]{:S(2)}) %collective-permute-start.44) | collective-permute-done | bytes 524320 | tf_op jit(solution)/shard_map/ppermute | solution.py:346
  444.1 6.2 %collective-permute-done.46 = bf16[128,1024]{1,0:T(8,128)(2,1)S(1)} collective-permute-done((bf16[128,1024]{1,0:T(8,128)(2,1)S(1)}, bf16[128,1024]{1,0:T(8,128)(2,1)S(1)}, u32[]{:S(2)}, u32[]{:S(2)}) %collective-permute-start.46) | collective-permute-done | bytes 262176 | tf_op jit(solution)/shard_map/ppermute | solution.py:346
  459.0 8.0 %collective-permute-done.49.other = bf16[256,1280]{1,0:T(8,128)(2,1)S(1)} collective-permute-done((bf16[256,1280]{1,0:T(8,128)(2,1)S(1)}, bf16[256,1280]{1,0:T(8,128)(2,1)S(1)}, u32[]{:S(2)}, u32[]{:S(2)}) %collective-permute-start.49) | collective-permute-done | bytes 655392 | tf_op jit(solution)/shard_map/ppermute | solution.py:406
  469.1 8.1 %embed_products.1 = bf16[8,3472,128]{2,1,0:T(8,128)(2,1)} custom-call(bf16[3456,128]{1,0:T(8,128)(2,1)} %copy-done.18, bf16[3456,128]{1,0:T(8,128)(2,1)} %copy-done.19, bf16[3456,128]{1,0:T(8,128)(2,1)} %collective-permute-done.1.refs_2_, bf16[3456,128]{1,0:T(8,128)(2,1)} %collective-permute-done.2.refs_3_, ...), custom_call_target="tpu_custom_call" | custom-call | tf_op jit(solution)/shard_map/embed_products/pallas_call | solution.py:1117
  479.9 7.8 %cells_to_genes.1 = (bf16[3456,128]{1,0:T(8,128)(2,1)}, bf16[3456,128]{1,0:T(8,128)(2,1)}, bf16[3456,128]{1,0:T(8,128)(2,1)}, bf16[3456,128]{1,0:T(8,128)(2,1)}) custom-call(bf16[4752,1024]{1,0:T(8,128)(2,1)} %all-gather.5.cloned.1.call-done.table, bf16[128,1024]{1,0:T(8,128)(2,1)} %add_convert_fusion.1.refs_4_.refs_0_, ...), custom_call_target="tpu_custom_call" | custom-call | tf_op jit(solution)/shard_map/cells_to_genes/pallas_call | solution.py:1055
  491.3 20.8 %collective-permute-done.56 = bf16[128,1280]{1,0:T(8,128)(2,1)S(1)} collective-permute-done((bf16[128,1280]{1,0:T(8,128)(2,1)}, bf16[128,1280]{1,0:T(8,128)(2,1)S(1)}, u32[]{:S(2)}, u32[]{:S(2)}) %collective-permute-start.56) | collective-permute-done | bytes 327712 | tf_op jit(solution)/shard_map/ppermute | solution.py:406
  515.8 31.7 %collective-permute-done.54.rest_2_ = bf16[3456,128]{1,0:T(8,128)(2,1)S(1)} collective-permute-done((bf16[3456,128]{1,0:T(8,128)(2,1)}, bf16[3456,128]{1,0:T(8,128)(2,1)S(1)}, u32[]{:S(2)}, u32[]{:S(2)}) %collective-permute-start.54) | collective-permute-done | bytes 884768 | tf_op jit(solution)/shard_map/ppermute | solution.py:346
  550.2 14.6 %collective-permute-done.58.refs_2_ = bf16[128,3328]{1,0:T(8,128)(2,1)S(1)} collective-permute-done((bf16[128,3328]{1,0:T(8,128)(2,1)S(1)}, bf16[128,3328]{1,0:T(8,128)(2,1)S(1)}, u32[]{:S(2)}, u32[]{:S(2)}) %collective-permute-start.58) | collective-permute-done | bytes 852000 | tf_op jit(solution)/shard_map/ppermute | solution.py:346
  590.5 16.6 %collective-permute-done.61.refs_2_ = bf16[3472,128]{1,0:T(8,128)(2,1)S(1)} collective-permute-done((bf16[3472,128]{1,0:T(8,128)(2,1)}, bf16[3472,128]{1,0:T(8,128)(2,1)S(1)}, u32[]{:S(2)}, u32[]{:S(2)}) %collective-permute-start.61) | collective-permute-done | bytes 888864 | tf_op jit(solution)/shard_map/ppermute | solution.py:346
  (512 shorter events, 314.6 us)
Async XLA Ops:
  7.2 103.7 %all-gather.5.cloned.1.call-start = ((), (), s32[]{:S(2)}) async-start(), calls=%async_computation.7 | async-start | bytes 10948608 | tf_op jit(solution)/shard_map/all_gather | solution.py:392
  14.4 164.6 %all-gather.7.cloned.1.call-start = ((), (), s32[]{:S(2)}) async-start(), calls=%async_computation.8 | async-start | bytes 6488064 | tf_op jit(solution)/shard_map/all_gather | solution.py:392
  27.0 40.4 %collective-permute-start.1 = (bf16[3456,128]{1,0:T(8,128)(2,1)}, bf16[3456,128]{1,0:T(8,128)(2,1)}, u32[]{:S(2)}, u32[]{:S(2)}) collective-permute-start(bf16[3456,128]{1,0:T(8,128)(2,1)} %get-tuple-element.103), channel_id=1, source_target_pairs={{0,16},{8,24},{16,0},{24,8},{1,17},{9,25},{17,1},{25,9},{2,18},{10... | collective-permute-start | bytes 2654216 | tf_op jit(solution)/shard_map/ppermute | solution.py:346
  28.5 38.9 %collective-permute-start.2 = (bf16[3456,128]{1,0:T(8,128)(2,1)}, bf16[3456,128]{1,0:T(8,128)(2,1)}, u32[]{:S(2)}, u32[]{:S(2)}) collective-permute-start(bf16[3456,128]{1,0:T(8,128)(2,1)} %get-tuple-element.104), channel_id=1, source_target_pairs={{0,24},{8,16},{16,8},{24,0},{1,25},{9,17},{17,9},{25,1},{2,26},{10... | collective-permute-start | bytes 2654216 | tf_op jit(solution)/shard_map/ppermute | solution.py:346
  68.6 39.5 %collective-permute-start.4 = (bf16[3456,128]{1,0:T(8,128)(2,1)}, bf16[3456,128]{1,0:T(8,128)(2,1)}, u32[]{:S(2)}, u32[]{:S(2)}) collective-permute-start(bf16[3456,128]{1,0:T(8,128)(2,1)} %get-tuple-element.106), channel_id=1, source_target_pairs={{0,16},{8,24},{16,0},{24,8},{1,17},{9,25},{17,1},{25,9},{2,18},{10... | collective-permute-start | bytes 2654216 | tf_op jit(solution)/shard_map/ppermute | solution.py:346
  69.5 38.7 %collective-permute-start.5 = (bf16[3456,128]{1,0:T(8,128)(2,1)}, bf16[3456,128]{1,0:T(8,128)(2,1)}, u32[]{:S(2)}, u32[]{:S(2)}) collective-permute-start(bf16[3456,128]{1,0:T(8,128)(2,1)} %get-tuple-element.107), channel_id=1, source_target_pairs={{0,24},{8,16},{16,8},{24,0},{1,25},{9,17},{17,9},{25,1},{2,26},{10... | collective-permute-start | bytes 2654216 | tf_op jit(solution)/shard_map/ppermute | solution.py:346
  153.7 34.4 %all-to-all-start = ((bf16[8,128,384]{2,1,0:T(8,128)(2,1)}), bf16[8,128,384]{2,1,0:T(8,128)(2,1)}, u32[]{:S(2)}, u32[]{:S(2)}) async-start(bf16[8,128,384]{2,1,0:T(8,128)(2,1)} %bitcast.22), calls=%async_computation | async-start | bytes 1572864 | tf_op jit(solution)/shard_map/all_to_all | solution.py:1462
  205.8 48.7 %all-gather.9.cloned.1.call-start = ((), (), s32[]{:S(2)}) async-start(), calls=%async_computation.9 | async-start | bytes 2359296 | tf_op jit(solution)/shard_map/all_gather | solution.py:392
  215.4 115.5 %all-gather.11.cloned.1.call-start = ((), (), s32[]{:S(2)}) async-start(), calls=%async_computation.10 | async-start | bytes 2621440 | tf_op jit(solution)/shard_map/all_gather | solution.py:1506
  218.4 43.0 %collective-permute-start.8 = (bf16[128,512]{1,0:T(8,128)(2,1)}, bf16[128,512]{1,0:T(8,128)(2,1)}, u32[]{:S(2)}, u32[]{:S(2)}) collective-permute-start(bf16[128,512]{1,0:T(8,128)(2,1)} %get-tuple-element.113), channel_id=1, source_target_pairs={{0,24},{8,16},{16,8},{24,0},{1,25},{9,17},{17,9},{25,1},{2,26},{10... | collective-permute-start | bytes 393224 | tf_op jit(solution)/shard_map/ppermute | solution.py:346
  221.2 39.5 %collective-permute-start.6 = (bf16[128,512]{1,0:T(8,128)(2,1)}, bf16[128,512]{1,0:T(8,128)(2,1)}, u32[]{:S(2)}, u32[]{:S(2)}) collective-permute-start(bf16[128,512]{1,0:T(8,128)(2,1)} %get-tuple-element.111), channel_id=1, source_target_pairs={{0,8},{8,0},{16,24},{24,16},{1,9},{9,1},{17,25},{25,17},{2,10},{10... | collective-permute-start | bytes 393224 | tf_op jit(solution)/shard_map/ppermute | solution.py:346
  274.7 103.6 %reduce-scatter.4.cloned.1.call-start = ((), (), s32[]{:S(2)}) async-start(), calls=%async_computation.11 | async-start | bytes 3981312 | tf_op jit(solution)/shard_map/reduce_scatter | solution.py:396
  351.3 126.0 %reduce-scatter.6.cloned.1.call-start = ((), (), s32[]{:S(2)}) async-start(), calls=%async_computation.12 | async-start | bytes 4718592 | tf_op jit(solution)/shard_map/reduce_scatter | solution.py:396
  382.0 184.7 %reduce-scatter.8.cloned.1.call-start = ((), (), s32[]{:S(2)}) async-start(), calls=%async_computation.13 | async-start | bytes 7999488 | tf_op jit(solution)/shard_map/reduce_scatter | solution.py:396
  386.6 41.3 %collective-permute-start.44 = (bf16[128,2048]{1,0:T(8,128)(2,1)}, bf16[128,2048]{1,0:T(8,128)(2,1)S(1)}, u32[]{:S(2)}, u32[]{:S(2)}) collective-permute-start(bf16[128,2048]{1,0:T(8,128)(2,1)} %get-tuple-element.154), channel_id=1, source_target_pairs={{0,24},{8,16},{16,8},{24,0},{1,25},{9,17},{17,9},{25,1},{2,26},{10... | collective-permute-start | bytes 1572872 | tf_op jit(solution)/shard_map/ppermute | solution.py:346
  388.1 39.8 %collective-permute-start.43 = (bf16[128,2048]{1,0:T(8,128)(2,1)}, bf16[128,2048]{1,0:T(8,128)(2,1)S(1)}, u32[]{:S(2)}, u32[]{:S(2)}) collective-permute-start(bf16[128,2048]{1,0:T(8,128)(2,1)} %get-tuple-element.153), channel_id=1, source_target_pairs={{0,16},{8,24},{16,0},{24,8},{1,17},{9,25},{17,1},{25,9},{2,18},{10... | collective-permute-start | bytes 1572872 | tf_op jit(solution)/shard_map/ppermute | solution.py:346
  477.3 34.8 %collective-permute-start.56 = (bf16[128,1280]{1,0:T(8,128)(2,1)}, bf16[128,1280]{1,0:T(8,128)(2,1)S(1)}, u32[]{:S(2)}, u32[]{:S(2)}) collective-permute-start(bf16[128,1280]{1,0:T(8,128)(2,1)} %get-tuple-element.163), channel_id=1, source_target_pairs={{0,4},{1,5},{2,6},{3,7},{4,0},{5,1},{6,2},{7,3},{8,12},{9,13},{10,... | collective-permute-start | bytes 983048 | tf_op jit(solution)/shard_map/ppermute | solution.py:406
  489.2 58.3 %collective-permute-start.54 = (bf16[3456,128]{1,0:T(8,128)(2,1)}, bf16[3456,128]{1,0:T(8,128)(2,1)S(1)}, u32[]{:S(2)}, u32[]{:S(2)}) collective-permute-start(bf16[3456,128]{1,0:T(8,128)(2,1)} %get-tuple-element.172), channel_id=1, source_target_pairs={{0,16},{8,24},{16,0},{24,8},{1,17},{9,25},{17,1},{25,9},{2,18},{10... | collective-permute-start | bytes 2654216 | tf_op jit(solution)/shard_map/ppermute | solution.py:346
  489.8 58.6 %collective-permute-start.55 = (bf16[3456,128]{1,0:T(8,128)(2,1)}, bf16[3456,128]{1,0:T(8,128)(2,1)S(1)}, u32[]{:S(2)}, u32[]{:S(2)}) collective-permute-start(bf16[3456,128]{1,0:T(8,128)(2,1)} %get-tuple-element.173), channel_id=1, source_target_pairs={{0,24},{8,16},{16,8},{24,0},{1,25},{9,17},{17,9},{25,1},{2,26},{10... | collective-permute-start | bytes 2654216 | tf_op jit(solution)/shard_map/ppermute | solution.py:346
  512.2 37.1 %collective-permute-start.59 = (bf16[128,3328]{1,0:T(8,128)(2,1)S(1)}, bf16[128,3328]{1,0:T(8,128)(2,1)S(1)}, u32[]{:S(2)}, u32[]{:S(2)}) collective-permute-start(bf16[128,3328]{1,0:T(8,128)(2,1)S(1)} %pad_maximum_fusion.8.refs_0_), channel_id=1, source_target_pairs={{0,24},{8,16},{16,8},{24,0},{1,25},{9,17},{17,9},{25,1},{2,26},{10... | collective-permute-start | bytes 2555912 | tf_op jit(solution)/shard_map/ppermute | solution.py:346
  512.6 52.3 %collective-permute-start.58 = (bf16[128,3328]{1,0:T(8,128)(2,1)S(1)}, bf16[128,3328]{1,0:T(8,128)(2,1)S(1)}, u32[]{:S(2)}, u32[]{:S(2)}) collective-permute-start(bf16[128,3328]{1,0:T(8,128)(2,1)S(1)} %pad_maximum_fusion.8.refs_0_), channel_id=1, source_target_pairs={{0,16},{8,24},{16,0},{24,8},{1,17},{9,25},{17,1},{25,9},{2,18},{10... | collective-permute-start | bytes 2555912 | tf_op jit(solution)/shard_map/ppermute | solution.py:346
  515.2 50.6 %collective-permute-start.57 = (bf16[128,3328]{1,0:T(8,128)(2,1)S(1)}, bf16[128,3328]{1,0:T(8,128)(2,1)S(1)}, u32[]{:S(2)}, u32[]{:S(2)}) collective-permute-start(bf16[128,3328]{1,0:T(8,128)(2,1)S(1)} %pad_maximum_fusion.8.refs_0_), channel_id=1, source_target_pairs={{0,8},{8,0},{16,24},{24,16},{1,9},{9,1},{17,25},{25,17},{2,10},{10... | collective-permute-start | bytes 2555912 | tf_op jit(solution)/shard_map/ppermute | solution.py:346
  568.1 39.0 %collective-permute-start.61 = (bf16[3472,128]{1,0:T(8,128)(2,1)}, bf16[3472,128]{1,0:T(8,128)(2,1)S(1)}, u32[]{:S(2)}, u32[]{:S(2)}) collective-permute-start(bf16[3472,128]{1,0:T(8,128)(2,1)} %bitcast.165), channel_id=1, source_target_pairs={{0,16},{8,24},{16,0},{24,8},{1,17},{9,25},{17,1},{25,9},{2,18},{10... | collective-permute-start | bytes 2666504 | tf_op jit(solution)/shard_map/ppermute | solution.py:346
  568.7 38.3 %collective-permute-start.60 = (bf16[3472,128]{1,0:T(8,128)(2,1)}, bf16[3472,128]{1,0:T(8,128)(2,1)S(1)}, u32[]{:S(2)}, u32[]{:S(2)}) collective-permute-start(bf16[3472,128]{1,0:T(8,128)(2,1)} %bitcast.166), channel_id=1, source_target_pairs={{0,8},{8,0},{16,24},{24,16},{1,9},{9,1},{17,25},{25,17},{2,10},{10... | collective-permute-start | bytes 2666504 | tf_op jit(solution)/shard_map/ppermute | solution.py:346
  (162 other events, 1668.2 us)
Sparse Core Ops, SparseCore 0:
  14.5 96.2 all-gather.4
  113.1 65.9 all-gather.6
  215.5 30.6 all-gather.8
  274.8 45.2 all-gather.10
  331.1 47.1 reduce-scatter.3
  381.1 58.8 reduce-scatter.5
  477.4 79.6 reduce-scatter.7

commit v5 on v4

--- a/solution.py
+++ b/solution.py
@@ -347,6 +347,16 @@
     ]
 
 
+def share_halves(rows):
+    half = rows.shape[0] // 2
+    upper, lower = rows[:half], rows[half:]
+    upper_x = lax.ppermute(upper, "slide", peers(1, 4))
+    lower_y = lax.ppermute(lower, "slide", peers(2, 4))
+    uppers = lax.ppermute(jnp.concatenate([upper, upper_x], axis=0), "slide", peers(2, 4))
+    lowers = lax.ppermute(jnp.concatenate([lower, lower_y], axis=0), "slide", peers(1, 4))
+    return [rows, upper_x, lower_y, uppers, lowers]
+
+
 def share(rows, count):
     return swap([rows] * count)
 
@@ -577,6 +587,35 @@
         compiler_params=pltpu.CompilerParams(vmem_limit_bytes=40 * 2**20),
         cost_estimate=COST,
         name="join",
+    )(me.reshape(1), *pieces)
+
+
+def order_kernel(count, me_ref, *refs):
+    pieces, out, sems = refs[:count], refs[-2], refs[-1]
+    height = pieces[0].shape[0]
+
+    def move(k):
+        first = pl.multiple_of(jnp.bitwise_xor(me_ref[0], k) * height, height)
+        return pltpu.make_async_copy(pieces[k], out.at[pl.ds(first, height), :], sems.at[k])
+
+    for k in range(count):
+        move(k).start()
+    for k in range(count):
+        move(k).wait()
+
+
+def order_rows(pieces, me):
+    count = len(pieces)
+    height, width = pieces[0].shape
+    return pl.pallas_call(
+        functools.partial(order_kernel, count),
+        out_shape=jax.ShapeDtypeStruct((count * height, width), pieces[0].dtype),
+        in_specs=[pl.BlockSpec(memory_space=pltpu.SMEM)]
+        + [pl.BlockSpec(memory_space=pl.ANY)] * count,
+        out_specs=pl.BlockSpec(memory_space=pltpu.VMEM),
+        scratch_shapes=[pltpu.SemaphoreType.DMA((count,))],
+        cost_estimate=COST,
+        name="order_rows",
     )(me.reshape(1), *pieces)
 
 
@@ -958,57 +997,65 @@
 
 
 def assemble_kernel(count, sizes, me_ref, *refs):
-    parts, decoder = refs[:count], refs[count : 2 * count]
-    down, up, qkv, attn, latent, decode, held, halves, sems = refs[2 * count :]
+    early, parts = refs[:5], refs[5 : 5 + count]
+    down, up, qkv, attn, latent, decode, middle, last, sems = refs[5 + count :]
     blocks, pairs, pair, quarter, half = sizes
-
-    def arrive(k):
-        place = jnp.bitwise_xor(me_ref[0], k)
-        return (
-            pltpu.make_async_copy(parts[k], held.at[place], sems.at[0, k]),
-            pltpu.make_async_copy(decoder[k], halves.at[place], sems.at[1, k]),
-        )
-
-    for k in range(count):
-        for one in arrive(k):
-            one.start()
-    for k in range(count):
-        for one in arrive(k):
-            one.wait()
+    me = me_ref[0]
     rows, width = attn.shape
+    cut = rows // 2
+    upper, lower = pl.ds(0, cut), pl.ds(cut, cut)
+    ours, upper_x, lower_y, uppers, lowers = early
+    moves = [
+        (ours, middle.at[me]),
+        (upper_x, middle.at[jnp.bitwise_xor(me, 1), upper, :]),
+        (lower_y, middle.at[jnp.bitwise_xor(me, 2), lower, :]),
+        (uppers.at[upper, :], middle.at[jnp.bitwise_xor(me, 2), upper, :]),
+        (uppers.at[lower, :], middle.at[jnp.bitwise_xor(me, 3), upper, :]),
+        (lowers.at[upper, :], middle.at[jnp.bitwise_xor(me, 1), lower, :]),
+        (lowers.at[lower, :], middle.at[jnp.bitwise_xor(me, 3), lower, :]),
+    ] + [(parts[k], last.at[jnp.bitwise_xor(me, k)]) for k in range(count)]
+    copies = [
+        pltpu.make_async_copy(source, target, sems.at[k])
+        for k, (source, target) in enumerate(moves)
+    ]
+    for one in copies:
+        one.start()
+    for one in copies:
+        one.wait()
     part = width // count
     ff = up.shape[1] // (count * blocks)
     latents, genes = decode.shape
 
-    def piece(q, spot, size):
-        return held[q, :, spot : spot + size].astype(jnp.float32)
+    def piece(array, q, spot, size):
+        return array[q, :, spot : spot + size].astype(jnp.float32)
 
     for q in range(count):
-        down[q * rows : (q + 1) * rows, :] = piece(q, 0, width)
+        down[q * rows : (q + 1) * rows, :] = piece(middle, q, 0, width)
         spot = width
         for b in range(blocks):
-            up[:, (b * count + q) * ff : (b * count + q + 1) * ff] = piece(q, spot, ff)
+            up[:, (b * count + q) * ff : (b * count + q + 1) * ff] = piece(middle, q, spot, ff)
             spot += ff
-        for j in range(pairs):
-            for t in range(3):
-                first = t * width + q * part + j * pair
-                qkv[:, first : first + pair] = piece(q, spot, pair)
-                spot += pair
-        for out in (attn, latent):
-            out[:, q * part : (q + 1) * part] = piece(q, spot, part)
-            spot += part
         for side in range(2):
             first = q * quarter + side * half
             size = min(half, quarter - side * half, genes - first)
             if size > 0:
-                decode[:, first : first + size] = halves[
-                    q, side * latents : (side + 1) * latents, :size
+                decode[:, first : first + size] = middle[
+                    q, side * latents : (side + 1) * latents, spot : spot + size
                 ].astype(jnp.float32)
-
-
-def assemble(parts, decoder, me, genes, quarter, half, latents, blocks, pairs, pair):
-    count = len(parts)
-    rows = parts[0].shape[0]
+        spot = 0
+        for j in range(pairs):
+            for t in range(3):
+                first = t * width + q * part + j * pair
+                qkv[:, first : first + pair] = piece(last, q, spot, pair)
+                spot += pair
+        for out in (attn, latent):
+            out[:, q * part : (q + 1) * part] = piece(last, q, spot, part)
+            spot += part
+
+
+def assemble(early, last, me, genes, quarter, half, latents, blocks, pairs, pair):
+    count = len(last)
+    rows = last[0].shape[0]
     width = blocks * rows
     shapes = [
         (count * rows, width),
@@ -1022,17 +1069,17 @@
         functools.partial(assemble_kernel, count, (blocks, pairs, pair, quarter, half)),
         out_shape=[jax.ShapeDtypeStruct(shape, jnp.float32) for shape in shapes],
         in_specs=[pl.BlockSpec(memory_space=pltpu.SMEM)]
-        + [pl.BlockSpec(memory_space=pl.ANY)] * (2 * count),
+        + [pl.BlockSpec(memory_space=pl.ANY)] * (5 + count),
         out_specs=[pl.BlockSpec(memory_space=pltpu.VMEM)] * len(shapes),
         scratch_shapes=[
-            pltpu.VMEM((count,) + parts[0].shape, jnp.bfloat16),
-            pltpu.VMEM((count,) + decoder[0].shape, jnp.bfloat16),
-            pltpu.SemaphoreType.DMA((2, count)),
+            pltpu.VMEM((count,) + early[0].shape, jnp.bfloat16),
+            pltpu.VMEM((count,) + last[0].shape, jnp.bfloat16),
+            pltpu.SemaphoreType.DMA((7 + count,)),
         ],
         compiler_params=pltpu.CompilerParams(vmem_limit_bytes=48 * 2**20),
         cost_estimate=COST,
         name="assemble",
-    )(me.reshape(1), *parts, *decoder)
+    )(me.reshape(1), *early, *last)
 
 
 def genes_kernel(count, table, *refs):
@@ -1465,12 +1512,16 @@
 
     out_shares = share(after(out_latent[:head_part], normed_one_all), slides)
     latent_cots = cots_to_latents(cot_parts, weight_decode)
-    head_rows = after(to_heads(projected), latent_cots[-1], *out_shares[1:])
+    centres_float = centres.astype(jnp.float32)
+    half_norms = 0.5 * jnp.sum(centres_float * centres_float, axis=0)
+    head_rows, half_norms, centres_float = lax.optimization_barrier(
+        (after(to_heads(projected), latent_cots[-1], *out_shares[1:]), half_norms, centres_float)
+    )
     per_pair = pair // HEAD_DIM
     weight_down = gather_blk(after(down_part, middle, head_rows))
     latent_shares = share(after(out_latent[head_part:], head_rows), slides)
-    weight_out = in_order(out_shares, me, 0)
-    weight_latent = in_order(latent_shares, me, 0)
+    weight_out = order_rows(out_shares, me)
+    weight_latent = order_rows(latent_shares, me)
     own_heads = to_heads(attend(head_rows, per_pair)).reshape(pairs, slides, cells, pair)
     own_heads = after(own_heads, *latent_shares[1:])
     attended_parts = swap(
@@ -1484,11 +1535,7 @@
     normed_two, norm_two_back = jax.vjp(layer_norm, h_one, norm_float[2], norm_float[3])
     normed_two_low = normed_two.astype(jnp.bfloat16)
     normed_two_all = jnp.concatenate(share(normed_two_low, slides), axis=0)
-    centres_float = centres.astype(jnp.float32)
-    half_norms = 0.5 * jnp.sum(centres_float * centres_float, axis=0)
-    normed_two_all, half_norms, centres_float = lax.optimization_barrier(
-        (after(normed_two_all, weight_latent), half_norms, centres_float)
-    )
+    normed_two_all = after(normed_two_all, weight_latent)
     hidden_pre = (
         jnp.dot(normed_two_all, weight_up, preferred_element_type=jnp.float32) + bias_up
     )
@@ -1558,23 +1605,14 @@
     out_heads = after(out_heads, *decoded_parts[1:-1])
     head_grads = attend_back(head_rows, out_heads, per_pair)
     middle_grad = scatter_blk(after(middle_local, decode_own, head_grads))
-    decode_half = jnp.concatenate(
-        [decode_own[:, :half], jnp.pad(decode_own[:, half:], ((0, 0), (0, 2 * half - quarter)))],
-        axis=0,
-    )
-    more_parts = swap(
+    cot_cols = swap(
         [
-            after(
-                jnp.concatenate(
-                    [decode_half, column_part(out_input, head_part, place_of(k))], axis=1
-                ),
-                head_grads,
-            )
+            after(column_part(out_input, head_part, place_of(k)), head_grads)
             for k in range(slides)
         ]
     )
     projected_grad = to_heads(head_grads).reshape(pairs, slides * cells, 3 * pair)
-    projected_grad = after(projected_grad, decoded_parts[-1], *more_parts[1:])
+    projected_grad = after(projected_grad, decoded_parts[-1], *cot_cols[1:])
     normed_one_parts = lowered(
         split_rows(
             jnp.einsum(
@@ -1589,8 +1627,8 @@
         after(projected_grad, normed_one_parts[-1]),
         [column_part(part, latent_part, me) for part in both_parts],
         both_rows,
-        more_parts,
-        half,
+        cot_cols,
+        0,
         me,
         lax.axis_index("blk"),
     )
@@ -1604,7 +1642,7 @@
         last_kept, last_sent = merge_half(last_kept, to_chip(last_sent, bit))
         bit *= 2
     h_zero_parts = [after(h_zero_parts[0], last_sent)] + h_zero_parts[1:]
-    last_grad = last_kept + to_chip(last_sent, bit).astype(jnp.float32)
+    last_other = to_chip(last_sent, bit)
 
     small_grad = jnp.concatenate(
         [
@@ -1623,15 +1661,24 @@
         embedding, [after(part, embed_local) for part in h_zero_parts], quarter
     )
     embed_own = scatter_blk(after(embed_local, middle_grad))[0]
-    gene_parts = swap(gene_rows)
-    grad_shares = share(
-        after(jnp.concatenate([middle_grad, last_grad.astype(jnp.bfloat16)], axis=1), embed_local), slides
-    )
-    embed_shares = share(after(embed_own, *gene_parts[1:], *grad_shares[1:]), slides)
+    decode_half = jnp.concatenate(
+        [decode_own[:, :half], jnp.pad(decode_own[:, half:], ((0, 0), (0, 2 * half - quarter)))],
+        axis=0,
+    )
+    early = after(jnp.concatenate([middle_grad, decode_half], axis=1), *h_zero_parts[1:])
+    early_parts = share_halves(early)
+    gene_parts = swap([after(part, *early_parts[1:3]) for part in gene_rows])
+    last_low = (last_kept + after(last_other, *gene_parts[1:3]).astype(jnp.float32)).astype(
+        jnp.bfloat16
+    )
+    last_shares = share(last_low, slides)
+    embed_shares = share(
+        after(embed_own, *gene_parts[1:], *last_shares[1:], *early_parts[1:]), slides
+    )
     expr_grad = spread_parts(gene_parts, me, genes)
     decoded = join_parts(decoded_parts, me, quarter, genes, jnp.bfloat16).T
     down_grad, up_grad, qkv_grad, attn_out_grad, latent_grad, decode_grad = assemble(
-        grad_shares, more_parts, me, genes, quarter, half, own_latents, blocks, pairs, pair
+        early_parts, last_shares, me, genes, quarter, half, own_latents, blocks, pairs, pair
     )
     embed_grad, norm_grad, means_grad, up_bias_grad = finish(
         embed_shares, me, quarter, genes, mean_cols, folds

time: 629 us -> 611 us (0.971)
  waiting for transfers between devices: 289 us -> 278 us
  Pallas kernels: 99.2 us -> 106 us
    ppermute x60, waiting for transfers between devices: 226 us -> 193 us  [swap(): lax.ppermute(pieces[k], 'slide', peers(k, count))]
    ppermute x0 -> x4, waiting for transfers between devices: none -> 25.2 us  [the longest x1 22.4 us: share_halves(): lax.ppermute(jnp.concatenate([upper, upper_x], axis=0), 'slide', peers(2,...]
    unnamed x243 -> x223, local copies, waits for them, and re-layouts: 34.9 us -> 37.4 us
  transfers between devices with their start and end apart: 74 -> 78, of which waited for: 37 -> 44; matrix products, arithmetic and copies ran while one was open for 12% -> 11% of each run, Pallas kernels for 15% -> 17%
where the time goes in v5:
time: 611 us; the launch traced here: 601 us
  waiting for transfers between devices  278 us (45%)
  Pallas kernels  106 us (17%)
  starting transfers between devices  96.3 us (16%)
  local copies, waits for them, and re-layouts  67.2 us (11%)
  other arithmetic  19.5 us (3%)
  matrix products  18 us (3%)
  between operations  16.2 us (3%)
    ppermute x60, waiting for transfers between devices, swap(): lax.ppermute(pieces[k], 'slide', peers(k, count))  193 us
    ppermute x60, starting transfers between devices, swap(): lax.ppermute(pieces[k], 'slide', peers(k, count))  73.5 us
    unnamed x223, local copies, waits for them, and re-layouts  37.4 us
    ppermute x2, waiting for transfers between devices, to_chip(): lax.ppermute(rows, 'blk', [(place, place ^ 2 * offset) for place in range...  25.4 us
    ppermute x1, waiting for transfers between devices, share_halves(): lax.ppermute(jnp.concatenate([upper, upper_x], axis=0), 'slide', peers(2,...  22.4 us
    all_to_all x4, starting transfers between devices, to_heads(): lax.all_to_all(rows.reshape(blocks, cells, rows.shape[-1]), 'blk', 0, 0,...  17 us
    all_to_all x4, waiting for transfers between devices, to_heads(): lax.all_to_all(rows.reshape(blocks, cells, rows.shape[-1]), 'blk', 0, 0,...  16.1 us
    all_gather x3, waiting for transfers between devices, gather_blk(): return lax.all_gather(piece, 'blk', axis=axis, tiled=True)  16 us
  transfers between devices with their start and end apart: 78, of which 44 were waited for; matrix products, arithmetic and copies ran while one was open for 11% of the time, Pallas kernels for 17%

profile of v5, /device:TPU:0, one launch (start us, length us, event | category | flops | bytes accessed | tf_op | source)
XLA Modules:
  0.0 601.1 jit_solution(17761554372086609854)
XLA Ops:
  18.3 6.6 %expression.1 = (bf16[3456,128]{1,0:T(8,128)(2,1)S(1)}, bf16[3456,128]{1,0:T(8,128)(2,1)}, bf16[3456,128]{1,0:T(8,128)(2,1)}, bf16[3456,128]{1,0:T(8,128)(2,1)}) custom-call(s32[1]{0:T(128)} %bitcast.me_ref, s32[1,128]{1,0:T(1,128)S(1)} %copy-done.45, s32[13500,1,128]{2,1,0:T(1,128)S(1)} %bitcast.139), custom_call_target="tpu_custom_call" | custom-call | tf_op jit(solution)/shard_map/expression/pallas_call | solution.py:478
  38.8 9.8 %collective-permute-done.refs_1_ = bf16[3456,128]{1,0:T(8,128)(2,1)} collective-permute-done((bf16[3456,128]{1,0:T(8,128)(2,1)}, bf16[3456,128]{1,0:T(8,128)(2,1)}, u32[]{:S(2)}, u32[]{:S(2)}) %collective-permute-start) | collective-permute-done | bytes 884768 | tf_op jit(solution)/shard_map/ppermute | solution.py:346
  48.6 19.6 %collective-permute-done.1.refs_2_ = bf16[3456,128]{1,0:T(8,128)(2,1)} collective-permute-done((bf16[3456,128]{1,0:T(8,128)(2,1)}, bf16[3456,128]{1,0:T(8,128)(2,1)}, u32[]{:S(2)}, u32[]{:S(2)}) %collective-permute-start.1) | collective-permute-done | bytes 884768 | tf_op jit(solution)/shard_map/ppermute | solution.py:346
  78.2 12.9 %collective-permute-done.3.refs_1_.refs_5_ = bf16[3456,128]{1,0:T(8,128)(2,1)} collective-permute-done((bf16[3456,128]{1,0:T(8,128)(2,1)}, bf16[3456,128]{1,0:T(8,128)(2,1)}, u32[]{:S(2)}, u32[]{:S(2)}) %collective-permute-start.3) | collective-permute-done | bytes 884768 | tf_op jit(solution)/shard_map/ppermute | solution.py:346
  91.1 17.8 %collective-permute-done.4.refs_2_.refs_6_ = bf16[3456,128]{1,0:T(8,128)(2,1)} collective-permute-done((bf16[3456,128]{1,0:T(8,128)(2,1)}, bf16[3456,128]{1,0:T(8,128)(2,1)}, u32[]{:S(2)}, u32[]{:S(2)}) %collective-permute-start.4) | collective-permute-done | bytes 884768 | tf_op jit(solution)/shard_map/ppermute | solution.py:346
  112.7 8.0 %embed_cells.1 = (f32[128,1024]{1,0:T(8,128)}, bf16[128,1024]{1,0:T(8,128)(2,1)}, bf16[128,1024]{1,0:T(8,128)(2,1)}, bf16[128,1024]{1,0:T(8,128)(2,1)}) custom-call(bf16[512,3456]{1,0:T(8,128)(2,1)} %copy-done.4, bf16[4752,1024]{1,0:T(8,128)(2,1)} %all-gather.5.cloned.1.call-done.table), custom_call_target="tpu_custom_call" | custom-call | tf_op jit(solution)/shard_map/embed_cells/pallas_call | solution.py:715
  130.4 5.9 collective-permute-done.10
  166.0 13.3 %all-gather.7.cloned.1.call-done = bf16[1024,2816]{1,0:T(8,128)(2,1)} async-done(((bf16[128,2816]{1,0:T(8,128)(2,1)}), bf16[1024,2816]{1,0:T(8,128)(2,1)}) %all-gather.7.cloned.1.call-update) | async-done | bytes 5767184 | tf_op jit(solution)/shard_map/all_gather | solution.py:402
  205.8 6.0 %all-to-all-done.1 = bf16[8,128,128]{2,1,0:T(8,128)(2,1)} async-done(((bf16[8,128,128]{2,1,0:T(8,128)(2,1)}), bf16[8,128,128]{2,1,0:T(8,128)(2,1)}, u32[]{:S(2)}, u32[]{:S(2)}) %all-to-all-start.1) | async-done | bytes 262176 | tf_op jit(solution)/shard_map/all_to_all | solution.py:1509
  279.0 11.5 %collective-permute-done.32.refs_3_ = bf16[128,1536]{1,0:T(8,128)(2,1)S(1)} collective-permute-done((bf16[128,1536]{1,0:T(8,128)(2,1)S(1)}, bf16[128,1536]{1,0:T(8,128)(2,1)S(1)}, u32[]{:S(2)}, u32[]{:S(2)}) %collective-permute-start.32) | collective-permute-done | bytes 393248 | tf_op jit(solution)/shard_map/ppermute | solution.py:346
  296.6 9.8 %feed_back.1 = (f32[128,1024]{1,0:T(8,128)}, bf16[512,1024]{1,0:T(8,128)(2,1)}, bf16[512,1024]{1,0:T(8,128)(2,1)}, f32[1,1024]{1,0:T(1,128)}, f32[128,1024]{1,0:...) custom-call(bf16[1024,1024]{1,0:T(8,128)(2,1)} %order_rows.3.latent, ...), custom_call_target="tpu_custom_call" | custom-call | tf_op jit(solution)/shard_map/feed_back/pallas_call | solution.py:838
  318.0 5.7 decoder_products.1
  356.0 5.9 all-to-all-done.2
  362.0 9.4 %attend_back.1 = bf16[1024,384]{1,0:T(8,128)(2,1)} custom-call(bf16[1024,384]{1,0:T(8,128)(2,1)S(1)} %bitcast.138, bf16[1024,128]{1,0:T(8,128)(2,1)S(1)} %bitcast.142), custom_call_target="tpu_custom_call" | custom-call | tf_op jit(solution)/shard_map/attend_back/pallas_call | solution.py:1345
  386.7 16.5 %collective-permute-done.42.refs_5_ = bf16[128,256]{1,0:T(8,128)(2,1)S(1)} collective-permute-done((bf16[128,256]{1,0:T(8,128)(2,1)S(1)}, bf16[128,256]{1,0:T(8,128)(2,1)S(1)}, u32[]{:S(2)}, u32[]{:S(2)}) %collective-permute-start.42) | collective-permute-done | bytes 65568 | tf_op jit(solution)/shard_map/ppermute | solution.py:346
  424.2 6.4 %collective-permute-done.46 = bf16[128,1024]{1,0:T(8,128)(2,1)S(1)} collective-permute-done((bf16[128,1024]{1,0:T(8,128)(2,1)S(1)}, bf16[128,1024]{1,0:T(8,128)(2,1)S(1)}, u32[]{:S(2)}, u32[]{:S(2)}) %collective-permute-start.46) | collective-permute-done | bytes 262176 | tf_op jit(solution)/shard_map/ppermute | solution.py:346
  438.2 11.1 %collective-permute-done.49.other = bf16[256,1280]{1,0:T(8,128)(2,1)S(1)} collective-permute-done((bf16[256,1280]{1,0:T(8,128)(2,1)S(1)}, bf16[256,1280]{1,0:T(8,128)(2,1)S(1)}, u32[]{:S(2)}, u32[]{:S(2)}) %collective-permute-start.49) | collective-permute-done | bytes 655392 | tf_op jit(solution)/shard_map/ppermute | solution.py:416
  451.0 8.1 %embed_products.1 = bf16[8,3472,128]{2,1,0:T(8,128)(2,1)} custom-call(bf16[3456,128]{1,0:T(8,128)(2,1)} %copy-done.17, bf16[3456,128]{1,0:T(8,128)(2,1)} %collective-permute-done.refs_1_, bf16[3456,128]{1,0:T(8,128)(2,1)} %collective-permute-done.1.refs_2_, bf16[3456,128]{1,0:T(8,128)(2,1)} %collective-permute-done.2.refs_3_, ...), custom_call_target="tpu_custom_call" | custom-call | tf_op jit(solution)/shard_map/embed_products/pallas_call | solution.py:1164
  463.6 8.1 %cells_to_genes.1 = (bf16[3456,128]{1,0:T(8,128)(2,1)}, bf16[3456,128]{1,0:T(8,128)(2,1)}, bf16[3456,128]{1,0:T(8,128)(2,1)}, bf16[3456,128]{1,0:T(8,128)(2,1)}) custom-call(bf16[4752,1024]{1,0:T(8,128)(2,1)} %all-gather.5.cloned.1.call-done.table, bf16[128,1024]{1,0:T(8,128)(2,1)} %add_convert_fusion.1.refs_4_.refs_0_, ...), custom_call_target="tpu_custom_call" | custom-call | tf_op jit(solution)/shard_map/cells_to_genes/pallas_call | solution.py:1102
  478.9 14.3 %collective-permute-done.58 = bf16[128,1280]{1,0:T(8,128)(2,1)S(1)} collective-permute-done((bf16[128,1280]{1,0:T(8,128)(2,1)S(1)}, bf16[128,1280]{1,0:T(8,128)(2,1)S(1)}, u32[]{:S(2)}, u32[]{:S(2)}) %collective-permute-start.58) | collective-permute-done | bytes 327712 | tf_op jit(solution)/shard_map/ppermute | solution.py:416
  493.6 21.1 %collective-permute-done.56.rest_2_ = bf16[3456,128]{1,0:T(8,128)(2,1)S(1)} collective-permute-done((bf16[3456,128]{1,0:T(8,128)(2,1)}, bf16[3456,128]{1,0:T(8,128)(2,1)S(1)}, u32[]{:S(2)}, u32[]{:S(2)}) %collective-permute-start.56) | collective-permute-done | bytes 884768 | tf_op jit(solution)/shard_map/ppermute | solution.py:346
  520.3 22.4 %collective-permute-done.62.refs_3_ = bf16[128,3840]{1,0:T(8,128)(2,1)S(1)} collective-permute-done((bf16[128,3840]{1,0:T(8,128)(2,1)S(1)}, bf16[128,3840]{1,0:T(8,128)(2,1)S(1)}, u32[]{:S(2)}, u32[]{:S(2)}) %collective-permute-start.62) | collective-permute-done | bytes 983072 | tf_op jit(solution)/shard_map/ppermute | solution.py:355
  564.7 6.9 %assemble.1 = (f32[512,1024]{1,0:T(8,128)}, f32[128,4096]{1,0:T(8,128)}, f32[128,3072]{1,0:T(8,128)}, f32[128,1024]{1,0:T(8,128)}, f32[128,1024]{1,0:T(8,128)}, /*index=5*/f32[64,13500]{1,0:T(8,128)}) custom-call(s32[1]{0:T(128)} %bitcast.me_ref, bf16[128,3840]{1,0:T(8,128)(2,1)S(1)} %fusion.18.refs_0_, ...), custom_call_target="tpu_custom_call" | custom-call | tf_op jit(solution)/shard_map/assemble/pallas_call | solution.py:1068
  574.1 15.7 %collective-permute-done.65.refs_2_ = bf16[3472,128]{1,0:T(8,128)(2,1)S(1)} collective-permute-done((bf16[3472,128]{1,0:T(8,128)(2,1)}, bf16[3472,128]{1,0:T(8,128)(2,1)S(1)}, u32[]{:S(2)}, u32[]{:S(2)}) %collective-permute-start.65) | collective-permute-done | bytes 888864 | tf_op jit(solution)/shard_map/ppermute | solution.py:346
  (498 shorter events, 312.1 us)
Async XLA Ops:
  7.2 104.5 %all-gather.5.cloned.1.call-start = ((), (), s32[]{:S(2)}) async-start(), calls=%async_computation.7 | async-start | bytes 10948608 | tf_op jit(solution)/shard_map/all_gather | solution.py:402
  15.2 164.1 %all-gather.7.cloned.1.call-start = ((), (), s32[]{:S(2)}) async-start(), calls=%async_computation.8 | async-start | bytes 6488064 | tf_op jit(solution)/shard_map/all_gather | solution.py:402
  27.8 40.4 %collective-permute-start.1 = (bf16[3456,128]{1,0:T(8,128)(2,1)}, bf16[3456,128]{1,0:T(8,128)(2,1)}, u32[]{:S(2)}, u32[]{:S(2)}) collective-permute-start(bf16[3456,128]{1,0:T(8,128)(2,1)} %get-tuple-element.108), channel_id=1, source_target_pairs={{0,16},{8,24},{16,0},{24,8},{1,17},{9,25},{17,1},{25,9},{2,18},{10... | collective-permute-start | bytes 2654216 | tf_op jit(solution)/shard_map/ppermute | solution.py:346
  29.3 38.9 %collective-permute-start.2 = (bf16[3456,128]{1,0:T(8,128)(2,1)}, bf16[3456,128]{1,0:T(8,128)(2,1)}, u32[]{:S(2)}, u32[]{:S(2)}) collective-permute-start(bf16[3456,128]{1,0:T(8,128)(2,1)} %get-tuple-element.109), channel_id=1, source_target_pairs={{0,24},{8,16},{16,8},{24,0},{1,25},{9,17},{17,9},{25,1},{2,26},{10... | collective-permute-start | bytes 2654216 | tf_op jit(solution)/shard_map/ppermute | solution.py:346
  69.4 39.5 %collective-permute-start.4 = (bf16[3456,128]{1,0:T(8,128)(2,1)}, bf16[3456,128]{1,0:T(8,128)(2,1)}, u32[]{:S(2)}, u32[]{:S(2)}) collective-permute-start(bf16[3456,128]{1,0:T(8,128)(2,1)} %get-tuple-element.111), channel_id=1, source_target_pairs={{0,16},{8,24},{16,0},{24,8},{1,17},{9,25},{17,1},{25,9},{2,18},{10... | collective-permute-start | bytes 2654216 | tf_op jit(solution)/shard_map/ppermute | solution.py:346
  70.3 38.7 %collective-permute-start.5 = (bf16[3456,128]{1,0:T(8,128)(2,1)}, bf16[3456,128]{1,0:T(8,128)(2,1)}, u32[]{:S(2)}, u32[]{:S(2)}) collective-permute-start(bf16[3456,128]{1,0:T(8,128)(2,1)} %get-tuple-element.112), channel_id=1, source_target_pairs={{0,24},{8,16},{16,8},{24,0},{1,25},{9,17},{17,9},{25,1},{2,26},{10... | collective-permute-start | bytes 2654216 | tf_op jit(solution)/shard_map/ppermute | solution.py:346
  155.5 33.7 %all-to-all-start = ((bf16[8,128,384]{2,1,0:T(8,128)(2,1)}), bf16[8,128,384]{2,1,0:T(8,128)(2,1)S(1)}, u32[]{:S(2)}, u32[]{:S(2)}) async-start(bf16[8,128,384]{2,1,0:T(8,128)(2,1)} %bitcast.22), calls=%async_computation | async-start | bytes 1572864 | tf_op jit(solution)/shard_map/all_to_all | solution.py:1509
  201.9 46.9 %all-gather.9.cloned.1.call-start = ((), (), s32[]{:S(2)}) async-start(), calls=%async_computation.9 | async-start | bytes 2359296 | tf_op jit(solution)/shard_map/all_gather | solution.py:402
  202.7 123.3 %all-gather.11.cloned.1.call-start = ((), (), s32[]{:S(2)}) async-start(), calls=%async_computation.10 | async-start | bytes 2621440 | tf_op jit(solution)/shard_map/all_gather | solution.py:1553
  268.6 105.6 %reduce-scatter.4.cloned.1.call-start = ((), (), s32[]{:S(2)}) async-start(), calls=%async_computation.11 | async-start | bytes 3981312 | tf_op jit(solution)/shard_map/reduce_scatter | solution.py:406
  347.6 111.5 %reduce-scatter.6.cloned.1.call-start = ((), (), s32[]{:S(2)}) async-start(), calls=%async_computation.12 | async-start | bytes 4718592 | tf_op jit(solution)/shard_map/reduce_scatter | solution.py:406
  374.2 33.9 %all-to-all-start.3 = ((bf16[8,128,384]{2,1,0:T(8,128)(2,1)}), bf16[8,128,384]{2,1,0:T(8,128)(2,1)S(1)}, u32[]{:S(2)}, u32[]{:S(2)}) async-start(bf16[8,128,384]{2,1,0:T(8,128)(2,1)} %bitcast.52), calls=%async_computation.3 | async-start | bytes 1572864 | tf_op jit(solution)/shard_map/all_to_all | solution.py:1509
  377.8 172.5 %reduce-scatter.8.cloned.1.call-start = ((), (), s32[]{:S(2)}) async-start(), calls=%async_computation.13 | async-start | bytes 7999488 | tf_op jit(solution)/shard_map/reduce_scatter | solution.py:406
  463.6 29.6 %collective-permute-start.58 = (bf16[128,1280]{1,0:T(8,128)(2,1)S(1)}, bf16[128,1280]{1,0:T(8,128)(2,1)S(1)}, u32[]{:S(2)}, u32[]{:S(2)}) collective-permute-start(bf16[128,1280]{1,0:T(8,128)(2,1)S(1)} %get-tuple-element.167), channel_id=1, source_target_pairs={{0,4},{1,5},{2,6},{3,7},{4,0},{5,1},{6,2},{7,3},{8,12},{9,13},{10,... | collective-permute-start | bytes 983048 | tf_op jit(solution)/shard_map/ppermute | solution.py:416
  474.4 40.2 %collective-permute-start.56 = (bf16[3456,128]{1,0:T(8,128)(2,1)}, bf16[3456,128]{1,0:T(8,128)(2,1)S(1)}, u32[]{:S(2)}, u32[]{:S(2)}) collective-permute-start(bf16[3456,128]{1,0:T(8,128)(2,1)} %get-tuple-element.182), channel_id=1, source_target_pairs={{0,16},{8,24},{16,0},{24,8},{1,17},{9,25},{17,1},{25,9},{2,18},{10... | collective-permute-start | bytes 2654216 | tf_op jit(solution)/shard_map/ppermute | solution.py:346
  475.2 39.4 %collective-permute-start.55 = (bf16[3456,128]{1,0:T(8,128)(2,1)}, bf16[3456,128]{1,0:T(8,128)(2,1)S(1)}, u32[]{:S(2)}, u32[]{:S(2)}) collective-permute-start(bf16[3456,128]{1,0:T(8,128)(2,1)} %get-tuple-element.180), channel_id=1, source_target_pairs={{0,8},{8,0},{16,24},{24,16},{1,9},{9,1},{17,25},{25,17},{2,10},{10... | collective-permute-start | bytes 2654216 | tf_op jit(solution)/shard_map/ppermute | solution.py:346
  476.9 65.8 %collective-permute-start.62 = (bf16[128,3840]{1,0:T(8,128)(2,1)S(1)}, bf16[128,3840]{1,0:T(8,128)(2,1)S(1)}, u32[]{:S(2)}, u32[]{:S(2)}) collective-permute-start(bf16[128,3840]{1,0:T(8,128)(2,1)S(1)} %pad_maximum_fusion.4), channel_id=1, source_target_pairs={{0,16},{8,24},{16,0},{24,8},{1,17},{9,25},{17,1},{25,9},{2,18},{10... | collective-permute-start | bytes 2949128 | tf_op jit(solution)/shard_map/ppermute | solution.py:355
  478.2 39.7 %collective-permute-start.57 = (bf16[3456,128]{1,0:T(8,128)(2,1)}, bf16[3456,128]{1,0:T(8,128)(2,1)S(1)}, u32[]{:S(2)}, u32[]{:S(2)}) collective-permute-start(bf16[3456,128]{1,0:T(8,128)(2,1)} %get-tuple-element.184), channel_id=1, source_target_pairs={{0,24},{8,16},{16,8},{24,0},{1,25},{9,17},{17,9},{25,1},{2,26},{10... | collective-permute-start | bytes 2654216 | tf_op jit(solution)/shard_map/ppermute | solution.py:346
  493.2 50.5 %collective-permute-start.63 = (bf16[128,3840]{1,0:T(8,128)(2,1)S(1)}, bf16[128,3840]{1,0:T(8,128)(2,1)S(1)}, u32[]{:S(2)}, u32[]{:S(2)}) collective-permute-start(bf16[128,3840]{1,0:T(8,128)(2,1)S(1)} %pad_maximum_fusion.5), channel_id=1, source_target_pairs={{0,8},{8,0},{16,24},{24,16},{1,9},{9,1},{17,25},{25,17},{2,10},{10... | collective-permute-start | bytes 2949128 | tf_op jit(solution)/shard_map/ppermute | solution.py:356
  514.7 31.1 %collective-permute-start.61 = (bf16[128,1280]{1,0:T(8,128)(2,1)S(1)}, bf16[128,1280]{1,0:T(8,128)(2,1)S(1)}, u32[]{:S(2)}, u32[]{:S(2)}) collective-permute-start(bf16[128,1280]{1,0:T(8,128)(2,1)S(1)} %add_convert_fusion.refs_5_), channel_id=1, source_target_pairs={{0,24},{8,16},{16,8},{24,0},{1,25},{9,17},{17,9},{25,1},{2,26},{10... | collective-permute-start | bytes 983048 | tf_op jit(solution)/shard_map/ppermute | solution.py:346
  516.7 32.2 %collective-permute-start.60 = (bf16[128,1280]{1,0:T(8,128)(2,1)S(1)}, bf16[128,1280]{1,0:T(8,128)(2,1)S(1)}, u32[]{:S(2)}, u32[]{:S(2)}) collective-permute-start(bf16[128,1280]{1,0:T(8,128)(2,1)S(1)} %add_convert_fusion.refs_5_), channel_id=1, source_target_pairs={{0,16},{8,24},{16,0},{24,8},{1,17},{9,25},{17,1},{25,9},{2,18},{10... | collective-permute-start | bytes 983048 | tf_op jit(solution)/shard_map/ppermute | solution.py:346
  518.9 30.7 %collective-permute-start.59 = (bf16[128,1280]{1,0:T(8,128)(2,1)S(1)}, bf16[128,1280]{1,0:T(8,128)(2,1)S(1)}, u32[]{:S(2)}, u32[]{:S(2)}) collective-permute-start(bf16[128,1280]{1,0:T(8,128)(2,1)S(1)} %add_convert_fusion.refs_5_), channel_id=1, source_target_pairs={{0,8},{8,0},{16,24},{24,16},{1,9},{9,1},{17,25},{25,17},{2,10},{10... | collective-permute-start | bytes 983048 | tf_op jit(solution)/shard_map/ppermute | solution.py:346
  552.5 37.2 %collective-permute-start.65 = (bf16[3472,128]{1,0:T(8,128)(2,1)}, bf16[3472,128]{1,0:T(8,128)(2,1)S(1)}, u32[]{:S(2)}, u32[]{:S(2)}) collective-permute-start(bf16[3472,128]{1,0:T(8,128)(2,1)} %bitcast.144), channel_id=1, source_target_pairs={{0,16},{8,24},{16,0},{24,8},{1,17},{9,25},{17,1},{25,9},{2,18},{10... | collective-permute-start | bytes 2666504 | tf_op jit(solution)/shard_map/ppermute | solution.py:346
  553.4 36.3 %collective-permute-start.64 = (bf16[3472,128]{1,0:T(8,128)(2,1)}, bf16[3472,128]{1,0:T(8,128)(2,1)S(1)}, u32[]{:S(2)}, u32[]{:S(2)}) collective-permute-start(bf16[3472,128]{1,0:T(8,128)(2,1)} %bitcast.145), channel_id=1, source_target_pairs={{0,8},{8,0},{16,24},{24,16},{1,9},{9,1},{17,25},{25,17},{2,10},{10... | collective-permute-start | bytes 2666504 | tf_op jit(solution)/shard_map/ppermute | solution.py:346
  (156 other events, 1758.1 us)
Sparse Core Ops, SparseCore 0:
  15.4 96.2 all-gather.4
  113.9 65.3 all-gather.6
  204.9 29.5 all-gather.8
  268.7 47.3 all-gather.10
  326.2 47.9 reduce-scatter.3
  377.0 58.8 reduce-scatter.5
  459.3 81.0 reduce-scatter.7

commit v6 on v5

--- a/solution.py
+++ b/solution.py
@@ -785,6 +785,75 @@
     return 0.5 * (1.0 + bent) + 0.5 * rows * (1.0 - bent * bent) * inner
 
 
+UNITS = 256
+
+
+def feed_forward_kernel(count, up, bias, down, *refs):
+    parts, stacked, total = refs[:count], refs[-2], refs[-1]
+    pre, hidden, *outs = refs[count:-2]
+    cells = parts[0].shape[0]
+    step = pl.program_id(0)
+
+    @pl.when(step == 0)
+    def _():
+        for k in range(count):
+            stacked[k * cells : (k + 1) * cells, :] = parts[k][...]
+
+    rows = jnp.dot(stacked[...], up[...], preferred_element_type=jnp.float32) + bias[...]
+    pre[...] = rows
+    bent = jnp.tanh(math.sqrt(2.0 / math.pi) * (rows + 0.044715 * (rows * rows * rows)))
+    low = (rows * (0.5 * (1.0 + bent))).astype(jnp.bfloat16)
+    hidden[...] = low
+    product = jnp.dot(low, down[...], preferred_element_type=jnp.float32)
+
+    @pl.when(step == 0)
+    def _():
+        total[...] = product
+
+    @pl.when(step > 0)
+    def _():
+        total[...] += product
+
+    @pl.when(step == pl.num_programs(0) - 1)
+    def _():
+        for k in range(count):
+            outs[k][...] = total[k * cells : (k + 1) * cells, :].astype(outs[k].dtype)
+
+
+def feed_forward(parts, up, bias, down):
+    count = len(parts)
+    cells, width = parts[0].shape
+    units = down.shape[0]
+    rows = count * cells
+    return pl.pallas_call(
+        functools.partial(feed_forward_kernel, count),
+        grid=(units // UNITS,),
+        out_shape=[
+            jax.ShapeDtypeStruct((rows, units), jnp.float32),
+            jax.ShapeDtypeStruct((rows, units), jnp.bfloat16),
+        ]
+        + [
+            jax.ShapeDtypeStruct((cells, width), jnp.float32 if k == 0 else jnp.bfloat16)
+            for k in range(count)
+        ],
+        in_specs=[
+            pl.BlockSpec((width, UNITS), lambda step: (0, step)),
+            pl.BlockSpec((1, UNITS), lambda step: (0, step)),
+            pl.BlockSpec((UNITS, width), lambda step: (step, 0)),
+        ]
+        + [pl.BlockSpec((cells, width), lambda step: (0, 0))] * count,
+        out_specs=[pl.BlockSpec((rows, UNITS), lambda step: (0, step))] * 2
+        + [pl.BlockSpec((cells, width), lambda step: (0, 0))] * count,
+        scratch_shapes=[
+            pltpu.VMEM((rows, width), jnp.bfloat16),
+            pltpu.VMEM((rows, width), jnp.float32),
+        ],
+        compiler_params=pltpu.CompilerParams(vmem_limit_bytes=48 * 2**20),
+        cost_estimate=COST,
+        name="feed_forward",
+    )(up, bias, down, *parts)
+
+
 def feed_back_kernel(count, latent, down, up, pre, *refs):
     parts = refs[:count]
     own, down_input, pre_grad, bias, *outs = refs[count:]
@@ -839,7 +908,9 @@
         functools.partial(feed_back_kernel, count),
         grid=(1,),
         out_shape=shapes,
-        in_specs=[whole(one) for one in operands],
+        in_specs=[whole(one) for one in operands[:2]]
+        + [pl.BlockSpec((width, units), lambda step: (0, 0))]
+        + [whole(one) for one in operands[3:]],
         out_specs=[whole(one) for one in shapes],
         compiler_params=pltpu.CompilerParams(vmem_limit_bytes=56 * 2**20),
         cost_estimate=COST,
@@ -1487,8 +1558,7 @@
             *cot_parts[1:],
         )
     )
-    weight_up, halves = jnp.split(middle, [model_width], axis=1)
-    halves = halves.reshape(blocks, 2, own_latents, half)
+    halves = middle[:, model_width:].reshape(blocks, 2, own_latents, half)
     weight_decode = jnp.concatenate(
         [
             halves[:, 0].reshape(latent_width, half),
@@ -1518,11 +1588,12 @@
         (after(to_heads(projected), latent_cots[-1], *out_shares[1:]), half_norms, centres_float)
     )
     per_pair = pair // HEAD_DIM
-    weight_down = gather_blk(after(down_part, middle, head_rows))
     latent_shares = share(after(out_latent[head_part:], head_rows), slides)
     weight_out = order_rows(out_shares, me)
     weight_latent = order_rows(latent_shares, me)
-    own_heads = to_heads(attend(head_rows, per_pair)).reshape(pairs, slides, cells, pair)
+    head_out = attend(head_rows, per_pair)
+    weight_down = gather_blk(after(down_part, middle, weight_out))
+    own_heads = to_heads(head_out).reshape(pairs, slides, cells, pair)
     own_heads = after(own_heads, *latent_shares[1:])
     attended_parts = swap(
         [
@@ -1534,19 +1605,13 @@
     h_one = h_zero + contract_cols(attended_low, weight_out)
     normed_two, norm_two_back = jax.vjp(layer_norm, h_one, norm_float[2], norm_float[3])
     normed_two_low = normed_two.astype(jnp.bfloat16)
-    normed_two_all = jnp.concatenate(share(normed_two_low, slides), axis=0)
-    normed_two_all = after(normed_two_all, weight_latent)
-    hidden_pre = (
-        jnp.dot(normed_two_all, weight_up, preferred_element_type=jnp.float32) + bias_up
-    )
-    hidden_low = jax.nn.gelu(hidden_pre).astype(jnp.bfloat16)
-    h_two_sum = collect(
-        lowered(
-            split_rows(
-                jnp.dot(hidden_low, weight_down, preferred_element_type=jnp.float32), slides
-            )
-        )
-    )
+    normed_two_rows = share(normed_two_low, slides)
+    normed_two_rows[0] = after(normed_two_rows[0], weight_latent)
+    hidden_pre, hidden_low, *h_two_parts = feed_forward(
+        normed_two_rows, middle, bias_up[None], weight_down
+    )
+    normed_two_all = jnp.concatenate(normed_two_rows, axis=0)
+    h_two_sum = collect(h_two_parts)
     latent_from_decode = collect(latent_cots)
     h_two = h_one + after(h_two_sum, latent_from_decode)
     h_two_low = h_two.astype(jnp.bfloat16)
@@ -1576,7 +1641,7 @@
         jnp.concatenate([pre_grad, latent.astype(jnp.bfloat16)], axis=1), slides
     )
     h_two_grad, down_input, pre_hidden_grad, up_bias_grad, *normed_two_parts = feed_back(
-        both_parts, weight_latent, weight_down, weight_up, hidden_pre
+        both_parts, weight_latent, weight_down, middle, hidden_pre
     )
     normed_two_grad = collect(normed_two_parts)
     latent_parts = [after(part, normed_two_parts[-1]) for part in both_parts]

time: 611 us -> 606 us (level)
  matrix products: 18 us -> 9.62 us
  Pallas kernels: 106 us -> 114 us
    ppermute x60, waiting for transfers between devices: 193 us -> 218 us  [swap(): lax.ppermute(pieces[k], 'slide', peers(k, count))]
    ppermute x1, waiting for transfers between devices: 22.4 us -> 0.01 us  [share_halves(): lax.ppermute(jnp.concatenate([upper, upper_x], axis=0), 'slide', peers(2,...]
    all_gather x3, waiting for transfers between devices: 16 us -> 2.74 us  [gather_blk(): return lax.all_gather(piece, 'blk', axis=axis, tiled=True)]
    pallas_call x0 -> x1, Pallas kernels: none -> 7.91 us  [feed_forward(): pl.pallas_call(functools.partial(feed_forward_kernel, count), grid=(units...]
    dot_general x2 -> x0, matrix products: 7.85 us -> none  [the longest x1 4.63 us: split_model(): jnp.dot(normed_two_all, weight_up, preferred_element_type=jnp.float32)]
    all_to_all x4, waiting for transfers between devices: 16.1 us -> 22.5 us  [to_heads(): lax.all_to_all(rows.reshape(blocks, cells, rows.shape[-1]), 'blk', 0, 0,...]
    unnamed x223 -> x255, local copies, waits for them, and re-layouts: 37.4 us -> 37.6 us
  transfers between devices with their start and end apart: 78 -> 78, of which waited for: 44 -> 44; matrix products, arithmetic and copies ran while one was open for 11% -> 9% of each run, Pallas kernels for 17% -> 19%
where the time goes in v6:
time: 606 us; the launch traced here: 596 us
  waiting for transfers between devices  274 us (45%)
  Pallas kernels  114 us (19%)
  starting transfers between devices  96 us (16%)
  local copies, waits for them, and re-layouts  67.6 us (11%)
  other arithmetic  18.3 us (3%)
  between operations  16.3 us (3%)
  matrix products  9.62 us (2%)
    ppermute x60, waiting for transfers between devices, swap(): lax.ppermute(pieces[k], 'slide', peers(k, count))  218 us
    ppermute x60, starting transfers between devices, swap(): lax.ppermute(pieces[k], 'slide', peers(k, count))  74.8 us
    unnamed x255, local copies, waits for them, and re-layouts  37.6 us
    ppermute x2, waiting for transfers between devices, to_chip(): lax.ppermute(rows, 'blk', [(place, place ^ 2 * offset) for place in range...  24.9 us
    all_to_all x4, waiting for transfers between devices, to_heads(): lax.all_to_all(rows.reshape(blocks, cells, rows.shape[-1]), 'blk', 0, 0,...  22.5 us
    all_to_all x4, starting transfers between devices, to_heads(): lax.all_to_all(rows.reshape(blocks, cells, rows.shape[-1]), 'blk', 0, 0,...  15.2 us
  transfers between devices with their start and end apart: 78, of which 44 were waited for; matrix products, arithmetic and copies ran while one was open for 9% of the time, Pallas kernels for 19%

profile of v6, /device:TPU:0, one launch (start us, length us, event | category | flops | bytes accessed | tf_op | source)
XLA Modules:
  0.0 595.8 jit_solution(13623014261610229082)
XLA Ops:
  18.2 6.6 %expression.1 = (bf16[3456,128]{1,0:T(8,128)(2,1)S(1)}, bf16[3456,128]{1,0:T(8,128)(2,1)}, bf16[3456,128]{1,0:T(8,128)(2,1)}, bf16[3456,128]{1,0:T(8,128)(2,1)}) custom-call(s32[1]{0:T(128)} %bitcast.me_ref, s32[1,128]{1,0:T(1,128)S(1)} %copy-done.55, s32[13500,1,128]{2,1,0:T(1,128)S(1)} %bitcast.133), custom_call_target="tpu_custom_call" | custom-call | tf_op jit(solution)/shard_map/expression/pallas_call | solution.py:478
  39.0 9.5 %collective-permute-done.refs_1_ = bf16[3456,128]{1,0:T(8,128)(2,1)S(1)} collective-permute-done((bf16[3456,128]{1,0:T(8,128)(2,1)}, bf16[3456,128]{1,0:T(8,128)(2,1)S(1)}, u32[]{:S(2)}, u32[]{:S(2)}) %collective-permute-start) | collective-permute-done | bytes 884768 | tf_op jit(solution)/shard_map/ppermute | solution.py:346
  48.5 19.7 %collective-permute-done.1.refs_2_ = bf16[3456,128]{1,0:T(8,128)(2,1)} collective-permute-done((bf16[3456,128]{1,0:T(8,128)(2,1)}, bf16[3456,128]{1,0:T(8,128)(2,1)}, u32[]{:S(2)}, u32[]{:S(2)}) %collective-permute-start.1) | collective-permute-done | bytes 884768 | tf_op jit(solution)/shard_map/ppermute | solution.py:346
  77.9 13.2 %collective-permute-done.3.refs_1_.refs_5_ = bf16[3456,128]{1,0:T(8,128)(2,1)} collective-permute-done((bf16[3456,128]{1,0:T(8,128)(2,1)}, bf16[3456,128]{1,0:T(8,128)(2,1)}, u32[]{:S(2)}, u32[]{:S(2)}) %collective-permute-start.3) | collective-permute-done | bytes 884768 | tf_op jit(solution)/shard_map/ppermute | solution.py:346
  91.1 17.8 %collective-permute-done.4.refs_2_.refs_6_ = bf16[3456,128]{1,0:T(8,128)(2,1)} collective-permute-done((bf16[3456,128]{1,0:T(8,128)(2,1)}, bf16[3456,128]{1,0:T(8,128)(2,1)}, u32[]{:S(2)}, u32[]{:S(2)}) %collective-permute-start.4) | collective-permute-done | bytes 884768 | tf_op jit(solution)/shard_map/ppermute | solution.py:346
  113.4 8.0 %embed_cells.1 = (f32[128,1024]{1,0:T(8,128)}, bf16[128,1024]{1,0:T(8,128)(2,1)}, bf16[128,1024]{1,0:T(8,128)(2,1)}, bf16[128,1024]{1,0:T(8,128)(2,1)}) custom-call(bf16[512,3456]{1,0:T(8,128)(2,1)} %copy-done.2, bf16[4752,1024]{1,0:T(8,128)(2,1)} %all-gather.5.cloned.1.call-done.table), custom_call_target="tpu_custom_call" | custom-call | tf_op jit(solution)/shard_map/embed_cells/pallas_call | solution.py:715
  129.8 6.0 %collective-permute-done.10 = bf16[128,1024]{1,0:T(8,128)(2,1)S(1)} collective-permute-done((bf16[128,1024]{1,0:T(8,128)(2,1)}, bf16[128,1024]{1,0:T(8,128)(2,1)S(1)}, u32[]{:S(2)}, u32[]{:S(2)}) %collective-permute-start.10) | collective-permute-done | bytes 262176 | tf_op jit(solution)/shard_map/ppermute | solution.py:346
  168.5 9.6 %collective-permute-done.16.refs_2_ = bf16[256,1024]{1,0:T(8,128)(2,1)S(1)} collective-permute-done((bf16[256,1024]{1,0:T(8,128)(2,1)S(1)}, bf16[256,1024]{1,0:T(8,128)(2,1)S(1)}, u32[]{:S(2)}, u32[]{:S(2)}) %collective-permute-start.16) | collective-permute-done | bytes 524320 | tf_op jit(solution)/shard_map/ppermute | solution.py:346
  208.3 10.3 %all-to-all-done.1 = bf16[8,128,128]{2,1,0:T(8,128)(2,1)} async-done(((bf16[8,128,128]{2,1,0:T(8,128)(2,1)}), bf16[8,128,128]{2,1,0:T(8,128)(2,1)}, u32[]{:S(2)}, u32[]{:S(2)}) %all-to-all-start.1) | async-done | bytes 262176 | tf_op jit(solution)/shard_map/all_to_all | solution.py:1579
  248.4 7.9 %feed_forward.1 = (f32[512,1024]{1,0:T(8,128)S(1)}, bf16[512,1024]{1,0:T(8,128)(2,1)S(1)}, f32[128,1024]{1,0:T(8,128)S(1)}, bf16[128,1024]{1,0:T(8,128)(2,1)S(1)...) custom-call(bf16[1024,2816]{1,0:T(8,128)(2,1)} %all-gather.7.cloned.1.call-done.up, ...), custom_call_target="tpu_custom_call" | custom-call | tf_op jit(solution)/shard_map/feed_forward/pallas_call | solution.py:828
  277.8 9.9 %collective-permute-done.30.refs_1_ = bf16[128,1536]{1,0:T(8,128)(2,1)S(1)} collective-permute-done((bf16[128,1536]{1,0:T(8,128)(2,1)S(1)}, bf16[128,1536]{1,0:T(8,128)(2,1)S(1)}, u32[]{:S(2)}, u32[]{:S(2)}) %collective-permute-start.30) | collective-permute-done | bytes 393248 | tf_op jit(solution)/shard_map/ppermute | solution.py:346
  294.0 9.6 %feed_back.1 = (f32[128,1024]{1,0:T(8,128)}, bf16[512,1024]{1,0:T(8,128)(2,1)}, bf16[512,1024]{1,0:T(8,128)(2,1)}, f32[1,1024]{1,0:T(1,128)}, f32[128,1024]{1,0:...) custom-call(bf16[1024,1024]{1,0:T(8,128)(2,1)} %order_rows.3.latent, ...), custom_call_target="tpu_custom_call" | custom-call | tf_op jit(solution)/shard_map/feed_back/pallas_call | solution.py:907
  315.7 5.8 decoder_products.1
  347.4 8.1 %all-to-all-done.2 = bf16[8,128,128]{2,1,0:T(8,128)(2,1)S(1)} async-done(((bf16[8,128,128]{2,1,0:T(8,128)(2,1)}), bf16[8,128,128]{2,1,0:T(8,128)(2,1)S(1)}, u32[]{:S(2)}, u32[]{:S(2)}) %all-to-all-start.2) | async-done | bytes 262176 | tf_op jit(solution)/shard_map/all_to_all | solution.py:1579
  355.5 10.8 %attend_back.1 = bf16[1024,384]{1,0:T(8,128)(2,1)} custom-call(bf16[1024,384]{1,0:T(8,128)(2,1)} %bitcast.23.rows_ref, bf16[1024,128]{1,0:T(8,128)(2,1)S(1)} %bitcast.136), custom_call_target="tpu_custom_call" | custom-call | tf_op jit(solution)/shard_map/attend_back/pallas_call | solution.py:1416
  382.3 15.7 %collective-permute-done.44.refs_7_ = bf16[128,256]{1,0:T(8,128)(2,1)S(1)} collective-permute-done((bf16[128,256]{1,0:T(8,128)(2,1)S(1)}, bf16[128,256]{1,0:T(8,128)(2,1)S(1)}, u32[]{:S(2)}, u32[]{:S(2)}) %collective-permute-start.44) | collective-permute-done | bytes 65568 | tf_op jit(solution)/shard_map/ppermute | solution.py:346
  419.1 6.4 %collective-permute-done.46 = bf16[128,1024]{1,0:T(8,128)(2,1)S(1)} collective-permute-done((bf16[128,1024]{1,0:T(8,128)(2,1)S(1)}, bf16[128,1024]{1,0:T(8,128)(2,1)S(1)}, u32[]{:S(2)}, u32[]{:S(2)}) %collective-permute-start.46) | collective-permute-done | bytes 262176 | tf_op jit(solution)/shard_map/ppermute | solution.py:346
  432.4 11.5 %collective-permute-done.49.other = bf16[256,1280]{1,0:T(8,128)(2,1)S(1)} collective-permute-done((bf16[256,1280]{1,0:T(8,128)(2,1)S(1)}, bf16[256,1280]{1,0:T(8,128)(2,1)S(1)}, u32[]{:S(2)}, u32[]{:S(2)}) %collective-permute-start.49) | collective-permute-done | bytes 655392 | tf_op jit(solution)/shard_map/ppermute | solution.py:416
  444.9 8.1 %embed_products.1 = bf16[8,3472,128]{2,1,0:T(8,128)(2,1)} custom-call(bf16[3456,128]{1,0:T(8,128)(2,1)} %copy-done.16, bf16[3456,128]{1,0:T(8,128)(2,1)} %copy-done.17, bf16[3456,128]{1,0:T(8,128)(2,1)} %collective-permute-done.1.refs_2_, bf16[3456,128]{1,0:T(8,128)(2,1)} %collective-permute-done.2.refs_3_, bf16[128,1024]{1,0:T(8,128)(2,1)} %copy-done.68, ...), custom_call_target="tpu_custom_call" | custom-call | tf_op jit(solution)/shard_map/embed_products/pallas_call | solution.py:1235
  457.7 8.1 %cells_to_genes.1 = (bf16[3456,128]{1,0:T(8,128)(2,1)}, bf16[3456,128]{1,0:T(8,128)(2,1)}, bf16[3456,128]{1,0:T(8,128)(2,1)}, bf16[3456,128]{1,0:T(8,128)(2,1)}) custom-call(bf16[4752,1024]{1,0:T(8,128)(2,1)} %all-gather.5.cloned.1.call-done.table, bf16[128,1024]{1,0:T(8,128)(2,1)} %copy-done.68, bf16[128,1024]{1,0:T(8,128)(2,1)} %collective-permute-done.50.refs_5_.refs_1_, ...), custom_call_target="tpu_custom_call" | custom-call | tf_op jit(solution)/shard_map/cells_to_genes/pallas_call | solution.py:1173
  473.7 13.4 %collective-permute-done.58 = bf16[128,1280]{1,0:T(8,128)(2,1)S(1)} collective-permute-done((bf16[128,1280]{1,0:T(8,128)(2,1)S(1)}, bf16[128,1280]{1,0:T(8,128)(2,1)S(1)}, u32[]{:S(2)}, u32[]{:S(2)}) %collective-permute-start.58) | collective-permute-done | bytes 327712 | tf_op jit(solution)/shard_map/ppermute | solution.py:416
  495.0 37.9 %collective-permute-done.57.rest_3_ = bf16[3456,128]{1,0:T(8,128)(2,1)S(1)} collective-permute-done((bf16[3456,128]{1,0:T(8,128)(2,1)}, bf16[3456,128]{1,0:T(8,128)(2,1)S(1)}, u32[]{:S(2)}, u32[]{:S(2)}) %collective-permute-start.57) | collective-permute-done | bytes 884768 | tf_op jit(solution)/shard_map/ppermute | solution.py:346
  560.2 6.9 %assemble.1 = (f32[512,1024]{1,0:T(8,128)}, f32[128,4096]{1,0:T(8,128)}, f32[128,3072]{1,0:T(8,128)}, f32[128,1024]{1,0:T(8,128)}, f32[128,1024]{1,0:T(8,128)}, /*index=5*/f32[64,13500]{1,0:T(8,128)}) custom-call(s32[1]{0:T(128)} %bitcast.me_ref, bf16[128,3840]{1,0:T(8,128)(2,1)S(1)} %fusion.10.refs_0_, ...), custom_call_target="tpu_custom_call" | custom-call | tf_op jit(solution)/shard_map/assemble/pallas_call | solution.py:1139
  567.8 16.6 %collective-permute-done.65.refs_2_ = bf16[3472,128]{1,0:T(8,128)(2,1)S(1)} collective-permute-done((bf16[3472,128]{1,0:T(8,128)(2,1)}, bf16[3472,128]{1,0:T(8,128)(2,1)S(1)}, u32[]{:S(2)}, u32[]{:S(2)}) %collective-permute-start.65) | collective-permute-done | bytes 888864 | tf_op jit(solution)/shard_map/ppermute | solution.py:346
  (527 shorter events, 302.3 us)
Async XLA Ops:
  7.2 104.5 %all-gather.5.cloned.1.call-start = ((), (), s32[]{:S(2)}) async-start(), calls=%async_computation.7 | async-start | bytes 10948608 | tf_op jit(solution)/shard_map/all_gather | solution.py:402
  15.2 167.3 %all-gather.7.cloned.1.call-start = ((), (), s32[]{:S(2)}) async-start(), calls=%async_computation.8 | async-start | bytes 6488064 | tf_op jit(solution)/shard_map/all_gather | solution.py:402
  27.8 40.4 %collective-permute-start.1 = (bf16[3456,128]{1,0:T(8,128)(2,1)}, bf16[3456,128]{1,0:T(8,128)(2,1)}, u32[]{:S(2)}, u32[]{:S(2)}) collective-permute-start(bf16[3456,128]{1,0:T(8,128)(2,1)} %get-tuple-element.114), channel_id=1, source_target_pairs={{0,16},{8,24},{16,0},{24,8},{1,17},{9,25},{17,1},{25,9},{2,18},{10... | collective-permute-start | bytes 2654216 | tf_op jit(solution)/shard_map/ppermute | solution.py:346
  29.3 38.9 %collective-permute-start.2 = (bf16[3456,128]{1,0:T(8,128)(2,1)}, bf16[3456,128]{1,0:T(8,128)(2,1)}, u32[]{:S(2)}, u32[]{:S(2)}) collective-permute-start(bf16[3456,128]{1,0:T(8,128)(2,1)} %get-tuple-element.115), channel_id=1, source_target_pairs={{0,24},{8,16},{16,8},{24,0},{1,25},{9,17},{17,9},{25,1},{2,26},{10... | collective-permute-start | bytes 2654216 | tf_op jit(solution)/shard_map/ppermute | solution.py:346
  69.4 39.5 %collective-permute-start.4 = (bf16[3456,128]{1,0:T(8,128)(2,1)}, bf16[3456,128]{1,0:T(8,128)(2,1)}, u32[]{:S(2)}, u32[]{:S(2)}) collective-permute-start(bf16[3456,128]{1,0:T(8,128)(2,1)} %get-tuple-element.117), channel_id=1, source_target_pairs={{0,16},{8,24},{16,0},{24,8},{1,17},{9,25},{17,1},{25,9},{2,18},{10... | collective-permute-start | bytes 2654216 | tf_op jit(solution)/shard_map/ppermute | solution.py:346
  70.3 38.7 %collective-permute-start.5 = (bf16[3456,128]{1,0:T(8,128)(2,1)}, bf16[3456,128]{1,0:T(8,128)(2,1)}, u32[]{:S(2)}, u32[]{:S(2)}) collective-permute-start(bf16[3456,128]{1,0:T(8,128)(2,1)} %get-tuple-element.118), channel_id=1, source_target_pairs={{0,24},{8,16},{16,8},{24,0},{1,25},{9,17},{17,9},{25,1},{2,26},{10... | collective-permute-start | bytes 2654216 | tf_op jit(solution)/shard_map/ppermute | solution.py:346
  159.3 35.9 %all-to-all-start = ((bf16[8,128,384]{2,1,0:T(8,128)(2,1)}), bf16[8,128,384]{2,1,0:T(8,128)(2,1)}, u32[]{:S(2)}, u32[]{:S(2)}) async-start(bf16[8,128,384]{2,1,0:T(8,128)(2,1)} %bitcast.22), calls=%async_computation | async-start | bytes 1572864 | tf_op jit(solution)/shard_map/all_to_all | solution.py:1579
  163.5 83.9 %all-gather.9.cloned.1.call-start = ((), (), s32[]{:S(2)}) async-start(), calls=%async_computation.9 | async-start | bytes 2359296 | tf_op jit(solution)/shard_map/all_gather | solution.py:402
  208.2 114.5 %all-gather.11.cloned.1.call-start = ((), (), s32[]{:S(2)}) async-start(), calls=%async_computation.10 | async-start | bytes 2621440 | tf_op jit(solution)/shard_map/all_gather | solution.py:1618
  235.5 25.4 %collective-permute-start.8 = (bf16[128,512]{1,0:T(8,128)(2,1)}, bf16[128,512]{1,0:T(8,128)(2,1)}, u32[]{:S(2)}, u32[]{:S(2)}) collective-permute-start(bf16[128,512]{1,0:T(8,128)(2,1)} %get-tuple-element.124), channel_id=1, source_target_pairs={{0,24},{8,16},{16,8},{24,0},{1,25},{9,17},{17,9},{25,1},{2,26},{10... | collective-permute-start | bytes 393224 | tf_op jit(solution)/shard_map/ppermute | solution.py:346
  236.0 24.0 %collective-permute-start.6 = (bf16[128,512]{1,0:T(8,128)(2,1)}, bf16[128,512]{1,0:T(8,128)(2,1)}, u32[]{:S(2)}, u32[]{:S(2)}) collective-permute-start(bf16[128,512]{1,0:T(8,128)(2,1)} %get-tuple-element.122), channel_id=1, source_target_pairs={{0,8},{8,0},{16,24},{24,16},{1,9},{9,1},{17,25},{25,17},{2,10},{10... | collective-permute-start | bytes 393224 | tf_op jit(solution)/shard_map/ppermute | solution.py:346
  270.3 98.7 %reduce-scatter.4.cloned.1.call-start = ((), (), s32[]{:S(2)}) async-start(), calls=%async_computation.11 | async-start | bytes 3981312 | tf_op jit(solution)/shard_map/reduce_scatter | solution.py:406
  341.3 111.8 %reduce-scatter.6.cloned.1.call-start = ((), (), s32[]{:S(2)}) async-start(), calls=%async_computation.12 | async-start | bytes 4718592 | tf_op jit(solution)/shard_map/reduce_scatter | solution.py:406
  369.0 34.0 %all-to-all-start.3 = ((bf16[8,128,384]{2,1,0:T(8,128)(2,1)}), bf16[8,128,384]{2,1,0:T(8,128)(2,1)S(1)}, u32[]{:S(2)}, u32[]{:S(2)}) async-start(bf16[8,128,384]{2,1,0:T(8,128)(2,1)} %bitcast.51), calls=%async_computation.3 | async-start | bytes 1572864 | tf_op jit(solution)/shard_map/all_to_all | solution.py:1579
  372.6 172.3 %reduce-scatter.8.cloned.1.call-start = ((), (), s32[]{:S(2)}) async-start(), calls=%async_computation.13 | async-start | bytes 7999488 | tf_op jit(solution)/shard_map/reduce_scatter | solution.py:406
  372.9 26.0 %collective-permute-start.41 = (bf16[3456,128]{1,0:T(8,128)(2,1)}, bf16[3456,128]{1,0:T(8,128)(2,1)S(1)}, u32[]{:S(2)}, u32[]{:S(2)}) collective-permute-start(bf16[3456,128]{1,0:T(8,128)(2,1)} %get-tuple-element.166), channel_id=1, source_target_pairs={{0,24},{8,16},{16,8},{24,0},{1,25},{9,17},{17,9},{25,1},{2,26},{10... | collective-permute-start | bytes 2654216 | tf_op jit(solution)/shard_map/ppermute | solution.py:346
  457.5 29.7 %collective-permute-start.58 = (bf16[128,1280]{1,0:T(8,128)(2,1)S(1)}, bf16[128,1280]{1,0:T(8,128)(2,1)S(1)}, u32[]{:S(2)}, u32[]{:S(2)}) collective-permute-start(bf16[128,1280]{1,0:T(8,128)(2,1)S(1)} %get-tuple-element.179), channel_id=1, source_target_pairs={{0,4},{1,5},{2,6},{3,7},{4,0},{5,1},{6,2},{7,3},{8,12},{9,13},{10,... | collective-permute-start | bytes 983048 | tf_op jit(solution)/shard_map/ppermute | solution.py:416
  470.8 64.6 %collective-permute-start.63 = (bf16[128,3840]{1,0:T(8,128)(2,1)S(1)}, bf16[128,3840]{1,0:T(8,128)(2,1)S(1)}, u32[]{:S(2)}, u32[]{:S(2)}) collective-permute-start(bf16[128,3840]{1,0:T(8,128)(2,1)S(1)} %pad_maximum_fusion.5), channel_id=1, source_target_pairs={{0,8},{8,0},{16,24},{24,16},{1,9},{9,1},{17,25},{25,17},{2,10},{10... | collective-permute-start | bytes 2949128 | tf_op jit(solution)/shard_map/ppermute | solution.py:356
  471.2 61.6 %collective-permute-start.57 = (bf16[3456,128]{1,0:T(8,128)(2,1)}, bf16[3456,128]{1,0:T(8,128)(2,1)S(1)}, u32[]{:S(2)}, u32[]{:S(2)}) collective-permute-start(bf16[3456,128]{1,0:T(8,128)(2,1)} %get-tuple-element.196), channel_id=1, source_target_pairs={{0,24},{8,16},{16,8},{24,0},{1,25},{9,17},{17,9},{25,1},{2,26},{10... | collective-permute-start | bytes 2654216 | tf_op jit(solution)/shard_map/ppermute | solution.py:346
  487.1 49.3 %collective-permute-start.62 = (bf16[128,3840]{1,0:T(8,128)(2,1)S(1)}, bf16[128,3840]{1,0:T(8,128)(2,1)S(1)}, u32[]{:S(2)}, u32[]{:S(2)}) collective-permute-start(bf16[128,3840]{1,0:T(8,128)(2,1)S(1)} %pad_maximum_fusion.4), channel_id=1, source_target_pairs={{0,16},{8,24},{16,0},{24,8},{1,17},{9,25},{17,1},{25,9},{2,18},{10... | collective-permute-start | bytes 2949128 | tf_op jit(solution)/shard_map/ppermute | solution.py:355
  492.0 47.0 %collective-permute-start.59 = (bf16[128,1280]{1,0:T(8,128)(2,1)S(1)}, bf16[128,1280]{1,0:T(8,128)(2,1)S(1)}, u32[]{:S(2)}, u32[]{:S(2)}) collective-permute-start(bf16[128,1280]{1,0:T(8,128)(2,1)S(1)} %add_convert_fusion.refs_5_), channel_id=1, source_target_pairs={{0,8},{8,0},{16,24},{24,16},{1,9},{9,1},{17,25},{25,17},{2,10},{10... | collective-permute-start | bytes 983048 | tf_op jit(solution)/shard_map/ppermute | solution.py:346
  493.7 46.0 %collective-permute-start.60 = (bf16[128,1280]{1,0:T(8,128)(2,1)S(1)}, bf16[128,1280]{1,0:T(8,128)(2,1)S(1)}, u32[]{:S(2)}, u32[]{:S(2)}) collective-permute-start(bf16[128,1280]{1,0:T(8,128)(2,1)S(1)} %add_convert_fusion.refs_5_), channel_id=1, source_target_pairs={{0,16},{8,24},{16,0},{24,8},{1,17},{9,25},{17,1},{25,9},{2,18},{10... | collective-permute-start | bytes 983048 | tf_op jit(solution)/shard_map/ppermute | solution.py:346
  546.4 38.0 %collective-permute-start.65 = (bf16[3472,128]{1,0:T(8,128)(2,1)}, bf16[3472,128]{1,0:T(8,128)(2,1)S(1)}, u32[]{:S(2)}, u32[]{:S(2)}) collective-permute-start(bf16[3472,128]{1,0:T(8,128)(2,1)} %bitcast.139), channel_id=1, source_target_pairs={{0,16},{8,24},{16,0},{24,8},{1,17},{9,25},{17,1},{25,9},{2,18},{10... | collective-permute-start | bytes 2666504 | tf_op jit(solution)/shard_map/ppermute | solution.py:346
  547.3 37.1 %collective-permute-start.66 = (bf16[3472,128]{1,0:T(8,128)(2,1)}, bf16[3472,128]{1,0:T(8,128)(2,1)S(1)}, u32[]{:S(2)}, u32[]{:S(2)}) collective-permute-start(bf16[3472,128]{1,0:T(8,128)(2,1)} %bitcast.140), channel_id=1, source_target_pairs={{0,24},{8,16},{16,8},{24,0},{1,25},{9,17},{17,9},{25,1},{2,26},{10... | collective-permute-start | bytes 2666504 | tf_op jit(solution)/shard_map/ppermute | solution.py:346
  (172 other events, 1783.2 us)
Sparse Core Ops, SparseCore 0:
  15.3 96.2 all-gather.4
  113.9 61.5 all-gather.6
  187.6 26.2 all-gather.8
  270.4 41.1 all-gather.10
  322.9 46.0 reduce-scatter.3
  371.8 58.9 reduce-scatter.5
  453.2 81.0 reduce-scatter.7

commit v7 on v6

--- a/solution.py
+++ b/solution.py
@@ -488,7 +488,7 @@
             pltpu.VMEM((count, quarter, cells), jnp.int32),
             pltpu.SemaphoreType.DMA((count,)),
         ],
-        compiler_params=pltpu.CompilerParams(vmem_limit_bytes=40 * 2**20),
+        compiler_params=pltpu.CompilerParams(vmem_limit_bytes=58 * 2**20),
         cost_estimate=COST,
         name="expression",
     )(me.reshape(1), library, jnp.transpose(counts, (2, 0, 1)))
@@ -785,7 +785,7 @@
     return 0.5 * (1.0 + bent) + 0.5 * rows * (1.0 - bent * bent) * inner
 
 
-UNITS = 256
+UNITS = 1024
 
 
 def feed_forward_kernel(count, up, bias, down, *refs):

time: 606 us -> 603 us (level)
  transfers between devices with their start and end apart: 78 -> 78, of which waited for: 44 -> 43; matrix products, arithmetic and copies ran while one was open for 9% -> 9% of each run, Pallas kernels for 19% -> 18%
where the time goes in v7:
time: 603 us; the launch traced here: 593 us
  waiting for transfers between devices  273 us (45%)
  Pallas kernels  112 us (19%)
  starting transfers between devices  95.6 us (16%)
  local copies, waits for them, and re-layouts  68 us (11%)
  other arithmetic  18.3 us (3%)
  between operations  16.3 us (3%)
  matrix products  9.62 us (2%)
    ppermute x60, waiting for transfers between devices, swap(): lax.ppermute(pieces[k], 'slide', peers(k, count))  215 us
    ppermute x60, starting transfers between devices, swap(): lax.ppermute(pieces[k], 'slide', peers(k, count))  74.4 us
    unnamed x255, local copies, waits for them, and re-layouts  37.9 us
    ppermute x2, waiting for transfers between devices, to_chip(): lax.ppermute(rows, 'blk', [(place, place ^ 2 * offset) for place in range...  25 us
    all_to_all x4, waiting for transfers between devices, to_heads(): lax.all_to_all(rows.reshape(blocks, cells, rows.shape[-1]), 'blk', 0, 0,...  22.5 us
    all_to_all x4, starting transfers between devices, to_heads(): lax.all_to_all(rows.reshape(blocks, cells, rows.shape[-1]), 'blk', 0, 0,...  15.2 us
  transfers between devices with their start and end apart: 78, of which 43 were waited for; matrix products, arithmetic and copies ran while one was open for 9% of the time, Pallas kernels for 18%

profile of v7, /device:TPU:0, one launch (start us, length us, event | category | flops | bytes accessed | tf_op | source)
XLA Modules:
  0.0 592.6 jit_solution(11430179208611250956)
XLA Ops:
  15.3 7.8 %expression.1 = (bf16[3456,128]{1,0:T(8,128)(2,1)}, bf16[3456,128]{1,0:T(8,128)(2,1)}, bf16[3456,128]{1,0:T(8,128)(2,1)}, bf16[3456,128]{1,0:T(8,128)(2,1)}) custom-call(s32[1]{0:T(128)} %bitcast.me_ref, s32[1,128]{1,0:T(1,128)} %library_ref.1, s32[13500,1,128]{2,1,0:T(1,128)} %bitcast.144), custom_call_target="tpu_custom_call" | custom-call | tf_op jit(solution)/shard_map/expression/pallas_call | solution.py:478
  37.3 9.4 %collective-permute-done.refs_1_ = bf16[3456,128]{1,0:T(8,128)(2,1)S(1)} collective-permute-done((bf16[3456,128]{1,0:T(8,128)(2,1)}, bf16[3456,128]{1,0:T(8,128)(2,1)S(1)}, u32[]{:S(2)}, u32[]{:S(2)}) %collective-permute-start) | collective-permute-done | bytes 884768 | tf_op jit(solution)/shard_map/ppermute | solution.py:346
  46.8 19.6 %collective-permute-done.1.refs_2_ = bf16[3456,128]{1,0:T(8,128)(2,1)S(1)} collective-permute-done((bf16[3456,128]{1,0:T(8,128)(2,1)}, bf16[3456,128]{1,0:T(8,128)(2,1)S(1)}, u32[]{:S(2)}, u32[]{:S(2)}) %collective-permute-start.1) | collective-permute-done | bytes 884768 | tf_op jit(solution)/shard_map/ppermute | solution.py:346
  78.8 11.4 %collective-permute-done.3.refs_1_.refs_5_ = bf16[3456,128]{1,0:T(8,128)(2,1)} collective-permute-done((bf16[3456,128]{1,0:T(8,128)(2,1)}, bf16[3456,128]{1,0:T(8,128)(2,1)}, u32[]{:S(2)}, u32[]{:S(2)}) %collective-permute-start.3) | collective-permute-done | bytes 884768 | tf_op jit(solution)/shard_map/ppermute | solution.py:346
  90.2 17.0 %collective-permute-done.4.refs_2_.refs_6_ = bf16[3456,128]{1,0:T(8,128)(2,1)} collective-permute-done((bf16[3456,128]{1,0:T(8,128)(2,1)}, bf16[3456,128]{1,0:T(8,128)(2,1)}, u32[]{:S(2)}, u32[]{:S(2)}) %collective-permute-start.4) | collective-permute-done | bytes 884768 | tf_op jit(solution)/shard_map/ppermute | solution.py:346
  113.4 8.0 %embed_cells.1 = (f32[128,1024]{1,0:T(8,128)}, bf16[128,1024]{1,0:T(8,128)(2,1)}, bf16[128,1024]{1,0:T(8,128)(2,1)}, bf16[128,1024]{1,0:T(8,128)(2,1)}) custom-call(bf16[512,3456]{1,0:T(8,128)(2,1)} %copy-done.2, bf16[4752,1024]{1,0:T(8,128)(2,1)} %all-gather.5.cloned.1.call-done.table), custom_call_target="tpu_custom_call" | custom-call | tf_op jit(solution)/shard_map/embed_cells/pallas_call | solution.py:715
  129.8 6.0 %collective-permute-done.10 = bf16[128,1024]{1,0:T(8,128)(2,1)S(1)} collective-permute-done((bf16[128,1024]{1,0:T(8,128)(2,1)}, bf16[128,1024]{1,0:T(8,128)(2,1)S(1)}, u32[]{:S(2)}, u32[]{:S(2)}) %collective-permute-start.10) | collective-permute-done | bytes 262176 | tf_op jit(solution)/shard_map/ppermute | solution.py:346
  168.5 9.5 %collective-permute-done.16.refs_2_ = bf16[256,1024]{1,0:T(8,128)(2,1)S(1)} collective-permute-done((bf16[256,1024]{1,0:T(8,128)(2,1)S(1)}, bf16[256,1024]{1,0:T(8,128)(2,1)S(1)}, u32[]{:S(2)}, u32[]{:S(2)}) %collective-permute-start.16) | collective-permute-done | bytes 524320 | tf_op jit(solution)/shard_map/ppermute | solution.py:346
  208.3 10.3 %all-to-all-done.1 = bf16[8,128,128]{2,1,0:T(8,128)(2,1)} async-done(((bf16[8,128,128]{2,1,0:T(8,128)(2,1)}), bf16[8,128,128]{2,1,0:T(8,128)(2,1)}, u32[]{:S(2)}, u32[]{:S(2)}) %all-to-all-start.1) | async-done | bytes 262176 | tf_op jit(solution)/shard_map/all_to_all | solution.py:1579
  274.7 9.9 %collective-permute-done.30.refs_1_ = bf16[128,1536]{1,0:T(8,128)(2,1)S(1)} collective-permute-done((bf16[128,1536]{1,0:T(8,128)(2,1)S(1)}, bf16[128,1536]{1,0:T(8,128)(2,1)S(1)}, u32[]{:S(2)}, u32[]{:S(2)}) %collective-permute-start.30) | collective-permute-done | bytes 393248 | tf_op jit(solution)/shard_map/ppermute | solution.py:346
  290.8 9.6 %feed_back.1 = (f32[128,1024]{1,0:T(8,128)}, bf16[512,1024]{1,0:T(8,128)(2,1)}, bf16[512,1024]{1,0:T(8,128)(2,1)}, f32[1,1024]{1,0:T(1,128)}, f32[128,1024]{1,0:...) custom-call(bf16[1024,1024]{1,0:T(8,128)(2,1)} %order_rows.3.latent, ...), custom_call_target="tpu_custom_call" | custom-call | tf_op jit(solution)/shard_map/feed_back/pallas_call | solution.py:907
  312.5 5.8 decoder_products.1
  344.3 8.1 %all-to-all-done.2 = bf16[8,128,128]{2,1,0:T(8,128)(2,1)S(1)} async-done(((bf16[8,128,128]{2,1,0:T(8,128)(2,1)}), bf16[8,128,128]{2,1,0:T(8,128)(2,1)S(1)}, u32[]{:S(2)}, u32[]{:S(2)}) %all-to-all-start.2) | async-done | bytes 262176 | tf_op jit(solution)/shard_map/all_to_all | solution.py:1579
  352.3 10.8 %attend_back.1 = bf16[1024,384]{1,0:T(8,128)(2,1)} custom-call(bf16[1024,384]{1,0:T(8,128)(2,1)} %bitcast.23.rows_ref, bf16[1024,128]{1,0:T(8,128)(2,1)S(1)} %bitcast.135), custom_call_target="tpu_custom_call" | custom-call | tf_op jit(solution)/shard_map/attend_back/pallas_call | solution.py:1416
  379.2 15.7 %collective-permute-done.44.refs_7_ = bf16[128,256]{1,0:T(8,128)(2,1)S(1)} collective-permute-done((bf16[128,256]{1,0:T(8,128)(2,1)S(1)}, bf16[128,256]{1,0:T(8,128)(2,1)S(1)}, u32[]{:S(2)}, u32[]{:S(2)}) %collective-permute-start.44) | collective-permute-done | bytes 65568 | tf_op jit(solution)/shard_map/ppermute | solution.py:346
  410.5 5.5 collective-permute-done.45
  416.0 6.3 %collective-permute-done.46 = bf16[128,1024]{1,0:T(8,128)(2,1)S(1)} collective-permute-done((bf16[128,1024]{1,0:T(8,128)(2,1)S(1)}, bf16[128,1024]{1,0:T(8,128)(2,1)S(1)}, u32[]{:S(2)}, u32[]{:S(2)}) %collective-permute-start.46) | collective-permute-done | bytes 262176 | tf_op jit(solution)/shard_map/ppermute | solution.py:346
  429.2 11.6 %collective-permute-done.49.other = bf16[256,1280]{1,0:T(8,128)(2,1)S(1)} collective-permute-done((bf16[256,1280]{1,0:T(8,128)(2,1)S(1)}, bf16[256,1280]{1,0:T(8,128)(2,1)S(1)}, u32[]{:S(2)}, u32[]{:S(2)}) %collective-permute-start.49) | collective-permute-done | bytes 655392 | tf_op jit(solution)/shard_map/ppermute | solution.py:416
  441.8 8.1 %embed_products.1 = bf16[8,3472,128]{2,1,0:T(8,128)(2,1)} custom-call(bf16[3456,128]{1,0:T(8,128)(2,1)} %get-tuple-element.112.refs_0_, bf16[3456,128]{1,0:T(8,128)(2,1)} %copy-done.16, bf16[3456,128]{1,0:T(8,128)(2,1)} %copy-done.17, bf16[3456,128]{1,0:T(8,128)(2,1)} %collective-permute-done.2.refs_3_, bf16[128,1024]{1,0:T(8,128)(2,1)} %copy-done.68, ...), custom_call_target="tpu_custom_call" | custom-call | tf_op jit(solution)/shard_map/embed_products/pallas_call | solution.py:1235
  454.5 8.1 %cells_to_genes.1 = (bf16[3456,128]{1,0:T(8,128)(2,1)}, bf16[3456,128]{1,0:T(8,128)(2,1)}, bf16[3456,128]{1,0:T(8,128)(2,1)}, bf16[3456,128]{1,0:T(8,128)(2,1)}) custom-call(bf16[4752,1024]{1,0:T(8,128)(2,1)} %all-gather.5.cloned.1.call-done.table, bf16[128,1024]{1,0:T(8,128)(2,1)} %copy-done.68, bf16[128,1024]{1,0:T(8,128)(2,1)} %collective-permute-done.50.refs_5_.refs_1_, ...), custom_call_target="tpu_custom_call" | custom-call | tf_op jit(solution)/shard_map/cells_to_genes/pallas_call | solution.py:1173
  470.6 13.4 %collective-permute-done.58 = bf16[128,1280]{1,0:T(8,128)(2,1)S(1)} collective-permute-done((bf16[128,1280]{1,0:T(8,128)(2,1)S(1)}, bf16[128,1280]{1,0:T(8,128)(2,1)S(1)}, u32[]{:S(2)}, u32[]{:S(2)}) %collective-permute-start.58) | collective-permute-done | bytes 327712 | tf_op jit(solution)/shard_map/ppermute | solution.py:416
  491.8 37.9 %collective-permute-done.57.rest_3_ = bf16[3456,128]{1,0:T(8,128)(2,1)S(1)} collective-permute-done((bf16[3456,128]{1,0:T(8,128)(2,1)}, bf16[3456,128]{1,0:T(8,128)(2,1)S(1)}, u32[]{:S(2)}, u32[]{:S(2)}) %collective-permute-start.57) | collective-permute-done | bytes 884768 | tf_op jit(solution)/shard_map/ppermute | solution.py:346
  557.1 6.9 %assemble.1 = (f32[512,1024]{1,0:T(8,128)}, f32[128,4096]{1,0:T(8,128)}, f32[128,3072]{1,0:T(8,128)}, f32[128,1024]{1,0:T(8,128)}, f32[128,1024]{1,0:T(8,128)}, /*index=5*/f32[64,13500]{1,0:T(8,128)}) custom-call(s32[1]{0:T(128)} %bitcast.me_ref, bf16[128,3840]{1,0:T(8,128)(2,1)S(1)} %fusion.10.refs_0_, ...), custom_call_target="tpu_custom_call" | custom-call | tf_op jit(solution)/shard_map/assemble/pallas_call | solution.py:1139
  564.7 16.6 %collective-permute-done.65.refs_2_ = bf16[3472,128]{1,0:T(8,128)(2,1)S(1)} collective-permute-done((bf16[3472,128]{1,0:T(8,128)(2,1)}, bf16[3472,128]{1,0:T(8,128)(2,1)S(1)}, u32[]{:S(2)}, u32[]{:S(2)}) %collective-permute-start.65) | collective-permute-done | bytes 888864 | tf_op jit(solution)/shard_map/ppermute | solution.py:346
  (527 shorter events, 303.2 us)
Async XLA Ops:
  7.2 104.4 %all-gather.5.cloned.1.call-start = ((), (), s32[]{:S(2)}) async-start(), calls=%async_computation.7 | async-start | bytes 10948608 | tf_op jit(solution)/shard_map/all_gather | solution.py:402
  15.2 167.3 %all-gather.7.cloned.1.call-start = ((), (), s32[]{:S(2)}) async-start(), calls=%async_computation.8 | async-start | bytes 6488064 | tf_op jit(solution)/shard_map/all_gather | solution.py:402
  23.1 23.7 %collective-permute-start = (bf16[3456,128]{1,0:T(8,128)(2,1)}, bf16[3456,128]{1,0:T(8,128)(2,1)S(1)}, u32[]{:S(2)}, u32[]{:S(2)}) collective-permute-start(bf16[3456,128]{1,0:T(8,128)(2,1)} %get-tuple-element.113), channel_id=1, source_target_pairs={{0,8},{8,0},{16,24},{24,16},{1,9},{9,1},{17,25},{25,17},{2,10},{10... | collective-permute-start | bytes 2654216 | tf_op jit(solution)/shard_map/ppermute | solution.py:346
  26.1 40.3 %collective-permute-start.1 = (bf16[3456,128]{1,0:T(8,128)(2,1)}, bf16[3456,128]{1,0:T(8,128)(2,1)S(1)}, u32[]{:S(2)}, u32[]{:S(2)}) collective-permute-start(bf16[3456,128]{1,0:T(8,128)(2,1)} %get-tuple-element.114), channel_id=1, source_target_pairs={{0,16},{8,24},{16,0},{24,8},{1,17},{9,25},{17,1},{25,9},{2,18},{10... | collective-permute-start | bytes 2654216 | tf_op jit(solution)/shard_map/ppermute | solution.py:346
  27.6 39.7 %collective-permute-start.2 = (bf16[3456,128]{1,0:T(8,128)(2,1)}, bf16[3456,128]{1,0:T(8,128)(2,1)}, u32[]{:S(2)}, u32[]{:S(2)}) collective-permute-start(bf16[3456,128]{1,0:T(8,128)(2,1)} %get-tuple-element.115), channel_id=1, source_target_pairs={{0,24},{8,16},{16,8},{24,0},{1,25},{9,17},{17,9},{25,1},{2,26},{10... | collective-permute-start | bytes 2654216 | tf_op jit(solution)/shard_map/ppermute | solution.py:346
  67.7 39.5 %collective-permute-start.4 = (bf16[3456,128]{1,0:T(8,128)(2,1)}, bf16[3456,128]{1,0:T(8,128)(2,1)}, u32[]{:S(2)}, u32[]{:S(2)}) collective-permute-start(bf16[3456,128]{1,0:T(8,128)(2,1)} %get-tuple-element.117), channel_id=1, source_target_pairs={{0,16},{8,24},{16,0},{24,8},{1,17},{9,25},{17,1},{25,9},{2,18},{10... | collective-permute-start | bytes 2654216 | tf_op jit(solution)/shard_map/ppermute | solution.py:346
  69.3 37.9 %collective-permute-start.5 = (bf16[3456,128]{1,0:T(8,128)(2,1)}, bf16[3456,128]{1,0:T(8,128)(2,1)}, u32[]{:S(2)}, u32[]{:S(2)}) collective-permute-start(bf16[3456,128]{1,0:T(8,128)(2,1)} %get-tuple-element.118), channel_id=1, source_target_pairs={{0,24},{8,16},{16,8},{24,0},{1,25},{9,17},{17,9},{25,1},{2,26},{10... | collective-permute-start | bytes 2654216 | tf_op jit(solution)/shard_map/ppermute | solution.py:346
  159.3 35.9 %all-to-all-start = ((bf16[8,128,384]{2,1,0:T(8,128)(2,1)}), bf16[8,128,384]{2,1,0:T(8,128)(2,1)}, u32[]{:S(2)}, u32[]{:S(2)}) async-start(bf16[8,128,384]{2,1,0:T(8,128)(2,1)} %bitcast.22), calls=%async_computation | async-start | bytes 1572864 | tf_op jit(solution)/shard_map/all_to_all | solution.py:1579
  163.5 83.9 %all-gather.9.cloned.1.call-start = ((), (), s32[]{:S(2)}) async-start(), calls=%async_computation.9 | async-start | bytes 2359296 | tf_op jit(solution)/shard_map/all_gather | solution.py:402
  195.2 23.4 %collective-permute-start.18 = (bf16[256,1024]{1,0:T(8,128)(2,1)}, bf16[256,1024]{1,0:T(8,128)(2,1)}, u32[]{:S(2)}, u32[]{:S(2)}) collective-permute-start(bf16[256,1024]{1,0:T(8,128)(2,1)} %get-tuple-element.132.refs_0_), channel_id=1, source_target_pairs={{0,8},{8,0},{16,24},{24,16},{1,9},{9,1},{17,25},{25,17},{2,10},{10... | collective-permute-start | bytes 1572872 | tf_op jit(solution)/shard_map/ppermute | solution.py:346
  208.2 111.4 %all-gather.11.cloned.1.call-start = ((), (), s32[]{:S(2)}) async-start(), calls=%async_computation.10 | async-start | bytes 2621440 | tf_op jit(solution)/shard_map/all_gather | solution.py:1618
  267.2 98.7 %reduce-scatter.4.cloned.1.call-start = ((), (), s32[]{:S(2)}) async-start(), calls=%async_computation.11 | async-start | bytes 3981312 | tf_op jit(solution)/shard_map/reduce_scatter | solution.py:406
  338.1 111.8 %reduce-scatter.6.cloned.1.call-start = ((), (), s32[]{:S(2)}) async-start(), calls=%async_computation.12 | async-start | bytes 4718592 | tf_op jit(solution)/shard_map/reduce_scatter | solution.py:406
  365.9 34.0 %all-to-all-start.3 = ((bf16[8,128,384]{2,1,0:T(8,128)(2,1)}), bf16[8,128,384]{2,1,0:T(8,128)(2,1)S(1)}, u32[]{:S(2)}, u32[]{:S(2)}) async-start(bf16[8,128,384]{2,1,0:T(8,128)(2,1)} %bitcast.51), calls=%async_computation.3 | async-start | bytes 1572864 | tf_op jit(solution)/shard_map/all_to_all | solution.py:1579
  369.5 172.3 %reduce-scatter.8.cloned.1.call-start = ((), (), s32[]{:S(2)}) async-start(), calls=%async_computation.13 | async-start | bytes 7999488 | tf_op jit(solution)/shard_map/reduce_scatter | solution.py:406
  369.8 25.9 %collective-permute-start.41 = (bf16[3456,128]{1,0:T(8,128)(2,1)}, bf16[3456,128]{1,0:T(8,128)(2,1)S(1)}, u32[]{:S(2)}, u32[]{:S(2)}) collective-permute-start(bf16[3456,128]{1,0:T(8,128)(2,1)} %get-tuple-element.166), channel_id=1, source_target_pairs={{0,24},{8,16},{16,8},{24,0},{1,25},{9,17},{17,9},{25,1},{2,26},{10... | collective-permute-start | bytes 2654216 | tf_op jit(solution)/shard_map/ppermute | solution.py:346
  454.3 29.6 %collective-permute-start.58 = (bf16[128,1280]{1,0:T(8,128)(2,1)S(1)}, bf16[128,1280]{1,0:T(8,128)(2,1)S(1)}, u32[]{:S(2)}, u32[]{:S(2)}) collective-permute-start(bf16[128,1280]{1,0:T(8,128)(2,1)S(1)} %get-tuple-element.179), channel_id=1, source_target_pairs={{0,4},{1,5},{2,6},{3,7},{4,0},{5,1},{6,2},{7,3},{8,12},{9,13},{10,... | collective-permute-start | bytes 983048 | tf_op jit(solution)/shard_map/ppermute | solution.py:416
  467.6 64.6 %collective-permute-start.63 = (bf16[128,3840]{1,0:T(8,128)(2,1)S(1)}, bf16[128,3840]{1,0:T(8,128)(2,1)S(1)}, u32[]{:S(2)}, u32[]{:S(2)}) collective-permute-start(bf16[128,3840]{1,0:T(8,128)(2,1)S(1)} %pad_maximum_fusion.5), channel_id=1, source_target_pairs={{0,8},{8,0},{16,24},{24,16},{1,9},{9,1},{17,25},{25,17},{2,10},{10... | collective-permute-start | bytes 2949128 | tf_op jit(solution)/shard_map/ppermute | solution.py:356
  468.2 61.5 %collective-permute-start.57 = (bf16[3456,128]{1,0:T(8,128)(2,1)}, bf16[3456,128]{1,0:T(8,128)(2,1)S(1)}, u32[]{:S(2)}, u32[]{:S(2)}) collective-permute-start(bf16[3456,128]{1,0:T(8,128)(2,1)} %get-tuple-element.196), channel_id=1, source_target_pairs={{0,24},{8,16},{16,8},{24,0},{1,25},{9,17},{17,9},{25,1},{2,26},{10... | collective-permute-start | bytes 2654216 | tf_op jit(solution)/shard_map/ppermute | solution.py:346
  484.0 49.2 %collective-permute-start.62 = (bf16[128,3840]{1,0:T(8,128)(2,1)S(1)}, bf16[128,3840]{1,0:T(8,128)(2,1)S(1)}, u32[]{:S(2)}, u32[]{:S(2)}) collective-permute-start(bf16[128,3840]{1,0:T(8,128)(2,1)S(1)} %pad_maximum_fusion.4), channel_id=1, source_target_pairs={{0,16},{8,24},{16,0},{24,8},{1,17},{9,25},{17,1},{25,9},{2,18},{10... | collective-permute-start | bytes 2949128 | tf_op jit(solution)/shard_map/ppermute | solution.py:355
  488.9 47.0 %collective-permute-start.59 = (bf16[128,1280]{1,0:T(8,128)(2,1)S(1)}, bf16[128,1280]{1,0:T(8,128)(2,1)S(1)}, u32[]{:S(2)}, u32[]{:S(2)}) collective-permute-start(bf16[128,1280]{1,0:T(8,128)(2,1)S(1)} %add_convert_fusion.refs_5_), channel_id=1, source_target_pairs={{0,8},{8,0},{16,24},{24,16},{1,9},{9,1},{17,25},{25,17},{2,10},{10... | collective-permute-start | bytes 983048 | tf_op jit(solution)/shard_map/ppermute | solution.py:346
  490.5 46.2 %collective-permute-start.60 = (bf16[128,1280]{1,0:T(8,128)(2,1)S(1)}, bf16[128,1280]{1,0:T(8,128)(2,1)S(1)}, u32[]{:S(2)}, u32[]{:S(2)}) collective-permute-start(bf16[128,1280]{1,0:T(8,128)(2,1)S(1)} %add_convert_fusion.refs_5_), channel_id=1, source_target_pairs={{0,16},{8,24},{16,0},{24,8},{1,17},{9,25},{17,1},{25,9},{2,18},{10... | collective-permute-start | bytes 983048 | tf_op jit(solution)/shard_map/ppermute | solution.py:346
  543.2 38.0 %collective-permute-start.65 = (bf16[3472,128]{1,0:T(8,128)(2,1)}, bf16[3472,128]{1,0:T(8,128)(2,1)S(1)}, u32[]{:S(2)}, u32[]{:S(2)}) collective-permute-start(bf16[3472,128]{1,0:T(8,128)(2,1)} %bitcast.138), channel_id=1, source_target_pairs={{0,16},{8,24},{16,0},{24,8},{1,17},{9,25},{17,1},{25,9},{2,18},{10... | collective-permute-start | bytes 2666504 | tf_op jit(solution)/shard_map/ppermute | solution.py:346
  544.1 37.1 %collective-permute-start.66 = (bf16[3472,128]{1,0:T(8,128)(2,1)}, bf16[3472,128]{1,0:T(8,128)(2,1)S(1)}, u32[]{:S(2)}, u32[]{:S(2)}) collective-permute-start(bf16[3472,128]{1,0:T(8,128)(2,1)} %bitcast.139), channel_id=1, source_target_pairs={{0,24},{8,16},{16,8},{24,0},{1,25},{9,17},{17,9},{25,1},{2,26},{10... | collective-permute-start | bytes 2666504 | tf_op jit(solution)/shard_map/ppermute | solution.py:346
  (172 other events, 1725.3 us)
Sparse Core Ops, SparseCore 0:
  15.3 96.2 all-gather.4
  113.9 61.5 all-gather.6
  187.5 26.2 all-gather.8
  267.3 41.1 all-gather.10
  319.7 46.1 reduce-scatter.3
  368.7 58.9 reduce-scatter.5
  450.1 81.0 reduce-scatter.7

commit v8 on v7

--- a/solution.py
+++ b/solution.py
@@ -1299,7 +1299,7 @@
     cells = latents[0].shape[0]
     last = latents[0].shape[1] // width - 1
     quarter = cots[0].shape[0]
-    step_rows = math.gcd(quarter, 1152)
+    step_rows = math.gcd(quarter, WIDE)
     return pl.pallas_call(
         functools.partial(decoder_kernel, count),
         grid=(quarter // step_rows,),

time: 603 us -> 603 us (level)
  transfers between devices with their start and end apart: 78 -> 78, of which waited for: 43 -> 44; matrix products, arithmetic and copies ran while one was open for 9% -> 9% of each run, Pallas kernels for 18% -> 18%
where the time goes in v8:
time: 603 us; the launch traced here: 593 us
  waiting for transfers between devices  273 us (45%)
  Pallas kernels  112 us (19%)
  starting transfers between devices  95.8 us (16%)
  local copies, waits for them, and re-layouts  68 us (11%)
  other arithmetic  18.3 us (3%)
  between operations  16.3 us (3%)
  matrix products  9.62 us (2%)
    ppermute x60, waiting for transfers between devices, swap(): lax.ppermute(pieces[k], 'slide', peers(k, count))  215 us
    ppermute x60, starting transfers between devices, swap(): lax.ppermute(pieces[k], 'slide', peers(k, count))  74.6 us
    unnamed x255, local copies, waits for them, and re-layouts  37.9 us
    ppermute x2, waiting for transfers between devices, to_chip(): lax.ppermute(rows, 'blk', [(place, place ^ 2 * offset) for place in range...  24.9 us
    all_to_all x4, waiting for transfers between devices, to_heads(): lax.all_to_all(rows.reshape(blocks, cells, rows.shape[-1]), 'blk', 0, 0,...  22.5 us
    all_to_all x4, starting transfers between devices, to_heads(): lax.all_to_all(rows.reshape(blocks, cells, rows.shape[-1]), 'blk', 0, 0,...  15.2 us
  transfers between devices with their start and end apart: 78, of which 44 were waited for; matrix products, arithmetic and copies ran while one was open for 9% of the time, Pallas kernels for 18%

profile of v8, /device:TPU:0, one launch (start us, length us, event | category | flops | bytes accessed | tf_op | source)
XLA Modules:
  0.0 592.6 jit_solution(1916616303754368051)
XLA Ops:
  15.3 7.8 %expression.1 = (bf16[3456,128]{1,0:T(8,128)(2,1)}, bf16[3456,128]{1,0:T(8,128)(2,1)}, bf16[3456,128]{1,0:T(8,128)(2,1)}, bf16[3456,128]{1,0:T(8,128)(2,1)}) custom-call(s32[1]{0:T(128)} %bitcast.me_ref, s32[1,128]{1,0:T(1,128)} %library_ref.1, s32[13500,1,128]{2,1,0:T(1,128)} %bitcast.144), custom_call_target="tpu_custom_call" | custom-call | tf_op jit(solution)/shard_map/expression/pallas_call | solution.py:478
  37.3 9.4 %collective-permute-done.refs_1_ = bf16[3456,128]{1,0:T(8,128)(2,1)S(1)} collective-permute-done((bf16[3456,128]{1,0:T(8,128)(2,1)}, bf16[3456,128]{1,0:T(8,128)(2,1)S(1)}, u32[]{:S(2)}, u32[]{:S(2)}) %collective-permute-start) | collective-permute-done | bytes 884768 | tf_op jit(solution)/shard_map/ppermute | solution.py:346
  46.8 19.6 %collective-permute-done.1.refs_2_ = bf16[3456,128]{1,0:T(8,128)(2,1)S(1)} collective-permute-done((bf16[3456,128]{1,0:T(8,128)(2,1)}, bf16[3456,128]{1,0:T(8,128)(2,1)S(1)}, u32[]{:S(2)}, u32[]{:S(2)}) %collective-permute-start.1) | collective-permute-done | bytes 884768 | tf_op jit(solution)/shard_map/ppermute | solution.py:346
  78.8 11.4 %collective-permute-done.3.refs_1_.refs_5_ = bf16[3456,128]{1,0:T(8,128)(2,1)} collective-permute-done((bf16[3456,128]{1,0:T(8,128)(2,1)}, bf16[3456,128]{1,0:T(8,128)(2,1)}, u32[]{:S(2)}, u32[]{:S(2)}) %collective-permute-start.3) | collective-permute-done | bytes 884768 | tf_op jit(solution)/shard_map/ppermute | solution.py:346
  90.2 17.0 %collective-permute-done.4.refs_2_.refs_6_ = bf16[3456,128]{1,0:T(8,128)(2,1)} collective-permute-done((bf16[3456,128]{1,0:T(8,128)(2,1)}, bf16[3456,128]{1,0:T(8,128)(2,1)}, u32[]{:S(2)}, u32[]{:S(2)}) %collective-permute-start.4) | collective-permute-done | bytes 884768 | tf_op jit(solution)/shard_map/ppermute | solution.py:346
  113.4 8.0 %embed_cells.1 = (f32[128,1024]{1,0:T(8,128)}, bf16[128,1024]{1,0:T(8,128)(2,1)}, bf16[128,1024]{1,0:T(8,128)(2,1)}, bf16[128,1024]{1,0:T(8,128)(2,1)}) custom-call(bf16[512,3456]{1,0:T(8,128)(2,1)} %copy-done.2, bf16[4752,1024]{1,0:T(8,128)(2,1)} %all-gather.5.cloned.1.call-done.table), custom_call_target="tpu_custom_call" | custom-call | tf_op jit(solution)/shard_map/embed_cells/pallas_call | solution.py:715
  129.8 6.0 %collective-permute-done.10 = bf16[128,1024]{1,0:T(8,128)(2,1)S(1)} collective-permute-done((bf16[128,1024]{1,0:T(8,128)(2,1)}, bf16[128,1024]{1,0:T(8,128)(2,1)S(1)}, u32[]{:S(2)}, u32[]{:S(2)}) %collective-permute-start.10) | collective-permute-done | bytes 262176 | tf_op jit(solution)/shard_map/ppermute | solution.py:346
  168.5 9.5 %collective-permute-done.16.refs_2_ = bf16[256,1024]{1,0:T(8,128)(2,1)S(1)} collective-permute-done((bf16[256,1024]{1,0:T(8,128)(2,1)S(1)}, bf16[256,1024]{1,0:T(8,128)(2,1)S(1)}, u32[]{:S(2)}, u32[]{:S(2)}) %collective-permute-start.16) | collective-permute-done | bytes 524320 | tf_op jit(solution)/shard_map/ppermute | solution.py:346
  208.3 10.3 %all-to-all-done.1 = bf16[8,128,128]{2,1,0:T(8,128)(2,1)} async-done(((bf16[8,128,128]{2,1,0:T(8,128)(2,1)}), bf16[8,128,128]{2,1,0:T(8,128)(2,1)}, u32[]{:S(2)}, u32[]{:S(2)}) %all-to-all-start.1) | async-done | bytes 262176 | tf_op jit(solution)/shard_map/all_to_all | solution.py:1579
  274.7 9.9 %collective-permute-done.30.refs_1_ = bf16[128,1536]{1,0:T(8,128)(2,1)S(1)} collective-permute-done((bf16[128,1536]{1,0:T(8,128)(2,1)S(1)}, bf16[128,1536]{1,0:T(8,128)(2,1)S(1)}, u32[]{:S(2)}, u32[]{:S(2)}) %collective-permute-start.30) | collective-permute-done | bytes 393248 | tf_op jit(solution)/shard_map/ppermute | solution.py:346
  290.8 9.6 %feed_back.1 = (f32[128,1024]{1,0:T(8,128)}, bf16[512,1024]{1,0:T(8,128)(2,1)}, bf16[512,1024]{1,0:T(8,128)(2,1)}, f32[1,1024]{1,0:T(1,128)}, f32[128,1024]{1,0:...) custom-call(bf16[1024,1024]{1,0:T(8,128)(2,1)} %order_rows.3.latent, ...), custom_call_target="tpu_custom_call" | custom-call | tf_op jit(solution)/shard_map/feed_back/pallas_call | solution.py:907
  312.5 5.7 decoder_products.1
  344.2 8.1 %all-to-all-done.2 = bf16[8,128,128]{2,1,0:T(8,128)(2,1)S(1)} async-done(((bf16[8,128,128]{2,1,0:T(8,128)(2,1)}), bf16[8,128,128]{2,1,0:T(8,128)(2,1)S(1)}, u32[]{:S(2)}, u32[]{:S(2)}) %all-to-all-start.2) | async-done | bytes 262176 | tf_op jit(solution)/shard_map/all_to_all | solution.py:1579
  352.3 10.8 %attend_back.1 = bf16[1024,384]{1,0:T(8,128)(2,1)} custom-call(bf16[1024,384]{1,0:T(8,128)(2,1)} %bitcast.23.rows_ref, bf16[1024,128]{1,0:T(8,128)(2,1)S(1)} %bitcast.135), custom_call_target="tpu_custom_call" | custom-call | tf_op jit(solution)/shard_map/attend_back/pallas_call | solution.py:1416
  379.1 15.7 %collective-permute-done.44.refs_7_ = bf16[128,256]{1,0:T(8,128)(2,1)S(1)} collective-permute-done((bf16[128,256]{1,0:T(8,128)(2,1)S(1)}, bf16[128,256]{1,0:T(8,128)(2,1)S(1)}, u32[]{:S(2)}, u32[]{:S(2)}) %collective-permute-start.44) | collective-permute-done | bytes 65568 | tf_op jit(solution)/shard_map/ppermute | solution.py:346
  410.4 5.5 collective-permute-done.45
  415.9 6.4 %collective-permute-done.46 = bf16[128,1024]{1,0:T(8,128)(2,1)S(1)} collective-permute-done((bf16[128,1024]{1,0:T(8,128)(2,1)S(1)}, bf16[128,1024]{1,0:T(8,128)(2,1)S(1)}, u32[]{:S(2)}, u32[]{:S(2)}) %collective-permute-start.46) | collective-permute-done | bytes 262176 | tf_op jit(solution)/shard_map/ppermute | solution.py:346
  429.2 11.5 %collective-permute-done.49.other = bf16[256,1280]{1,0:T(8,128)(2,1)S(1)} collective-permute-done((bf16[256,1280]{1,0:T(8,128)(2,1)S(1)}, bf16[256,1280]{1,0:T(8,128)(2,1)S(1)}, u32[]{:S(2)}, u32[]{:S(2)}) %collective-permute-start.49) | collective-permute-done | bytes 655392 | tf_op jit(solution)/shard_map/ppermute | solution.py:416
  441.7 8.1 %embed_products.1 = bf16[8,3472,128]{2,1,0:T(8,128)(2,1)} custom-call(bf16[3456,128]{1,0:T(8,128)(2,1)} %get-tuple-element.112.refs_0_, bf16[3456,128]{1,0:T(8,128)(2,1)} %copy-done.16, bf16[3456,128]{1,0:T(8,128)(2,1)} %copy-done.17, bf16[3456,128]{1,0:T(8,128)(2,1)} %collective-permute-done.2.refs_3_, bf16[128,1024]{1,0:T(8,128)(2,1)} %copy-done.68, ...), custom_call_target="tpu_custom_call" | custom-call | tf_op jit(solution)/shard_map/embed_products/pallas_call | solution.py:1235
  454.4 8.1 %cells_to_genes.1 = (bf16[3456,128]{1,0:T(8,128)(2,1)}, bf16[3456,128]{1,0:T(8,128)(2,1)}, bf16[3456,128]{1,0:T(8,128)(2,1)}, bf16[3456,128]{1,0:T(8,128)(2,1)}) custom-call(bf16[4752,1024]{1,0:T(8,128)(2,1)} %all-gather.5.cloned.1.call-done.table, bf16[128,1024]{1,0:T(8,128)(2,1)} %copy-done.68, bf16[128,1024]{1,0:T(8,128)(2,1)} %collective-permute-done.50.refs_5_.refs_1_, ...), custom_call_target="tpu_custom_call" | custom-call | tf_op jit(solution)/shard_map/cells_to_genes/pallas_call | solution.py:1173
  470.4 13.4 %collective-permute-done.58 = bf16[128,1280]{1,0:T(8,128)(2,1)S(1)} collective-permute-done((bf16[128,1280]{1,0:T(8,128)(2,1)S(1)}, bf16[128,1280]{1,0:T(8,128)(2,1)S(1)}, u32[]{:S(2)}, u32[]{:S(2)}) %collective-permute-start.58) | collective-permute-done | bytes 327712 | tf_op jit(solution)/shard_map/ppermute | solution.py:416
  491.7 37.9 %collective-permute-done.57.rest_3_ = bf16[3456,128]{1,0:T(8,128)(2,1)S(1)} collective-permute-done((bf16[3456,128]{1,0:T(8,128)(2,1)}, bf16[3456,128]{1,0:T(8,128)(2,1)S(1)}, u32[]{:S(2)}, u32[]{:S(2)}) %collective-permute-start.57) | collective-permute-done | bytes 884768 | tf_op jit(solution)/shard_map/ppermute | solution.py:346
  557.0 6.9 %assemble.1 = (f32[512,1024]{1,0:T(8,128)}, f32[128,4096]{1,0:T(8,128)}, f32[128,3072]{1,0:T(8,128)}, f32[128,1024]{1,0:T(8,128)}, f32[128,1024]{1,0:T(8,128)}, /*index=5*/f32[64,13500]{1,0:T(8,128)}) custom-call(s32[1]{0:T(128)} %bitcast.me_ref, bf16[128,3840]{1,0:T(8,128)(2,1)S(1)} %fusion.10.refs_0_, ...), custom_call_target="tpu_custom_call" | custom-call | tf_op jit(solution)/shard_map/assemble/pallas_call | solution.py:1139
  564.6 16.6 %collective-permute-done.65.refs_2_ = bf16[3472,128]{1,0:T(8,128)(2,1)S(1)} collective-permute-done((bf16[3472,128]{1,0:T(8,128)(2,1)}, bf16[3472,128]{1,0:T(8,128)(2,1)S(1)}, u32[]{:S(2)}, u32[]{:S(2)}) %collective-permute-start.65) | collective-permute-done | bytes 888864 | tf_op jit(solution)/shard_map/ppermute | solution.py:346
  (527 shorter events, 303.2 us)
Async XLA Ops:
  7.2 104.4 %all-gather.5.cloned.1.call-start = ((), (), s32[]{:S(2)}) async-start(), calls=%async_computation.7 | async-start | bytes 10948608 | tf_op jit(solution)/shard_map/all_gather | solution.py:402
  15.2 167.3 %all-gather.7.cloned.1.call-start = ((), (), s32[]{:S(2)}) async-start(), calls=%async_computation.8 | async-start | bytes 6488064 | tf_op jit(solution)/shard_map/all_gather | solution.py:402
  23.1 23.7 %collective-permute-start = (bf16[3456,128]{1,0:T(8,128)(2,1)}, bf16[3456,128]{1,0:T(8,128)(2,1)S(1)}, u32[]{:S(2)}, u32[]{:S(2)}) collective-permute-start(bf16[3456,128]{1,0:T(8,128)(2,1)} %get-tuple-element.113), channel_id=1, source_target_pairs={{0,8},{8,0},{16,24},{24,16},{1,9},{9,1},{17,25},{25,17},{2,10},{10... | collective-permute-start | bytes 2654216 | tf_op jit(solution)/shard_map/ppermute | solution.py:346
  26.1 40.3 %collective-permute-start.1 = (bf16[3456,128]{1,0:T(8,128)(2,1)}, bf16[3456,128]{1,0:T(8,128)(2,1)S(1)}, u32[]{:S(2)}, u32[]{:S(2)}) collective-permute-start(bf16[3456,128]{1,0:T(8,128)(2,1)} %get-tuple-element.114), channel_id=1, source_target_pairs={{0,16},{8,24},{16,0},{24,8},{1,17},{9,25},{17,1},{25,9},{2,18},{10... | collective-permute-start | bytes 2654216 | tf_op jit(solution)/shard_map/ppermute | solution.py:346
  27.6 39.7 %collective-permute-start.2 = (bf16[3456,128]{1,0:T(8,128)(2,1)}, bf16[3456,128]{1,0:T(8,128)(2,1)}, u32[]{:S(2)}, u32[]{:S(2)}) collective-permute-start(bf16[3456,128]{1,0:T(8,128)(2,1)} %get-tuple-element.115), channel_id=1, source_target_pairs={{0,24},{8,16},{16,8},{24,0},{1,25},{9,17},{17,9},{25,1},{2,26},{10... | collective-permute-start | bytes 2654216 | tf_op jit(solution)/shard_map/ppermute | solution.py:346
  67.7 39.5 %collective-permute-start.4 = (bf16[3456,128]{1,0:T(8,128)(2,1)}, bf16[3456,128]{1,0:T(8,128)(2,1)}, u32[]{:S(2)}, u32[]{:S(2)}) collective-permute-start(bf16[3456,128]{1,0:T(8,128)(2,1)} %get-tuple-element.117), channel_id=1, source_target_pairs={{0,16},{8,24},{16,0},{24,8},{1,17},{9,25},{17,1},{25,9},{2,18},{10... | collective-permute-start | bytes 2654216 | tf_op jit(solution)/shard_map/ppermute | solution.py:346
  69.3 37.9 %collective-permute-start.5 = (bf16[3456,128]{1,0:T(8,128)(2,1)}, bf16[3456,128]{1,0:T(8,128)(2,1)}, u32[]{:S(2)}, u32[]{:S(2)}) collective-permute-start(bf16[3456,128]{1,0:T(8,128)(2,1)} %get-tuple-element.118), channel_id=1, source_target_pairs={{0,24},{8,16},{16,8},{24,0},{1,25},{9,17},{17,9},{25,1},{2,26},{10... | collective-permute-start | bytes 2654216 | tf_op jit(solution)/shard_map/ppermute | solution.py:346
  159.3 35.9 %all-to-all-start = ((bf16[8,128,384]{2,1,0:T(8,128)(2,1)}), bf16[8,128,384]{2,1,0:T(8,128)(2,1)}, u32[]{:S(2)}, u32[]{:S(2)}) async-start(bf16[8,128,384]{2,1,0:T(8,128)(2,1)} %bitcast.22), calls=%async_computation | async-start | bytes 1572864 | tf_op jit(solution)/shard_map/all_to_all | solution.py:1579
  163.5 83.9 %all-gather.9.cloned.1.call-start = ((), (), s32[]{:S(2)}) async-start(), calls=%async_computation.9 | async-start | bytes 2359296 | tf_op jit(solution)/shard_map/all_gather | solution.py:402
  195.2 23.4 %collective-permute-start.18 = (bf16[256,1024]{1,0:T(8,128)(2,1)}, bf16[256,1024]{1,0:T(8,128)(2,1)}, u32[]{:S(2)}, u32[]{:S(2)}) collective-permute-start(bf16[256,1024]{1,0:T(8,128)(2,1)} %get-tuple-element.132.refs_0_), channel_id=1, source_target_pairs={{0,8},{8,0},{16,24},{24,16},{1,9},{9,1},{17,25},{25,17},{2,10},{10... | collective-permute-start | bytes 1572872 | tf_op jit(solution)/shard_map/ppermute | solution.py:346
  208.2 111.3 %all-gather.11.cloned.1.call-start = ((), (), s32[]{:S(2)}) async-start(), calls=%async_computation.10 | async-start | bytes 2621440 | tf_op jit(solution)/shard_map/all_gather | solution.py:1618
  267.2 98.6 %reduce-scatter.4.cloned.1.call-start = ((), (), s32[]{:S(2)}) async-start(), calls=%async_computation.11 | async-start | bytes 3981312 | tf_op jit(solution)/shard_map/reduce_scatter | solution.py:406
  338.0 111.8 %reduce-scatter.6.cloned.1.call-start = ((), (), s32[]{:S(2)}) async-start(), calls=%async_computation.12 | async-start | bytes 4718592 | tf_op jit(solution)/shard_map/reduce_scatter | solution.py:406
  365.8 34.0 %all-to-all-start.3 = ((bf16[8,128,384]{2,1,0:T(8,128)(2,1)}), bf16[8,128,384]{2,1,0:T(8,128)(2,1)S(1)}, u32[]{:S(2)}, u32[]{:S(2)}) async-start(bf16[8,128,384]{2,1,0:T(8,128)(2,1)} %bitcast.51), calls=%async_computation.3 | async-start | bytes 1572864 | tf_op jit(solution)/shard_map/all_to_all | solution.py:1579
  369.4 172.3 %reduce-scatter.8.cloned.1.call-start = ((), (), s32[]{:S(2)}) async-start(), calls=%async_computation.13 | async-start | bytes 7999488 | tf_op jit(solution)/shard_map/reduce_scatter | solution.py:406
  369.7 26.0 %collective-permute-start.41 = (bf16[3456,128]{1,0:T(8,128)(2,1)}, bf16[3456,128]{1,0:T(8,128)(2,1)S(1)}, u32[]{:S(2)}, u32[]{:S(2)}) collective-permute-start(bf16[3456,128]{1,0:T(8,128)(2,1)} %get-tuple-element.166), channel_id=1, source_target_pairs={{0,24},{8,16},{16,8},{24,0},{1,25},{9,17},{17,9},{25,1},{2,26},{10... | collective-permute-start | bytes 2654216 | tf_op jit(solution)/shard_map/ppermute | solution.py:346
  454.2 29.6 %collective-permute-start.58 = (bf16[128,1280]{1,0:T(8,128)(2,1)S(1)}, bf16[128,1280]{1,0:T(8,128)(2,1)S(1)}, u32[]{:S(2)}, u32[]{:S(2)}) collective-permute-start(bf16[128,1280]{1,0:T(8,128)(2,1)S(1)} %get-tuple-element.179), channel_id=1, source_target_pairs={{0,4},{1,5},{2,6},{3,7},{4,0},{5,1},{6,2},{7,3},{8,12},{9,13},{10,... | collective-permute-start | bytes 983048 | tf_op jit(solution)/shard_map/ppermute | solution.py:416
  467.5 64.6 %collective-permute-start.63 = (bf16[128,3840]{1,0:T(8,128)(2,1)S(1)}, bf16[128,3840]{1,0:T(8,128)(2,1)S(1)}, u32[]{:S(2)}, u32[]{:S(2)}) collective-permute-start(bf16[128,3840]{1,0:T(8,128)(2,1)S(1)} %pad_maximum_fusion.5), channel_id=1, source_target_pairs={{0,8},{8,0},{16,24},{24,16},{1,9},{9,1},{17,25},{25,17},{2,10},{10... | collective-permute-start | bytes 2949128 | tf_op jit(solution)/shard_map/ppermute | solution.py:356
  468.0 61.6 %collective-permute-start.57 = (bf16[3456,128]{1,0:T(8,128)(2,1)}, bf16[3456,128]{1,0:T(8,128)(2,1)S(1)}, u32[]{:S(2)}, u32[]{:S(2)}) collective-permute-start(bf16[3456,128]{1,0:T(8,128)(2,1)} %get-tuple-element.196), channel_id=1, source_target_pairs={{0,24},{8,16},{16,8},{24,0},{1,25},{9,17},{17,9},{25,1},{2,26},{10... | collective-permute-start | bytes 2654216 | tf_op jit(solution)/shard_map/ppermute | solution.py:346
  483.9 49.2 %collective-permute-start.62 = (bf16[128,3840]{1,0:T(8,128)(2,1)S(1)}, bf16[128,3840]{1,0:T(8,128)(2,1)S(1)}, u32[]{:S(2)}, u32[]{:S(2)}) collective-permute-start(bf16[128,3840]{1,0:T(8,128)(2,1)S(1)} %pad_maximum_fusion.4), channel_id=1, source_target_pairs={{0,16},{8,24},{16,0},{24,8},{1,17},{9,25},{17,1},{25,9},{2,18},{10... | collective-permute-start | bytes 2949128 | tf_op jit(solution)/shard_map/ppermute | solution.py:355
  488.7 47.0 %collective-permute-start.59 = (bf16[128,1280]{1,0:T(8,128)(2,1)S(1)}, bf16[128,1280]{1,0:T(8,128)(2,1)S(1)}, u32[]{:S(2)}, u32[]{:S(2)}) collective-permute-start(bf16[128,1280]{1,0:T(8,128)(2,1)S(1)} %add_convert_fusion.refs_5_), channel_id=1, source_target_pairs={{0,8},{8,0},{16,24},{24,16},{1,9},{9,1},{17,25},{25,17},{2,10},{10... | collective-permute-start | bytes 983048 | tf_op jit(solution)/shard_map/ppermute | solution.py:346
  490.4 46.1 %collective-permute-start.60 = (bf16[128,1280]{1,0:T(8,128)(2,1)S(1)}, bf16[128,1280]{1,0:T(8,128)(2,1)S(1)}, u32[]{:S(2)}, u32[]{:S(2)}) collective-permute-start(bf16[128,1280]{1,0:T(8,128)(2,1)S(1)} %add_convert_fusion.refs_5_), channel_id=1, source_target_pairs={{0,16},{8,24},{16,0},{24,8},{1,17},{9,25},{17,1},{25,9},{2,18},{10... | collective-permute-start | bytes 983048 | tf_op jit(solution)/shard_map/ppermute | solution.py:346
  543.2 38.0 %collective-permute-start.65 = (bf16[3472,128]{1,0:T(8,128)(2,1)}, bf16[3472,128]{1,0:T(8,128)(2,1)S(1)}, u32[]{:S(2)}, u32[]{:S(2)}) collective-permute-start(bf16[3472,128]{1,0:T(8,128)(2,1)} %bitcast.138), channel_id=1, source_target_pairs={{0,16},{8,24},{16,0},{24,8},{1,17},{9,25},{17,1},{25,9},{2,18},{10... | collective-permute-start | bytes 2666504 | tf_op jit(solution)/shard_map/ppermute | solution.py:346
  544.0 37.2 %collective-permute-start.66 = (bf16[3472,128]{1,0:T(8,128)(2,1)}, bf16[3472,128]{1,0:T(8,128)(2,1)S(1)}, u32[]{:S(2)}, u32[]{:S(2)}) collective-permute-start(bf16[3472,128]{1,0:T(8,128)(2,1)} %bitcast.139), channel_id=1, source_target_pairs={{0,24},{8,16},{16,8},{24,0},{1,25},{9,17},{17,9},{25,1},{2,26},{10... | collective-permute-start | bytes 2666504 | tf_op jit(solution)/shard_map/ppermute | solution.py:346
  (172 other events, 1724.4 us)
Sparse Core Ops, SparseCore 0:
  15.3 96.2 all-gather.4
  113.9 61.5 all-gather.6
  187.5 26.2 all-gather.8
  267.3 41.1 all-gather.10
  319.7 46.0 reduce-scatter.3
  368.6 58.9 reduce-scatter.5
  450.0 81.0 reduce-scatter.7
